TPU v7x, 32 devices: a whole 2x2x4 slice. The times are simulated.
32 devices in a mesh: wide: 8 (over z, x), narrow: 4 (over y, core).
Axes of the slice: x: 2, y: 2, z: 4, core: 2. Of those that a mesh axis runs over, the one named last changes fastest.
Arguments:
- tokens: bfloat16 [16384, 1024], P(('wide', 'narrow')), may hold values from -20 to 20
- lengths: int32 [16], P('wide'), may hold values from 128 to 1024, as said below
- norm_gain: float32 [1024], replicated, may hold values from 0.25 to 1.75
- w_query: bfloat16 [1024, 1024], P(None, 'narrow'), may hold values from -0.1875 to 0.1875
- w_key: bfloat16 [1024, 512], P(None, 'narrow'), may hold values from -0.1875 to 0.1875
- w_value: bfloat16 [1024, 512], P(None, 'narrow'), may hold values from -0.1875 to 0.1875
- query_scale: float32 [64], replicated, may hold values from 0.8 to 1.8
- key_scale: float32 [64], replicated, may hold values from 0.8 to 1.8
- w_out: bfloat16 [1024, 1024], P('narrow'), may hold values from -1.5 to 1.5
- ffn_gain: float32 [1024], replicated, may hold values from 0.25 to 1.75
- w_gate: bfloat16 [1024, 4608], P(None, 'narrow'), may hold values from -0.1875 to 0.1875
- w_up: bfloat16 [1024, 4608], P(None, 'narrow'), may hold values from -0.1875 to 0.1875
- w_down: bfloat16 [4608, 1024], P('narrow'), may hold values from -0.09375 to 0.09375
- cotangent: bfloat16 [16384, 1024], P(('wide', 'narrow')), may hold values from -6 to 6
Outputs:
- output: bfloat16 [16384, 1024], P(('wide', 'narrow'))
- tokens_grad: float32 [16384, 1024], P(('wide', 'narrow'))
- norm_gain_grad: float32 [1024], replicated
- query_grad: float32 [1024, 1024], P(None, 'narrow')
- key_grad: float32 [1024, 512], P(None, 'narrow')
- value_grad: float32 [1024, 512], P(None, 'narrow')
- query_scale_grad: float32 [64], replicated
- key_scale_grad: float32 [64], replicated
- out_grad: float32 [1024, 1024], P('narrow')
- ffn_gain_grad: float32 [1024], replicated
- gate_grad: float32 [1024, 4608], P(None, 'narrow')
- up_grad: float32 [1024, 4608], P(None, 'narrow')
- down_grad: float32 [4608, 1024], P('narrow')
Inputs may be any that keep to these rules, and one draw needn't show every extreme that they name: `lengths`: slots of a sequence at or past its length are padding. Some sequence has exactly 1024 in every draw.
All inputs are finite; a program needn't handle non-finite values.
Results may differ from a plain program's by a relative error of at most 0.02.
Values may be sent and summed in bfloat16 or wider, within the bound.
A program may use at most 192 MiB of HBM per device.

v0:
```python
import math

import jax
import jax.numpy as jnp
from jax import lax
from jax.sharding import PartitionSpec as P

HD = 64
LEN = 1024


EPSILON = 1e-05
ROPE_BASE = 1000000.0


def rope_tables(length, width):
    half_width = width // 2
    frequency = ROPE_BASE ** (-(2.0 * jnp.arange(half_width, dtype=jnp.float32)) / width)
    angles = jnp.arange(length, dtype=jnp.float32)[:, None] * frequency[None, :]
    return (jnp.cos(angles), jnp.sin(angles))


def rotate(values_in, cosine, sine):
    half_width = values_in.shape[-1] // 2
    front_half = values_in[..., :half_width]
    back_half = values_in[..., half_width:]
    cos_b = cosine[:, None, :]
    sin_b = sine[:, None, :]
    return jnp.concatenate(
        [front_half * cos_b - back_half * sin_b, back_half * cos_b + front_half * sin_b], axis=-1
    )


def rotate_back(grad_in, cosine, sine):
    half_width = grad_in.shape[-1] // 2
    front_half = grad_in[..., :half_width]
    back_half = grad_in[..., half_width:]
    cos_b = cosine[:, None, :]
    sin_b = sine[:, None, :]
    return jnp.concatenate(
        [front_half * cos_b + back_half * sin_b, back_half * cos_b - front_half * sin_b], axis=-1
    )


def row_norm(values_in, gain_vec):
    inv_rms = lax.rsqrt(jnp.mean(values_in * values_in, axis=-1, keepdims=True) + EPSILON)
    return (values_in * inv_rms * gain_vec, inv_rms)


def row_norm_back(values_in, inv_rms, gain_vec, grad_in):
    scaled = grad_in * gain_vec
    back_part = inv_rms * scaled - values_in * (inv_rms * inv_rms * inv_rms) * jnp.mean(
        values_in * scaled, axis=-1, keepdims=True
    )
    gain_part = jnp.sum((grad_in * values_in * inv_rms).reshape(-1, values_in.shape[-1]), axis=0)
    return (back_part, gain_part)


def contract_rows(left_side, right_side):
    return lax.dot_general(
        left_side, right_side, (((0,), (0,)), ((), ())), preferred_element_type=jnp.float32
    )


def times_transposed(left_side, right_side):
    return lax.dot_general(
        left_side, right_side, (((1,), (1,)), ((), ())), preferred_element_type=jnp.float32
    )


def causal_allowed(row_count, length):
    row_ids = jnp.arange(row_count)[:, None]
    col_ids = jnp.arange(row_count)[None, :]
    return (col_ids <= row_ids) & (col_ids < length)


def masked_scores(grouped, keys, length, score_scale):
    scores = (
        jnp.einsum("qkgd,skd->kgqs", grouped, keys, preferred_element_type=jnp.float32)
        * score_scale
    )
    return jnp.where(causal_allowed(grouped.shape[0], length), scores, -1e30)


def attend(queries, keys, values, length, score_scale):
    row_count = queries.shape[0]
    grouped = queries.reshape(row_count, keys.shape[1], -1, queries.shape[-1])
    scores = masked_scores(grouped, keys, length, score_scale)
    highest = jnp.max(scores, axis=-1, keepdims=True)
    exponent = jnp.exp(scores - highest)
    totals = jnp.sum(exponent, axis=-1, keepdims=True)
    probabilities = (exponent / totals).astype(jnp.bfloat16)
    mixed_rows = jnp.einsum(
        "kgqs,skd->qkgd", probabilities, values, preferred_element_type=jnp.float32
    )
    return (mixed_rows.reshape(queries.shape).astype(jnp.bfloat16), highest + jnp.log(totals))


def attend_back(queries, keys, values, log_total, grad_out, length, score_scale):
    row_count = queries.shape[0]
    grouped = queries.reshape(row_count, keys.shape[1], -1, queries.shape[-1])
    grad_grouped = grad_out.reshape(grouped.shape)
    scores = masked_scores(grouped, keys, length, score_scale)
    probabilities = jnp.exp(scores - log_total)
    grad_probs = jnp.einsum(
        "qkgd,skd->kgqs", grad_grouped, values, preferred_element_type=jnp.float32
    )
    inner = jnp.sum(probabilities * grad_probs, axis=-1, keepdims=True)
    grad_scores = (probabilities * (grad_probs - inner)).astype(jnp.bfloat16)
    grad_query = (
        jnp.einsum("kgqs,skd->qkgd", grad_scores, keys, preferred_element_type=jnp.float32)
        * score_scale
    )
    grad_key = (
        jnp.einsum("kgqs,qkgd->skd", grad_scores, grouped, preferred_element_type=jnp.float32)
        * score_scale
    )
    grad_value = jnp.einsum(
        "kgqs,qkgd->skd",
        probabilities.astype(jnp.bfloat16),
        grad_grouped,
        preferred_element_type=jnp.float32,
    )
    return (grad_query.reshape(queries.shape), grad_key, grad_value)


def ffn_front(rows_two, w_gate, w_up):
    gate_pre = jnp.dot(rows_two, w_gate, preferred_element_type=jnp.float32)
    up_pre = jnp.dot(rows_two, w_up, preferred_element_type=jnp.float32)
    hidden = (jax.nn.silu(gate_pre) * up_pre).astype(jnp.bfloat16)
    return (gate_pre, up_pre, hidden)


def on_device(
    tokens,
    lengths,
    norm_gain,
    w_query,
    w_key,
    w_value,
    query_scale,
    key_scale,
    w_out,
    ffn_gain,
    w_gate,
    w_up,
    w_down,
    cotangent,
):
    seq_count = lengths.shape[0]
    head_count = w_query.shape[1] // HD
    kv_count = w_key.shape[1] // HD
    group_rows = seq_count * LEN
    cosine, sine = rope_tables(LEN, HD)
    score_scale = 1.0 / math.sqrt(HD)
    residual = tokens.astype(jnp.float32)
    normed_one, inv_one = row_norm(residual, norm_gain)
    normed_low_one = normed_one.astype(jnp.bfloat16)
    rows_one = lax.all_gather(normed_low_one, "narrow", axis=0, tiled=True)
    query_raw = jnp.dot(rows_one, w_query, preferred_element_type=jnp.float32).reshape(
        seq_count, LEN, head_count, HD
    )
    key_raw = jnp.dot(rows_one, w_key, preferred_element_type=jnp.float32).reshape(
        seq_count, LEN, kv_count, HD
    )
    value_heads = (
        jnp.dot(rows_one, w_value, preferred_element_type=jnp.float32)
        .astype(jnp.bfloat16)
        .reshape(seq_count, LEN, kv_count, HD)
    )
    query_normed, query_inv = row_norm(query_raw, query_scale)
    key_normed, key_inv = row_norm(key_raw, key_scale)
    queries = rotate(query_normed, cosine, sine).astype(jnp.bfloat16)
    keys = rotate(key_normed, cosine, sine).astype(jnp.bfloat16)

    def attend_entry(entries):
        return attend(entries[0], entries[1], entries[2], entries[3], score_scale)

    attended, log_total = lax.map(attend_entry, (queries, keys, value_heads, lengths))
    mixed_heads = attended.reshape(group_rows, head_count * HD)
    middle = residual + lax.psum_scatter(
        jnp.dot(mixed_heads, w_out, preferred_element_type=jnp.float32).astype(jnp.bfloat16),
        "narrow",
        scatter_dimension=0,
        tiled=True,
    ).astype(jnp.float32)
    normed_two, inv_two = row_norm(middle, ffn_gain)
    normed_low_two = normed_two.astype(jnp.bfloat16)
    rows_two = lax.all_gather(normed_low_two, "narrow", axis=0, tiled=True)
    gate_pre, up_pre, hidden = ffn_front(rows_two, w_gate, w_up)
    output = middle + lax.psum_scatter(
        jnp.dot(hidden, w_down, preferred_element_type=jnp.float32).astype(jnp.bfloat16),
        "narrow",
        scatter_dimension=0,
        tiled=True,
    ).astype(jnp.float32)
    grad_rows = lax.all_gather(cotangent, "narrow", axis=0, tiled=True)
    grad_down = contract_rows(hidden, grad_rows)
    grad_hidden = times_transposed(grad_rows, w_down)
    sigmoid_gate = jax.nn.sigmoid(gate_pre)
    grad_gate = (
        grad_hidden * up_pre * sigmoid_gate * (1.0 + gate_pre * (1.0 - sigmoid_gate))
    ).astype(jnp.bfloat16)
    grad_up = (grad_hidden * gate_pre * sigmoid_gate).astype(jnp.bfloat16)
    grad_w_gate = contract_rows(rows_two, grad_gate)
    grad_w_up = contract_rows(rows_two, grad_up)
    grad_normed_two = lax.psum_scatter(
        (times_transposed(grad_gate, w_gate) + times_transposed(grad_up, w_up)).astype(
            jnp.bfloat16
        ),
        "narrow",
        scatter_dimension=0,
        tiled=True,
    ).astype(jnp.float32)
    back_two, gain_two = row_norm_back(middle, inv_two, ffn_gain, grad_normed_two)
    grad_middle = cotangent.astype(jnp.float32) + back_two
    branch_rows = lax.all_gather(grad_middle.astype(jnp.bfloat16), "narrow", axis=0, tiled=True)
    grad_w_out = contract_rows(mixed_heads, branch_rows)
    grad_mixed = (
        times_transposed(branch_rows, w_out)
        .astype(jnp.bfloat16)
        .reshape(seq_count, LEN, head_count, HD)
    )

    def back_entry(entries):
        return attend_back(
            entries[0], entries[1], entries[2], entries[3], entries[4], entries[5], score_scale
        )

    grad_rot_q, grad_rot_k, grad_values = lax.map(
        back_entry, (queries, keys, value_heads, log_total, grad_mixed, lengths)
    )
    grad_query_heads, query_scale_part = row_norm_back(
        query_raw, query_inv, query_scale, rotate_back(grad_rot_q, cosine, sine)
    )
    grad_key_heads, key_scale_part = row_norm_back(
        key_raw, key_inv, key_scale, rotate_back(grad_rot_k, cosine, sine)
    )
    grad_queries = grad_query_heads.reshape(group_rows, head_count * HD).astype(jnp.bfloat16)
    grad_keys = grad_key_heads.reshape(group_rows, kv_count * HD).astype(jnp.bfloat16)
    grad_value_rows = grad_values.reshape(group_rows, kv_count * HD).astype(jnp.bfloat16)
    grad_w_query = contract_rows(rows_one, grad_queries)
    grad_w_key = contract_rows(rows_one, grad_keys)
    grad_w_value = contract_rows(rows_one, grad_value_rows)
    grad_normed_one = lax.psum_scatter(
        (
            times_transposed(grad_queries, w_query)
            + times_transposed(grad_keys, w_key)
            + times_transposed(grad_value_rows, w_value)
        ).astype(jnp.bfloat16),
        "narrow",
        scatter_dimension=0,
        tiled=True,
    ).astype(jnp.float32)
    back_one, gain_one = row_norm_back(residual, inv_one, norm_gain, grad_normed_one)
    grad_tokens = grad_middle + back_one
    all_summed = (
        lax.psum(grad_w_query.astype(jnp.bfloat16), "wide").astype(jnp.float32),
        lax.psum(grad_w_key.astype(jnp.bfloat16), "wide").astype(jnp.float32),
        lax.psum(grad_w_value.astype(jnp.bfloat16), "wide").astype(jnp.float32),
        lax.psum(grad_w_out.astype(jnp.bfloat16), "wide").astype(jnp.float32),
        lax.psum(grad_w_gate.astype(jnp.bfloat16), "wide").astype(jnp.float32),
        lax.psum(grad_w_up.astype(jnp.bfloat16), "wide").astype(jnp.float32),
        lax.psum(grad_down.astype(jnp.bfloat16), "wide").astype(jnp.float32),
    )
    summed_query, summed_key, summed_value, summed_out, summed_gate, summed_up, summed_down = (
        all_summed
    )
    gain_summed = lax.psum(
        (gain_one, gain_two, query_scale_part, key_scale_part), ("wide", "narrow")
    )
    return (
        output.astype(jnp.bfloat16),
        grad_tokens,
        gain_summed[0],
        summed_query,
        summed_key,
        summed_value,
        gain_summed[2],
        gain_summed[3],
        summed_out,
        gain_summed[1],
        summed_gate,
        summed_up,
        summed_down,
    )


def solution(mesh):
    placed = (
        P(("wide", "narrow"), None),
        P("wide"),
        P(),
        P(None, "narrow"),
        P(None, "narrow"),
        P(None, "narrow"),
        P(),
        P(),
        P("narrow", None),
        P(),
        P(None, "narrow"),
        P(None, "narrow"),
        P("narrow", None),
        P(("wide", "narrow"), None),
    )
    return jax.shard_map(
        on_device,
        mesh=mesh,
        in_specs=placed,
        out_specs=(
            P(("wide", "narrow"), None),
            P(("wide", "narrow"), None),
            P(),
            P(None, "narrow"),
            P(None, "narrow"),
            P(None, "narrow"),
            P(),
            P(),
            P("narrow", None),
            P(),
            P(None, "narrow"),
            P(None, "narrow"),
            P("narrow", None),
        ),
        check_vma=False,
    )
```

profile of v0, /device:TPU:0, one launch (start us, length us, event | category | flops | bytes accessed | tf_op | source)
XLA Modules:
  0.0 990.6 jit_solution(9623713344463483777)
XLA Ops:
  13.9 36.0 %all-gather.5.cloned.1.call-done = bf16[2048,1024]{1,0:T(8,128)(2,1)} async-done(((bf16[512,1024]{1,0:T(8,128)(2,1)}), bf16[2048,1024]{1,0:T(8,128)(2,1)}) %all-gather.5.cloned.1.call-update) | async-done | bytes 4194320 | tf_op jit(solution)/shard_map/all_gather | solution.py:159
  93.2 34.4 %while.26 = (s32[]{:T(128)}, bf16[2,1024,4,64]{1,3,2,0:T(8,128)(2,1)S(1)}, f32[2,2,2,1024,1]{3,2,1,4,0:T(2,128)}, bf16[2,1024,2,64]{1,3,2,0:T(8,128)(2,1)}, s32[...) while((s32[]{:T(128)}, ...), condition=%wide.region_6.7_spmd, body=%wide.region_3.6_spmd.sunk | while | flops 1126429696 | bytes 58329216 | solution.py:179
  133.2 44.6 %reduce-scatter.5.cloned.1.call-done = bf16[512,1024]{1,0:T(8,128)(2,1)} async-done(((bf16[2048,1024]{1,0:T(8,128)(2,1)}), bf16[512,1024]{1,0:T(8,128)(2,1)}) %reduce-scatter.5.cloned.1.call-update) | async-done | bytes 1048592 | tf_op jit(solution)/shard_map/reduce_scatter | solution.py:181
  182.8 34.0 %all-gather.7.cloned.1.call-done = bf16[2048,1024]{1,0:T(8,128)(2,1)} async-done(((bf16[512,1024]{1,0:T(8,128)(2,1)}), bf16[2048,1024]{1,0:T(8,128)(2,1)}) %all-gather.7.cloned.1.call-update) | async-done | bytes 4194320 | tf_op jit(solution)/shard_map/all_gather | solution.py:189
  216.8 11.0 %fusion.72 = f32[2048,1152]{1,0:T(8,128)} fusion(bf16[2048,1024]{1,0:T(8,128)(2,1)} %all-gather.7.cloned.1.call-done, bf16[1024,1152]{1,0:T(8,128)(2,1)} %param.29), kind=kOutput, calls=%fused_computation.150 | convolution fusion | flops 4831838208 | bytes 15990784 | tf_op jit(solution)/shard_map/dot_general | solution.py:129
  235.7 17.1 %all-gather.9.cloned.1.call-done = bf16[2048,1024]{1,0:T(8,128)(2,1)} async-done(((bf16[512,1024]{1,0:T(8,128)(2,1)}), bf16[2048,1024]{1,0:T(8,128)(2,1)}) %all-gather.9.cloned.1.call-update) | async-done | bytes 4194320 | tf_op jit(solution)/shard_map/all_gather | solution.py:197
  252.8 18.3 %multiply_convert_fusion = (bf16[2048,1152]{1,0:T(8,128)(2,1)}, bf16[2048,1152]{1,0:T(8,128)(2,1)}, bf16[2048,1152]{1,0:T(8,128)(2,1)}) fusion(f32[2048,1152]{1,0:T(8,128)} %fusion.71, f32[2048,1152]{1,0:T(8,128)} %fusion.72, bf16[2048,1024]{1,0:T(8,128)(2,1)} %all-gather.9.cloned.1.call-done, bf16[1152,1024]{1,0:T(8,128)(2,1)S(1)} %copy-done), kind=kOutput, calls=%fused_computation.58 | convolution fusion | flops 4869586944 | bytes 39583744 | tf_op jit(solution)/shard_map/dot_general | solution.py:66
  286.7 44.4 %reduce-scatter.9.cloned.1.call-done = bf16[512,1024]{1,0:T(8,128)(2,1)} async-done(((bf16[2048,1024]{1,0:T(8,128)(2,1)}), bf16[512,1024]{1,0:T(8,128)(2,1)}) %reduce-scatter.9.cloned.1.call-update) | async-done | bytes 1048592 | tf_op jit(solution)/shard_map/reduce_scatter | solution.py:207
  355.5 17.5 %all-gather.11.cloned.1.call-done = bf16[2048,1024]{1,0:T(8,128)(2,1)} async-done(((bf16[512,1024]{1,0:T(8,128)(2,1)}), bf16[2048,1024]{1,0:T(8,128)(2,1)}) %all-gather.11.cloned.1.call-update) | async-done | bytes 4194320 | tf_op jit(solution)/shard_map/all_gather | solution.py:217
  382.4 164.1 %while.27 = (s32[]{:T(128)}, f32[2,1024,4,64]{1,0,3,2:T(2,128)}, f32[2,1024,2,64]{1,0,3,2:T(2,128)}, bf16[2,1024,2,64]{1,3,2,0:T(8,128)(2,1)}, bf16[2,1024,2,64]...) while((s32[]{:T(128)}, f32[2,1024,4,64]{1,0,3,2:T(2,128)}, ...), condition=%wide.region_14.15_spmd, body=%wide.region_12.14_spmd.sunk | while | flops 2749756416 | bytes 147704016 | solution.py:230
  386.3 9.2 fusion.161
  403.6 12.2 %fusion.163 = (f32[2,2,1024]{2,1,0:T(2,128)S(1)}, f32[2,1024,1024,2]{2,1,3,0:T(8,128)}) fusion(f32[2,1024,1024,2]{2,1,3,0:T(8,128)} %fusion.161, f32[2,2,1024]{2,1,0:T(2,128)S(1)} %dynamic-slice_bitcast_fusion.2, pred[1024,1024]{0,1:T(8,128)(4,1)S(1)} %fusion.162, bf16[1024,2,2,64]{0,3,2,1:T(8,128)(2,1)S(1)} %bitcast.277, ...), kind=kOutput, calls=%fused_computation.24.clone.1 | convolution fusion | flops 557838336 | bytes 35422212 | tf_op jit(solution)/shard_map/while/body/eval_jaxpr/qkgd,skd->kgqs/dot_general | solution.py:105
  415.9 12.1 %fusion.164 = bf16[2,2,1024,1024]{2,3,1,0:T(8,128)(2,1)S(1)} fusion(f32[2,1024,1024,2]{2,1,3,0:T(8,128)} %get-tuple-element.357, f32[2,1024,1024,2]{2,1,3,0:T(8,128)} %fusion.161, f32[2,2,1024]{2,1,0:T(2,128)S(1)} %get-tuple-element.358, f32[2,2,1024]{2,1,0:T(2,128)S(1)} %dynamic-slice_bitcast_fusion.2, pred[1024,1024]{0,1:T(8,128)(4,1)S(1)} %fusion.162), kind=kLoop, calls=%fused_computation.26.clone.1 | loop fusion | flops 25165824 | bytes 43024384 | tf_op jit(solution)/shard_map/while/body/eval_jaxpr/convert_element_type | solution.py:109
  435.6 10.0 %dynamic_update_slice.31 = f32[2,1024,2,64]{1,0,3,2:T(2,128)} dynamic-update-slice(f32[2,1024,2,64]{1,0,3,2:T(2,128)} %get-tuple-element.397, f32[1,1024,2,64]{1,0,3,2:T(1,128)} %copy.163, s32[]{:T(128)S(6)} %copy.182, s32[]{:T(128)} %constant.56.clone.1..sunk, s32[]{:T(128)} %constant.56.clone.1..sunk, s32[]{:T(128)} %constant.56.clone.1..sunk) | dynamic-update-slice | bytes 1048580 | tf_op jit(solution)/shard_map/while/body/jit(dynamic_update_index_in_dim)/dynamic_update_slice | solution.py:230
  445.6 18.8 %dynamic_update_slice.30 = f32[2,1024,4,64]{1,0,3,2:T(2,128)} dynamic-update-slice(f32[2,1024,4,64]{1,0,3,2:T(2,128)} %get-tuple-element.396, f32[1,1024,4,64]{1,0,3,2:T(1,128)S(1)} %copy.162, s32[]{:T(128)S(6)} %copy.182, s32[]{:T(128)} %constant.56.clone.1..sunk, s32[]{:T(128)} %constant.56.clone.1..sunk, s32[]{:T(128)} %constant.56.clone.1..sunk) | dynamic-update-slice | bytes 2097156 | tf_op jit(solution)/shard_map/while/body/jit(dynamic_update_index_in_dim)/dynamic_update_slice | solution.py:230
  485.4 12.2 %fusion.163 = (f32[2,2,1024]{2,1,0:T(2,128)S(1)}, f32[2,1024,1024,2]{2,1,3,0:T(8,128)}) fusion(f32[2,1024,1024,2]{2,1,3,0:T(8,128)} %fusion.161, f32[2,2,1024]{2,1,0:T(2,128)S(1)} %dynamic-slice_bitcast_fusion.2, pred[1024,1024]{0,1:T(8,128)(4,1)S(1)} %fusion.162, bf16[1024,2,2,64]{0,3,2,1:T(8,128)(2,1)S(1)} %bitcast.277, ...), kind=kOutput, calls=%fused_computation.24.clone.1 | convolution fusion | flops 557838336 | bytes 35422212 | tf_op jit(solution)/shard_map/while/body/eval_jaxpr/qkgd,skd->kgqs/dot_general | solution.py:105
  497.6 12.1 %fusion.164 = bf16[2,2,1024,1024]{2,3,1,0:T(8,128)(2,1)S(1)} fusion(f32[2,1024,1024,2]{2,1,3,0:T(8,128)} %get-tuple-element.357, f32[2,1024,1024,2]{2,1,3,0:T(8,128)} %fusion.161, f32[2,2,1024]{2,1,0:T(2,128)S(1)} %get-tuple-element.358, f32[2,2,1024]{2,1,0:T(2,128)S(1)} %dynamic-slice_bitcast_fusion.2, pred[1024,1024]{0,1:T(8,128)(4,1)S(1)} %fusion.162), kind=kLoop, calls=%fused_computation.26.clone.1 | loop fusion | flops 25165824 | bytes 43024384 | tf_op jit(solution)/shard_map/while/body/eval_jaxpr/convert_element_type | solution.py:109
  517.4 10.0 %dynamic_update_slice.31 = f32[2,1024,2,64]{1,0,3,2:T(2,128)} dynamic-update-slice(f32[2,1024,2,64]{1,0,3,2:T(2,128)} %get-tuple-element.397, f32[1,1024,2,64]{1,0,3,2:T(1,128)} %copy.163, s32[]{:T(128)S(6)} %copy.182, s32[]{:T(128)} %constant.56.clone.1..sunk, s32[]{:T(128)} %constant.56.clone.1..sunk, s32[]{:T(128)} %constant.56.clone.1..sunk) | dynamic-update-slice | bytes 1048580 | tf_op jit(solution)/shard_map/while/body/jit(dynamic_update_index_in_dim)/dynamic_update_slice | solution.py:230
  527.4 18.8 %dynamic_update_slice.30 = f32[2,1024,4,64]{1,0,3,2:T(2,128)} dynamic-update-slice(f32[2,1024,4,64]{1,0,3,2:T(2,128)} %get-tuple-element.396, f32[1,1024,4,64]{1,0,3,2:T(1,128)S(1)} %copy.162, s32[]{:T(128)S(6)} %copy.182, s32[]{:T(128)} %constant.56.clone.1..sunk, s32[]{:T(128)} %constant.56.clone.1..sunk, s32[]{:T(128)} %constant.56.clone.1..sunk) | dynamic-update-slice | bytes 2097156 | tf_op jit(solution)/shard_map/while/body/jit(dynamic_update_index_in_dim)/dynamic_update_slice | solution.py:230
  587.9 9.6 convolution_convert_fusion.3
  597.6 10.0 %convolution_convert_fusion = bf16[1152,1024]{1,0:T(8,128)(2,1)} fusion(bf16[2048,1152]{1,0:T(8,128)(2,1)} %get-tuple-element.218, bf16[2048,1024]{1,0:T(8,128)(2,1)} %all-gather.9.cloned.1.call-done), kind=kOutput, calls=%fused_computation.73 | convolution fusion | flops 4833017856 | bytes 11272192 | tf_op jit(solution)/shard_map/dot_general | solution.py:60
  607.6 9.5 convolution_convert_fusion.1
  671.7 42.8 %all-reduce = (f32[1024]{0:T(1024)}, f32[64]{0:T(128)}, f32[64]{0:T(128)}, f32[1024]{0:T(1024)}) all-reduce(f32[1024]{0:T(1024)S(1)} %get-tuple-element.163, f32[64]{0:T(128)S(1)} %fusion.46, f32[64]{0:T(128)S(1)} %fusion.65, f32[1024]{0:T(1024)S(1)} %copy-done.62), channel_id=1, replica_groups=mesh['wide'=8,'narrow'=4] {'wide','narrow'}, use_global_device_ids=true, to_apply=%region_20.21 | all-reduce | flops 2176 | bytes 17408 | tf_op jit(solution)/shard_map/psum | solution.py:269
  719.0 248.8 %all-reduce.4.cloned.1.call-done = (bf16[1024,256]{1,0:T(8,128)(2,1)}, bf16[1024,128]{1,0:T(8,128)(2,1)}, bf16[1024,128]{1,0:T(8,128)(2,1)}, bf16[256,1024]{1,0:...) async-done(((bf16[1024,256]{1,0:T(8,128)(2,1)}, bf16[1024,128]{1,0:T(8,128)(2,1)}, bf16[1024,128]{1,0:T(8,128)(2,1)}, ...) | async-done | bytes 8650768 | tf_op jit(solution)/shard_map/psum | solution.py:258
  (340 shorter events, 315.6 us)
Async XLA Ops:
  7.2 245.6 %copy-start = (bf16[1152,1024]{1,0:T(8,128)(2,1)S(1)}, bf16[1152,1024]{1,0:T(8,128)(2,1)}, u32[]{:S(2)}) copy-start(bf16[1152,1024]{1,0:T(8,128)(2,1)} %param.30) | copy-start | bytes 7077892
  7.2 42.8 %all-gather.5.cloned.1.call-start = ((), (), s32[]{:S(2)}) async-start(), calls=%async_computation.4 | async-start | bytes 5242880 | tf_op jit(solution)/shard_map/all_gather | solution.py:159
  12.6 165.2 %reduce-scatter.5.cloned.1.call-start = ((), (), s32[]{:S(2)}) async-start(), calls=%async_computation.5 | async-start | bytes 5242880 | tf_op jit(solution)/shard_map/reduce_scatter | solution.py:181
  13.9 75.2 %copy-start.24 = (f32[1024,32]{0,1:T(8,128)}, f32[1024,32]{0,1:T(8,128)S(1)}, u32[]{:S(2)}) copy-start(f32[1024,32]{0,1:T(8,128)S(1)} %get-tuple-element.241) | copy-start | bytes 393220
  133.2 44.7 %copy-start.1 = (bf16[512,1024]{1,0:T(8,128)(2,1)S(1)}, bf16[512,1024]{1,0:T(8,128)(2,1)}, u32[]{:S(2)}) copy-start(bf16[512,1024]{1,0:T(8,128)(2,1)} %param.18) | copy-start | bytes 3145732
  133.2 46.4 %copy-start.50 = (f32[1024]{0:T(1024)S(1)}, f32[1024]{0:T(1024)}, u32[]{:S(2)}) copy-start(f32[1024]{0:T(1024)} %param.27) | copy-start | bytes 12292
  133.2 83.6 %all-gather.7.cloned.1.call-start = ((), (), s32[]{:S(2)}) async-start(), calls=%async_computation.6 | async-start | bytes 5242880 | tf_op jit(solution)/shard_map/all_gather | solution.py:189
  179.5 154.6 %copy-start.53 = (f32[512]{0:T(512)}, f32[512]{0:T(512)S(1)}, u32[]{:S(2)}) copy-start(f32[512]{0:T(512)S(1)} %get-tuple-element.240) | copy-start | bytes 6148
  179.5 154.6 %copy-start.58 = (f32[512]{0:T(512)}, f32[512]{0:T(512)S(1)}, u32[]{:S(2)}) copy-start(f32[512]{0:T(512)S(1)} %get-tuple-element.239) | copy-start | bytes 6148
  182.1 70.6 %all-gather.9.cloned.1.call-start = ((), (), s32[]{:S(2)}) async-start(), calls=%async_computation.8 | async-start | bytes 5242880 | tf_op jit(solution)/shard_map/all_gather | solution.py:197
  182.7 148.4 %reduce-scatter.9.cloned.1.call-start = ((), (), s32[]{:S(2)}) async-start(), calls=%async_computation.9 | async-start | bytes 5242880 | tf_op jit(solution)/shard_map/reduce_scatter | solution.py:207
  286.4 52.0 %copy-start.69 = (f32[64]{0:T(128)S(1)}, f32[64]{0:T(128)}, u32[]{:S(2)}) copy-start(f32[64]{0:T(128)} %param.25) | copy-start | bytes 772
  286.4 52.6 %copy-start.65 = (f32[64]{0:T(128)S(1)}, f32[64]{0:T(128)}, u32[]{:S(2)}) copy-start(f32[64]{0:T(128)} %param.24) | copy-start | bytes 772
  286.4 53.3 %copy-start.52 = (f32[2,1024,2]{1,0,2:T(2,128)S(1)}, f32[2,1024,2]{1,0,2:T(2,128)}, u32[]{:S(2)}) copy-start(f32[2,1024,2]{1,0,2:T(2,128)} %get-tuple-element.235) | copy-start | bytes 49156
  286.5 86.5 %all-gather.11.cloned.1.call-start = ((), (), s32[]{:S(2)}) async-start(), calls=%async_computation.10 | async-start | bytes 5242880 | tf_op jit(solution)/shard_map/all_gather | solution.py:217
  338.3 331.2 %reduce-scatter.11.cloned.1.call-start = ((), (), s32[]{:S(2)}) async-start(), calls=%async_computation.11 | async-start | bytes 5242880 | tf_op jit(solution)/shard_map/reduce_scatter | solution.py:245
  382.4 166.8 %copy-start.25 = (f32[1024,32]{0,1:T(8,128)S(1)}, f32[1024,32]{0,1:T(8,128)}, u32[]{:S(2)}) copy-start(f32[1024,32]{0,1:T(8,128)} %copy-done.24) | copy-start | bytes 393220
  587.9 126.6 %reduce-scatter.7.cloned.1.call-start = ((), (), s32[]{:S(2)}) async-start(), calls=%async_computation.7 | async-start | bytes 5242880 | tf_op jit(solution)/shard_map/reduce_scatter | solution.py:191
  597.5 370.3 %all-reduce.4.cloned.1.call-start = ((), (), s32[]{:S(2)}) async-start(), calls=%async_computation.12 | async-start | bytes 17301504 | tf_op jit(solution)/shard_map/psum | solution.py:258
  664.7 49.7 %copy-start.51 = (f32[1024]{0:T(1024)S(1)}, f32[1024]{0:T(1024)}, u32[]{:S(2)}) copy-start(f32[1024]{0:T(1024)} %param.27) | copy-start | bytes 12292
  664.8 49.7 %copy-start.54 = (f32[512]{0:T(512)S(1)}, f32[512]{0:T(512)}, u32[]{:S(2)}) copy-start(f32[512]{0:T(512)} %copy-done.53) | copy-start | bytes 6148
  664.8 49.7 %copy-start.59 = (f32[512]{0:T(512)S(1)}, f32[512]{0:T(512)}, u32[]{:S(2)}) copy-start(f32[512]{0:T(512)} %copy-done.58) | copy-start | bytes 6148
  664.8 49.7 %copy-start.61 = (f32[512]{0:T(512)S(1)}, f32[512]{0:T(512)}, u32[]{:S(2)}) copy-start(f32[512]{0:T(512)} %copy-done.60) | copy-start | bytes 6148
  664.8 49.7 %copy-start.63 = (f32[512]{0:T(512)S(1)}, f32[512]{0:T(512)}, u32[]{:S(2)}) copy-start(f32[512]{0:T(512)} %get-tuple-element.237) | copy-start | bytes 6148
  (69 other events, 417.2 us)
Sparse Core Ops, SparseCore 0:
  12.8 37.1 all-gather.4
  133.3 44.4 reduce-scatter.4
  182.3 34.4 all-gather.6
  218.3 34.4 all-gather.8
  286.5 44.5 reduce-scatter.8
  338.5 34.4 all-gather.10
  588.0 44.5 reduce-scatter.10
  635.2 44.5 reduce-scatter.6
  685.9 281.9 all-reduce.3
where the time goes:
time: 999 us; the launch traced here: 991 us
  waiting for transfers between devices  443 us (44%)
  matrix products  210 us (21%)
  local copies, waits for them, and re-layouts  167 us (17%)
  other arithmetic  112 us (11%)
  blocking collectives  42.8 us (4%)
  between operations  15.1 us (2%)
    psum x1, waiting for transfers between devices, on_device(): lax.psum(grad_w_query.astype(jnp.bfloat16), 'wide').astype(jnp.float32)  249 us
    dynamic_update_slice x8, local copies, waits for them, and re-layouts, on_device(): lax.map(back_entry, (queries, keys, value_heads, log_total, grad_mixed, l...  62.4 us
    reduce_scatter x1, waiting for transfers between devices, on_device(): lax.psum_scatter(jnp.dot(mixed_heads, w_out, preferred_element_type=jnp.f...  44.6 us
    reduce_scatter x1, waiting for transfers between devices, on_device(): lax.psum_scatter((times_transposed(grad_gate, w_gate) + times_transposed(...  44.4 us
    dot_general x7, matrix products, times_transposed(): lax.dot_general(left_side, right_side, (((1,), (1,)), ((), ())), preferre...  43 us
    psum x1, blocking collectives, on_device(): lax.psum((gain_one, gain_two, query_scale_part, key_scale_part), ('wide',...  42.8 us
    all_gather x1, waiting for transfers between devices, on_device(): rows_one = lax.all_gather(normed_low_one, 'narrow', axis=0, tiled=True)  36 us
    dot_general x7, matrix products, contract_rows(): lax.dot_general(left_side, right_side, (((0,), (0,)), ((), ())), preferre...  35 us
  transfers between devices with their start and end apart: 9, of which 7 were waited for; matrix products, arithmetic and copies ran while one was open for 12% of the time, Pallas kernels for 0%

commit v1 on v0

v1 whole, which is shorter than its diff:
```python
import functools
import math

import jax
import jax.numpy as jnp
from jax import lax
from jax.experimental import pallas as pl
from jax.experimental.pallas import tpu as pltpu
from jax.sharding import PartitionSpec as P

HD = 64
LEN = 1024
BLK = 256
TILE = 2 * HD

EPSILON = 1e-05
ROPE_BASE = 1000000.0
F32 = jnp.float32
BF16 = jnp.bfloat16
VMEM_LIMIT = 48 * 1024 * 1024


def rope_tables(length, width):
    half_width = width // 2
    frequency = ROPE_BASE ** (-(2.0 * jnp.arange(half_width, dtype=jnp.float32)) / width)
    angles = jnp.arange(length, dtype=jnp.float32)[:, None] * frequency[None, :]
    return (jnp.cos(angles), jnp.sin(angles))


def row_norm(values_in, gain_vec):
    inv_rms = lax.rsqrt(jnp.mean(values_in * values_in, axis=-1, keepdims=True) + EPSILON)
    return (values_in * inv_rms * gain_vec, inv_rms)


def row_norm_back(values_in, inv_rms, gain_vec, grad_in):
    scaled = grad_in * gain_vec
    back_part = inv_rms * scaled - values_in * (inv_rms * inv_rms * inv_rms) * jnp.mean(
        values_in * scaled, axis=-1, keepdims=True
    )
    gain_part = jnp.sum((grad_in * values_in * inv_rms).reshape(-1, values_in.shape[-1]), axis=0)
    return (back_part, gain_part)


def contract(left_side, right_side, left_dim, right_dim):
    return lax.dot_general(
        left_side,
        right_side,
        (((left_dim,), (right_dim,)), ((), ())),
        preferred_element_type=F32,
    )


def lanes(shape):
    return lax.broadcasted_iota(jnp.int32, shape, 1)


def group_ones():
    rows = lax.broadcasted_iota(jnp.int32, (TILE, TILE), 0) // HD
    cols = lax.broadcasted_iota(jnp.int32, (TILE, TILE), 1) // HD
    return jnp.where(rows == cols, 1.0, 0.0).astype(BF16)


def group_sum(values_in, ones):
    high = values_in.astype(BF16)
    rest = (values_in - high.astype(F32)).astype(BF16)
    return contract(high, ones, 1, 0) + contract(rest, ones, 1, 0)


def swap_halves(values_in):
    half = HD // 2
    front = lax.rem(lanes(values_in.shape), HD) < half
    return jnp.where(
        front, pltpu.roll(values_in, TILE - half, 1), pltpu.roll(values_in, half, 1)
    )


def attention_forward(
    len_ref, x_ref, wq_ref, wk_ref, wv_ref, qs_ref, ks_ref, cos_ref, sin_ref,
    att_ref, q_ref, k_ref, v_ref, qraw_ref, kraw_ref, rinv_ref,
    vaug_ref,
):
    length = len_ref[0]
    heads = wk_ref.shape[1] // HD
    ones = group_ones()

    def norm_rope(raw, scale, cosine, sine):
        inv = lax.rsqrt(group_sum(raw * raw, ones) * (1.0 / HD) + EPSILON)
        scaled = raw * inv * scale
        return scaled * cosine + swap_halves(scaled) * sine

    for start in range(0, LEN, BLK):
        rows = slice(start, start + BLK)
        x = x_ref[rows, :]
        cosine, sine = cos_ref[rows, :], sin_ref[rows, :]
        real = (lax.broadcasted_iota(jnp.int32, (BLK, TILE), 0) + start) < length
        q_raw = contract(x, wq_ref[...], 1, 0)
        qraw_ref[rows, :] = q_raw
        for t in range(heads):
            cols = slice(t * TILE, (t + 1) * TILE)
            turned = norm_rope(q_raw[:, cols], qs_ref[...], cosine, sine)
            q_ref[rows, cols] = (turned * (1.0 / math.sqrt(HD))).astype(BF16)
        k_raw = contract(x, wk_ref[...], 1, 0)
        kraw_ref[rows, :] = k_raw
        v_raw = contract(x, wv_ref[...], 1, 0)
        for t in range(heads // 2):
            cols = slice(t * TILE, (t + 1) * TILE)
            turned = norm_rope(k_raw[:, cols], ks_ref[...], cosine, sine)
            k_ref[rows, cols] = jnp.where(real, turned, 0.0).astype(BF16)
            v_pair = jnp.where(real, v_raw[:, cols], 0.0)
            v_ref[rows, cols] = v_pair.astype(BF16)
            lane = lanes((BLK, TILE))
            mark = jnp.where(real & (lane == HD), 1.0, 0.0)
            vaug_ref[2 * t, rows, :] = jnp.where(lane < HD, v_pair, mark).astype(BF16)
            vaug_ref[2 * t + 1, rows, :] = jnp.where(
                lane < HD, pltpu.roll(v_pair, HD, 1), mark
            ).astype(BF16)

    row_ids = lax.rem(lax.broadcasted_iota(jnp.int32, (2 * BLK, BLK), 0), BLK)
    causal = lax.broadcasted_iota(jnp.int32, (2 * BLK, BLK), 1) <= row_ids
    for h in range(heads):
        for i in range(LEN // BLK):
            rows = slice(i * BLK, (i + 1) * BLK)
            low = h * TILE
            q_two = jnp.concatenate(
                [q_ref[rows, low : low + HD], q_ref[rows, low + HD : low + TILE]], axis=0
            )
            total = jnp.zeros((2 * BLK, TILE), F32)
            for j in range(i + 1):
                keys = slice(j * BLK, (j + 1) * BLK)
                scores = contract(q_two, k_ref[keys, h * HD : (h + 1) * HD], 1, 1)
                weight = jnp.exp(scores)
                if i == j:
                    weight = jnp.where(causal, weight, 0.0)
                total += contract(weight.astype(BF16), vaug_ref[h, keys, :], 1, 0)
            inv = 1.0 / total[:, HD : HD + 1]
            mixed = total[:, :HD] * inv
            att_ref[rows, low : low + HD] = mixed[:BLK].astype(BF16)
            att_ref[rows, low + HD : low + TILE] = mixed[BLK:].astype(BF16)
            rinv_ref[rows, low : low + HD] = jnp.broadcast_to(inv[:BLK], (BLK, HD))
            rinv_ref[rows, low + HD : low + TILE] = jnp.broadcast_to(inv[BLK:], (BLK, HD))


def attention_backward(
    len_ref, g_ref, wo_ref, q_ref, k_ref, v_ref, att_ref, qraw_ref, kraw_ref, rinv_ref,
    qs_ref, ks_ref, cos_ref, sin_ref,
    gq_ref, gk_ref, gv_ref, qsg_ref, ksg_ref,
    vaug_ref, aug_ref, dk_ref, dv_ref,
):
    length = len_ref[0]
    heads = k_ref.shape[1] // HD
    ones = group_ones()
    lane = lanes((BLK, TILE))

    for start in range(0, LEN, BLK):
        rows = slice(start, start + BLK)
        grad = contract(g_ref[rows, :], wo_ref[...], 1, 1).astype(BF16).astype(F32)
        for t in range(heads):
            cols = slice(t * TILE, (t + 1) * TILE)
            part = (grad[:, cols] * rinv_ref[rows, cols]).astype(BF16).astype(F32)
            inner = group_sum(part * att_ref[rows, cols].astype(F32), ones)
            for which in range(2):
                mine = part if which == 0 else pltpu.roll(part, HD, 1)
                sums = pltpu.roll(inner, HD, 1) if which == 0 else inner
                high = sums.astype(BF16).astype(F32)
                tail = jnp.where(
                    lane == HD, -high, jnp.where(lane == HD + 1, high - sums, 0.0)
                )
                aug_ref[2 * t + which, rows, :] = jnp.where(lane < HD, mine, tail).astype(BF16)
        for t in range(heads // 2):
            v_pair = v_ref[rows, t * TILE : (t + 1) * TILE].astype(F32)
            mark = jnp.where(lane < HD + 2, 1.0, 0.0)
            vaug_ref[2 * t, rows, :] = jnp.where(lane < HD, v_pair, mark).astype(BF16)
            vaug_ref[2 * t + 1, rows, :] = jnp.where(
                lane < HD, pltpu.roll(v_pair, HD, 1), mark
            ).astype(BF16)

    dk_ref[...] = jnp.zeros_like(dk_ref)
    dv_ref[...] = jnp.zeros_like(dv_ref)
    col_ids = lax.rem(lax.broadcasted_iota(jnp.int32, (BLK, 2 * BLK), 1), BLK)
    causal = lax.broadcasted_iota(jnp.int32, (BLK, 2 * BLK), 0) <= col_ids

    def turn_back(grad, cosine, sine):
        return grad * cosine - swap_halves(grad) * sine

    def norm_back(raw, turned, scale):
        inv = lax.rsqrt(group_sum(raw * raw, ones) * (1.0 / HD) + EPSILON)
        scaled = turned * scale
        unit = raw * inv
        inner = group_sum(unit * scaled, ones) * (1.0 / HD)
        gain = jnp.sum(turned * unit, axis=0, keepdims=True)
        return inv * (scaled - unit * inner), gain

    q_gain = jnp.zeros((1, TILE), F32)
    for h in range(heads):
        keys_turned = jnp.transpose(
            k_ref[:, (h // 2) * TILE : (h // 2 + 1) * TILE].astype(F32)
        )[(h % 2) * HD : (h % 2 + 1) * HD].astype(BF16)
        for i in range(LEN // BLK):
            rows = slice(i * BLK, (i + 1) * BLK)
            low = h * TILE
            q_two = jnp.concatenate(
                [q_ref[rows, low : low + HD], q_ref[rows, low + HD : low + TILE]], axis=0
            )
            aug = jnp.concatenate([aug_ref[2 * h, rows, :], aug_ref[2 * h + 1, rows, :]], axis=0)
            dq = jnp.zeros((HD, 2 * BLK), F32)
            for j in range(i + 1):
                keys = slice(j * BLK, (j + 1) * BLK)
                weight = jnp.exp(contract(k_ref[keys, h * HD : (h + 1) * HD], q_two, 1, 1))
                if i == j:
                    weight = jnp.where(causal, weight, 0.0)
                slope = (weight * contract(vaug_ref[h, keys, :], aug, 1, 1)).astype(BF16)
                dv_ref[h, keys, :] += contract(weight.astype(BF16), aug, 1, 0)
                dk_ref[h, keys, :] += contract(slope, q_two, 1, 0)
                dq += contract(keys_turned[:, keys], slope, 1, 0)
            both = jnp.concatenate([dq[:, :BLK], dq[:, BLK:]], axis=0)
            grad = jnp.transpose(both) * (1.0 / math.sqrt(HD))
            cols = slice(low, low + TILE)
            turned = turn_back(grad, cos_ref[rows, :], sin_ref[rows, :])
            out, gain = norm_back(qraw_ref[rows, cols], turned, qs_ref[...])
            gq_ref[rows, cols] = out.astype(BF16)
            q_gain += gain
    qsg_ref[...] = q_gain

    k_gain = jnp.zeros((1, TILE), F32)
    for start in range(0, LEN, BLK):
        rows = slice(start, start + BLK)
        real = (lax.broadcasted_iota(jnp.int32, (BLK, TILE), 0) + start) < length
        for t in range(heads // 2):
            cols = slice(t * TILE, (t + 1) * TILE)
            grad = jnp.concatenate([dk_ref[2 * t, rows, :], dk_ref[2 * t + 1, rows, :]], axis=1)
            grad = jnp.where(real, grad, 0.0)
            turned = turn_back(grad, cos_ref[rows, :], sin_ref[rows, :])
            out, gain = norm_back(kraw_ref[rows, cols], turned, ks_ref[...])
            gk_ref[rows, cols] = out.astype(BF16)
            k_gain += gain
            values = jnp.where(
                lane < HD, dv_ref[2 * t, rows, :], pltpu.roll(dv_ref[2 * t + 1, rows, :], HD, 1)
            )
            gv_ref[rows, cols] = jnp.where(real, values, 0.0).astype(BF16)
    ksg_ref[...] = k_gain


VM = pl.BlockSpec(memory_space=pltpu.VMEM)
SM = pl.BlockSpec(memory_space=pltpu.SMEM)


def run_forward(length, rows, wq, wk, wv, qs, ks, cosine, sine):
    nq, nk = wq.shape[1], wk.shape[1]
    shape = jax.ShapeDtypeStruct
    return pl.pallas_call(
        attention_forward,
        out_shape=(
            shape((LEN, nq), BF16),
            shape((LEN, nq), BF16),
            shape((LEN, nk), BF16),
            shape((LEN, nk), BF16),
            shape((LEN, nq), F32),
            shape((LEN, nk), F32),
            shape((LEN, nq), F32),
        ),
        in_specs=[SM] + [VM] * 8,
        out_specs=[VM] * 7,
        scratch_shapes=[pltpu.VMEM((nk // HD, LEN, TILE), BF16)],
        compiler_params=pltpu.CompilerParams(vmem_limit_bytes=VMEM_LIMIT),
        cost_estimate=pl.CostEstimate(
            flops=2 * LEN * rows.shape[1] * 2 * nq + 8 * LEN * LEN * nq,
            bytes_accessed=8 * 1024 * 1024,
            transcendentals=0,
        ),
        name="attention_forward",
    )(length, rows, wq, wk, wv, qs, ks, cosine, sine)


def run_backward(length, grads, wo, q, k, v, att, q_raw, k_raw, rinv, qs, ks, cosine, sine):
    nq, nk = q.shape[1], k.shape[1]
    heads = nk // HD
    shape = jax.ShapeDtypeStruct
    return pl.pallas_call(
        attention_backward,
        out_shape=(
            shape((LEN, nq), BF16),
            shape((LEN, nk), BF16),
            shape((LEN, nk), BF16),
            shape((1, TILE), F32),
            shape((1, TILE), F32),
        ),
        in_specs=[SM] + [VM] * 13,
        out_specs=[VM] * 5,
        scratch_shapes=[
            pltpu.VMEM((heads, LEN, TILE), BF16),
            pltpu.VMEM((2 * heads, LEN, TILE), BF16),
            pltpu.VMEM((heads, LEN, HD), F32),
            pltpu.VMEM((heads, LEN, TILE), F32),
        ],
        compiler_params=pltpu.CompilerParams(vmem_limit_bytes=VMEM_LIMIT),
        cost_estimate=pl.CostEstimate(
            flops=2 * LEN * grads.shape[1] * nq + 24 * LEN * LEN * nq,
            bytes_accessed=8 * 1024 * 1024,
            transcendentals=0,
        ),
        name="attention_backward",
    )(length, grads, wo, q, k, v, att, q_raw, k_raw, rinv, qs, ks, cosine, sine)


def ring_order(count):
    side = 2 ** (int(math.log2(count)) // 2) if count > 1 else 1
    tall = count // side
    order = [0]
    for col in range(tall):
        steps = range(1, side) if col % 2 == 0 else range(side - 1, 0, -1)
        order += [col * side + s for s in steps]
    order += [col * side for col in range(tall - 1, 0, -1)]
    return order


def on_device(
    wide, narrow,
    tokens, lengths, norm_gain, w_query, w_key, w_value, query_scale, key_scale, w_out,
    ffn_gain, w_gate, w_up, w_down, cotangent,
):
    sequences = lengths.shape[0]
    side = narrow // sequences
    own = tokens.shape[0]
    me = lax.axis_index("narrow")
    place, mine = lax.rem(me, side), me // side

    def across(array, turn=1):
        return lax.ppermute(
            array, "narrow", [(i, (i + turn * side) % narrow) for i in range(narrow)]
        )

    def within(array, turn):
        return lax.ppermute(
            array,
            "narrow",
            [(i, (i // side) * side + (i % side + turn) % side) for i in range(narrow)],
        )

    def gather(array):
        size = array.shape[0]
        whole = jnp.zeros((side * size,) + array.shape[1:], array.dtype)
        whole = lax.dynamic_update_slice(whole, array, (place * size, 0))
        for turn in range(1, side):
            source = lax.rem(place + side - turn, side)
            whole = lax.dynamic_update_slice(whole, within(array, turn), (source * size, 0))
        return whole

    def scatter(parts):
        size = parts.shape[0] // side
        total = lax.dynamic_slice_in_dim(parts, place * size, size).astype(F32)
        for turn in range(1, side):
            target = lax.rem(place + turn, side)
            total += within(
                lax.dynamic_slice_in_dim(parts, target * size, size).astype(BF16), turn
            ).astype(F32)
        return total

    cosine, sine = rope_tables(LEN, HD)
    cosine = jnp.concatenate([cosine] * 4, axis=1)
    sine = jnp.concatenate([-sine, sine, -sine, sine], axis=1)
    qs = jnp.concatenate([query_scale] * 2)[None, :]
    ks = jnp.concatenate([key_scale] * 2)[None, :]
    length = lax.dynamic_slice_in_dim(lengths, mine, 1)

    weights = [(w_query, w_key, w_value, w_out)]
    weights += [tuple(across(w, t) for w in weights[0]) for t in range(1, sequences)]
    joined = w_key.shape[1] % TILE != 0
    if joined:
        weights = [
            tuple(jnp.concatenate(ws, axis=1 if n < 3 else 0) for n, ws in enumerate(zip(*weights)))
        ]

    residual = tokens.astype(F32)
    normed_one, inv_one = row_norm(residual, norm_gain)
    rows_one = gather(normed_one.astype(BF16))
    saved = [run_forward(length, rows_one, *w[:3], qs, ks, cosine, sine) for w in weights]
    mixed = contract(saved[0][0], weights[0][3], 1, 0)
    for s, w in zip(saved[1:], weights[1:]):
        mixed += contract(s[0], w[3], 1, 0)
    middle = residual + scatter(mixed)

    normed_two, inv_two = row_norm(middle, ffn_gain)
    low_two = normed_two.astype(BF16)

    blocks = []
    for turn in range(sequences):
        rows = gather(across(low_two, turn) if turn else low_two)
        grads = gather(across(cotangent, turn) if turn else cotangent)
        gate_pre = contract(rows, w_gate, 1, 0)
        up_pre = contract(rows, w_up, 1, 0)
        sigmoid_gate = jax.nn.sigmoid(gate_pre)
        hidden = (gate_pre * sigmoid_gate * up_pre).astype(BF16)
        grad_hidden = contract(grads, w_down, 1, 1)
        grad_gate = (
            grad_hidden * up_pre * sigmoid_gate * (1.0 + gate_pre * (1.0 - sigmoid_gate))
        ).astype(BF16)
        grad_up = (grad_hidden * gate_pre * sigmoid_gate).astype(BF16)
        back = contract(grad_gate, w_gate, 1, 1) + contract(grad_up, w_up, 1, 1)
        blocks.append((rows, grads, hidden, grad_gate, grad_up, back))

    def to_owners(parts):
        total = scatter(parts[0])
        for turn in range(1, sequences):
            total += across(scatter(parts[turn]).astype(BF16), sequences - turn).astype(F32)
        return total

    grad_normed_two = to_owners([b[5] for b in blocks])
    rows_two, grad_rows, hidden, grad_gate, grad_up = (
        jnp.concatenate([b[n] for b in blocks], axis=0) for n in range(5)
    )
    output = middle + to_owners([contract(b[2], w_down, 1, 0) for b in blocks])
    grad_down = contract(hidden, grad_rows, 0, 0).astype(BF16)
    grad_w_gate = contract(rows_two, grad_gate, 0, 0).astype(BF16)
    grad_w_up = contract(rows_two, grad_up, 0, 0).astype(BF16)

    back_two, gain_two = row_norm_back(middle, inv_two, ffn_gain, grad_normed_two)
    grad_middle = cotangent.astype(F32) + back_two
    branch = gather(grad_middle.astype(BF16))

    q_gain, k_gain = 0.0, 0.0
    back_one = 0.0
    weight_grads = []
    for s, (wq, wk, wv, wo) in zip(saved, weights):
        att, q, k, v, q_raw, k_raw, rinv = s
        gq, gk, gv, qg, kg = run_backward(
            length, branch, wo, q, k, v, att, q_raw, k_raw, rinv, qs, ks, cosine, sine
        )
        q_gain += qg[0, :HD] + qg[0, HD:]
        k_gain += kg[0, :HD] + kg[0, HD:]
        back_one += contract(gq, wq, 1, 1) + contract(gk, wk, 1, 1) + contract(gv, wv, 1, 1)
        weight_grads.append(
            (
                contract(rows_one, gq, 0, 0),
                contract(rows_one, gk, 0, 0),
                contract(rows_one, gv, 0, 0),
                contract(att, branch, 0, 0),
            )
        )
    if joined:
        weight_grads = [
            tuple(
                jnp.split(w, sequences, axis=1 if n < 3 else 0)[p]
                for n, w in enumerate(weight_grads[0])
            )
            for p in range(sequences)
        ]
    own_grads = list(weight_grads[0])
    for turn in range(1, sequences):
        for n in range(4):
            own_grads[n] += across(weight_grads[turn][n].astype(BF16), sequences - turn).astype(F32)
    grad_normed_one = scatter(back_one)
    back_one, gain_one = row_norm_back(residual, inv_one, norm_gain, grad_normed_one)
    grad_tokens = grad_middle + back_one

    grad_down, grad_w_gate, grad_w_up = lax.psum((grad_down, grad_w_gate, grad_w_up), "wide")
    grad_down, grad_w_gate, grad_w_up, *own_grads = lax.optimization_barrier(
        (grad_down, grad_w_gate, grad_w_up, *own_grads)
    )
    summed = lax.psum(tuple(g.astype(BF16) for g in own_grads), "wide")
    gain_summed = lax.psum((gain_one, gain_two, q_gain, k_gain), ("wide", "narrow"))
    return (
        output.astype(BF16),
        grad_tokens,
        gain_summed[0],
        summed[0].astype(F32),
        summed[1].astype(F32),
        summed[2].astype(F32),
        gain_summed[2],
        gain_summed[3],
        summed[3].astype(F32),
        gain_summed[1],
        grad_w_gate.astype(F32),
        grad_w_up.astype(F32),
        grad_down.astype(F32),
    )


def solution(mesh):
    rows = P(("wide", "narrow"), None)
    columns, depth, copied = P(None, "narrow"), P("narrow", None), P()
    return jax.shard_map(
        functools.partial(on_device, mesh.shape["wide"], mesh.shape["narrow"]),
        mesh=mesh,
        in_specs=(
            rows, P("wide"), copied, columns, columns, columns, copied, copied, depth,
            copied, columns, columns, depth, rows,
        ),
        out_specs=(
            rows, rows, copied, columns, columns, columns, copied, copied, depth,
            copied, columns, columns, depth,
        ),
        check_vma=False,
    )
```

time: 999 us -> 573 us (0.57)
  waiting for transfers between devices: 443 us -> 259 us
  local copies, waits for them, and re-layouts: 167 us -> 29 us
  matrix products: 210 us -> 114 us
  other arithmetic: 112 us -> 36.4 us
  Pallas kernels: 0 us -> 49.6 us
  starting transfers between devices: 0.54 us -> 18.9 us
    all_gather x4 -> x0, waiting for transfers between devices: 105 us -> none  [the longest x1 36 us: on_device(): rows_one = lax.all_gather(normed_low_one, 'narrow', axis=0, tiled=True)]
    dot_general x35 -> x31, matrix products: 210 us -> 114 us  [contract(): lax.dot_general(left_side, right_side, (((left_dim,), (right_dim,)), ((),...]
    reduce_scatter x4 -> x0, waiting for transfers between devices: 89.1 us -> none  [the longest x1 44.6 us: on_device(): lax.psum_scatter(jnp.dot(mixed_heads, w_out, preferred_element_type=jnp.f...]
    ppermute x0 -> x24, waiting for transfers between devices: none -> 56.1 us  [the longest x12 56.1 us: across(): lax.ppermute(array, 'narrow', [(i, (i + turn * side) % narrow) for i in r...]
    dynamic_update_slice x10 -> x9, local copies, waits for them, and re-layouts: 62.5 us -> 6.93 us  [the longest x6 4.16 us: gather(): lax.dynamic_update_slice(whole, within(array, turn), (source * size, 0))]
    pallas_call x0 -> x4, Pallas kernels: none -> 49.6 us  [the longest x2 29.9 us: run_backward(): pl.pallas_call(attention_backward, out_shape=(shape((LEN, nq), BF16), sha...]
    psum x1 -> x2, waiting for transfers between devices: 249 us -> 203 us  [the longest x1 164 us: on_device(): lax.psum((grad_down, grad_w_gate, grad_w_up), 'wide')]
    convert_element_type x14 -> x9, other arithmetic: 53.8 us -> 14.3 us  [the longest x1 2.72 us: on_device(): grad_down.astype(F32)]
  transfers between devices with their start and end apart: 9 -> 26, of which waited for: 7 -> 7; matrix products, arithmetic and copies ran while one was open for 12% -> 26% of each run, Pallas kernels for 0% -> 9%
where the time goes in v1:
time: 573 us; the launch traced here: 563 us
  waiting for transfers between devices  259 us (45%)
  matrix products  114 us (20%)
  Pallas kernels  49.6 us (9%)
  blocking collectives  40.8 us (7%)
  other arithmetic  36.4 us (6%)
  local copies, waits for them, and re-layouts  29 us (5%)
  starting transfers between devices  18.9 us (3%)
  between operations  15.2 us (3%)
    psum x1, waiting for transfers between devices, on_device(): lax.psum((grad_down, grad_w_gate, grad_w_up), 'wide')  164 us
    dot_general x31, matrix products, contract(): lax.dot_general(left_side, right_side, (((left_dim,), (right_dim,)), ((),...  114 us
    ppermute x12, waiting for transfers between devices, across(): lax.ppermute(array, 'narrow', [(i, (i + turn * side) % narrow) for i in r...  56.1 us
    psum x1, blocking collectives, on_device(): lax.psum((gain_one, gain_two, q_gain, k_gain), ('wide', 'narrow'))  40.8 us
    psum x1, waiting for transfers between devices, on_device(): summed = lax.psum(tuple((g.astype(BF16) for g in own_grads)), 'wide')  38.9 us
    pallas_call x2, Pallas kernels, run_backward(): pl.pallas_call(attention_backward, out_shape=(shape((LEN, nq), BF16), sha...  29.9 us
    pallas_call x2, Pallas kernels, run_forward(): pl.pallas_call(attention_forward, out_shape=(shape((LEN, nq), BF16), shap...  19.7 us
    ppermute x12, starting transfers between devices, across(): lax.ppermute(array, 'narrow', [(i, (i + turn * side) % narrow) for i in r...  15.7 us
  transfers between devices with their start and end apart: 26, of which 7 were waited for; matrix products, arithmetic and copies ran while one was open for 26% of the time, Pallas kernels for 9%

profile of v1, /device:TPU:0, one launch (start us, length us, event | category | flops | bytes accessed | tf_op | source)
XLA Modules:
  0.0 563.1 jit_solution(9362332887976483528)
XLA Ops:
  25.4 9.7 %attention_forward.2 = (bf16[1024,256]{1,0:T(8,128)(2,1)S(1)}, bf16[1024,256]{1,0:T(8,128)(2,1)S(1)}, bf16[1024,128]{1,0:T(8,128)(2,1)S(1)}, bf16[1024,128]{1,0:...) custom-call(s32[1]{0:T(128)} %dynamic_slice.39.len_ref, ...), custom_call_target="tpu_custom_call" | custom-call | flops 3221225472 | bytes 8388608 | tf_op jit(solution)/shard_map/attention_forward/pallas_call | solution.py:250
  39.4 10.0 %attention_forward.3 = (bf16[1024,256]{1,0:T(8,128)(2,1)S(1)}, bf16[1024,256]{1,0:T(8,128)(2,1)S(1)}, bf16[1024,128]{1,0:T(8,128)(2,1)S(1)}, bf16[1024,128]{1,0:...) custom-call(s32[1]{0:T(128)} %dynamic_slice.39.len_ref, ...), custom_call_target="tpu_custom_call" | custom-call | flops 3221225472 | bytes 8388608 | tf_op jit(solution)/shard_map/attention_forward/pallas_call | solution.py:250
  55.1 17.8 %collective-permute-done.14 = bf16[512,1024]{1,0:T(8,128)(2,1)} collective-permute-done((bf16[512,1024]{1,0:T(8,128)(2,1)}, bf16[512,1024]{1,0:T(8,128)(2,1)}, u32[]{:S(2)}, u32[]{:S(2)}) %collective-permute-start.14) | collective-permute-done | bytes 1048608 | tf_op jit(solution)/shard_map/ppermute | solution.py:328
  83.2 4.9 fusion.43
  88.1 8.1 %multiply_convert_fusion.2 = (bf16[1024,1152]{1,0:T(8,128)(2,1)}, bf16[1024,1152]{1,0:T(8,128)(2,1)}, bf16[1024,1152]{1,0:T(8,128)(2,1)}) fusion(f32[1024,1152]{1,0:T(8,128)} %fusion.43, f32[1024,1152]{1,0:T(8,128)S(1)} %fusion.44, bf16[1024,1024]{1,0:T(8,128)(2,1)S(1)} %constant_dynamic-update-slice_fusion.4, bf16[1152,1024]{1,0:T(8,128)(2,1)S(1)} %copy-done), kind=kOutput, calls=%fused_computation.14 | convolution fusion | flops 2434793472 | bytes 20971520 | tf_op jit(solution)/shard_map/dot_general | solution.py:45
  96.2 4.7 fusion.49
  111.6 4.5 fusion.47
  116.1 4.4 fusion.46
  120.6 8.9 %multiply_convert_fusion = (bf16[1024,1152]{1,0:T(8,128)(2,1)}, bf16[1024,1152]{1,0:T(8,128)(2,1)}, bf16[1024,1152]{1,0:T(8,128)(2,1)}) fusion(f32[1024,1152]{1,0:T(8,128)} %fusion.46, f32[1024,1152]{1,0:T(8,128)} %fusion.47, bf16[1024,1024]{1,0:T(8,128)(2,1)S(1)} %constant_dynamic-update-slice_fusion.2, bf16[1152,1024]{1,0:T(8,128)(2,1)S(1)} %copy-done), kind=kOutput, calls=%fused_computation.12 | convolution fusion | flops 2434793472 | bytes 20971520 | tf_op jit(solution)/shard_map/dot_general | solution.py:45
  129.5 4.7 fusion.48
  142.8 9.5 %fusion.21 = bf16[1152,1024]{1,0:T(8,128)(2,1)} fusion(bf16[1024,1024]{1,0:T(8,128)(2,1)} %copy-done.42, bf16[1024,1024]{1,0:T(8,128)(2,1)S(1)} %copy-done.41, bf16[1024,1152]{1,0:T(8,128)(2,1)} %get-tuple-element.105, bf16[1024,1152]{1,0:T(8,128)(2,1)} %get-tuple-element.102), kind=kOutput, calls=%fused_computation.33 | convolution fusion | flops 4850843648 | bytes 11272192 | tf_op jit(solution)/shard_map/dot_general | solution.py:45
  155.8 9.0 %fusion.15 = bf16[1024,1152]{1,0:T(8,128)(2,1)} fusion(bf16[1024,1152]{1,0:T(8,128)(2,1)} %get-tuple-element.103, bf16[1024,1152]{1,0:T(8,128)(2,1)S(1)} %copy-done.62, bf16[1024,1024]{1,0:T(8,128)(2,1)S(1)} %copy-done.44, bf16[1024,1024]{1,0:T(8,128)(2,1)S(1)} %constant_dynamic-update-slice_fusion.8), kind=kOutput, calls=%fused_computation.31 | convolution fusion | flops 4850843648 | bytes 11272192 | tf_op jit(solution)/shard_map/dot_general | solution.py:45
  164.7 14.6 %collective-permute-done.11 = bf16[512,1024]{1,0:T(8,128)(2,1)S(1)} collective-permute-done((bf16[512,1024]{1,0:T(8,128)(2,1)S(1)}, bf16[512,1024]{1,0:T(8,128)(2,1)S(1)}, u32[]{:S(2)}, u32[]{:S(2)}) %collective-permute-start.11) | collective-permute-done | bytes 1048608 | tf_op jit(solution)/shard_map/ppermute | solution.py:328
  179.3 22.3 %collective-permute-done.17 = bf16[512,1024]{1,0:T(8,128)(2,1)S(1)} collective-permute-done((bf16[512,1024]{1,0:T(8,128)(2,1)S(1)}, bf16[512,1024]{1,0:T(8,128)(2,1)S(1)}, u32[]{:S(2)}, u32[]{:S(2)}) %collective-permute-start.17) | collective-permute-done | bytes 1048608 | tf_op jit(solution)/shard_map/ppermute | solution.py:328
  201.6 3.7 multiply_reduce_fusion
  206.9 4.1 constant_dynamic-update-slice_fusion.1
  211.0 7.0 %fusion.18 = bf16[1024,1152]{1,0:T(8,128)(2,1)} fusion(bf16[1024,1152]{1,0:T(8,128)(2,1)S(1)} %copy-done.66, bf16[1024,1152]{1,0:T(8,128)(2,1)S(1)} %copy-done.64, bf16[1024,1024]{1,0:T(8,128)(2,1)S(1)} %copy-done.44, bf16[1024,1024]{1,0:T(8,128)(2,1)S(1)} %constant_dynamic-update-slice_fusion.8), kind=kOutput, calls=%fused_computation.32 | convolution fusion | flops 4850843648 | bytes 11272192 | tf_op jit(solution)/shard_map/dot_general | solution.py:45
  224.9 15.0 %attention_backward.3 = (bf16[1024,256]{1,0:T(8,128)(2,1)S(1)}, bf16[1024,128]{1,0:T(8,128)(2,1)S(1)}, bf16[1024,128]{1,0:T(8,128)(2,1)S(1)}, f32[1,128]{1,0:T(1,128)S(1)}, f32[1,128]{1,0:T(1,128)S(1)}) custom-call(s32[1]{0:T(128)} %dynamic_slice.39.len_ref, bf16[1024,1024]{1,0:T(8,128)(2,1)} %constant_dynamic-update-slice_fusion.g_ref, ...), custom_call_target="tpu_custom_call" | custom-call | flops 6979321856 | bytes 8388608 | tf_op jit(solution)/shard_map/attention_backward/pallas_call | solution.py:278
  250.1 14.9 %attention_backward.2 = (bf16[1024,256]{1,0:T(8,128)(2,1)S(1)}, bf16[1024,128]{1,0:T(8,128)(2,1)S(1)}, bf16[1024,128]{1,0:T(8,128)(2,1)S(1)}, f32[1,128]{1,0:T(1,128)S(1)}, f32[1,128]{1,0:T(1,128)S(1)}) custom-call(s32[1]{0:T(128)} %dynamic_slice.39.len_ref, bf16[1024,1024]{1,0:T(8,128)(2,1)} %constant_dynamic-update-slice_fusion.g_ref, ...), custom_call_target="tpu_custom_call" | custom-call | flops 6979321856 | bytes 8388608 | tf_op jit(solution)/shard_map/attention_backward/pallas_call | solution.py:278
  276.6 5.3 add_add_fusion
  290.8 164.2 %all-reduce.8.cloned.1.call-done = (bf16[1152,1024]{1,0:T(8,128)(2,1)}, bf16[1024,1152]{1,0:T(8,128)(2,1)}, bf16[1024,1152]{1,0:T(8,128)(2,1)}) async-done(((bf16[1152,1024]{1,0:T(8,128)(2,1)}, bf16[1024,1152]{1,0:T(8,128)(2,1)}, bf16[1024,1152]{1,0:T(8,128)(2,1)}), (bf16[1152,1024]{1,0:T(8,128)(2,1)}, bf16[1024,1152]{1,0:T(8,128)(2,1)}, bf16[1024,1152]{1,0:T(8,128)(2,1)})) %all-reduce.8.cloned.1.call-update) | async-done | bytes 7077904 | tf_op jit(solution)/shard_map/psum | solution.py:455
  458.1 40.8 %all-reduce = (f32[1024]{0:T(1024)}, f32[64]{0:T(128)}, f32[64]{0:T(128)}, f32[1024]{0:T(1024)}) all-reduce(f32[1024]{0:T(1024)S(1)} %get-tuple-element.75, f32[64]{0:T(128)S(1)} %add_bitcast_fusion.1, f32[64]{0:T(128)S(1)} %add_bitcast_fusion, f32[1024]{0:T(1024)S(1)} %get-tuple-element.77), channel_id=1, replica_groups=mesh['wide'=8,'narrow'=4] {'wide','narrow'}, use_global_device_ids=true, to_apply=%region_5.6 | all-reduce | flops 2176 | bytes 17408 | tf_op jit(solution)/shard_map/psum | solution.py:460
  498.9 4.1 fusion.31
  511.0 38.9 %all-reduce.6.cloned.1.call-done = (bf16[1024,256]{1,0:T(8,128)(2,1)}, bf16[1024,128]{1,0:T(8,128)(2,1)}, bf16[1024,128]{1,0:T(8,128)(2,1)}, bf16[256,1024]{1,0:T(8,128)(2,1)}) async-done(((bf16[1024,256]{1,0:T(8,128)(2,1)}, bf16[1024,128]{1,0:T(8,128)(2,1)}, bf16[1024,128]{1,0:T(8,128)(2,1)}, bf16[256,1024]{1,0:T(8,128)(2,1)}), (bf16[1024,256]{1,0:T(8,128)(2,1)}, bf16[1024,128]{1,0:T(8,128)(2,1)}, ...) | async-done | bytes 1572880 | tf_op jit(solution)/shard_map/psum | solution.py:459
  (251 shorter events, 116.8 us)
Async XLA Ops:
  7.2 447.8 %all-reduce.8.cloned.1.call-start = ((), (), s32[]{:S(2)}) async-start(), calls=%async_computation.1 | async-start | bytes 14155776 | tf_op jit(solution)/shard_map/psum | solution.py:455
  12.0 9.9 %collective-permute-start = (bf16[512,1024]{1,0:T(8,128)(2,1)}, bf16[512,1024]{1,0:T(8,128)(2,1)}, u32[]{:S(2)}, u32[]{:S(2)}) collective-permute-start(bf16[512,1024]{1,0:T(8,128)(2,1)} %get-tuple-element.99), channel_id=1, source_target_pairs={{0,1},{1,0},{2,3},{3,2},{4,5},{5,4},{6,7},{7,6},{8,9},{9,8},{10,11... | collective-permute-start | bytes 3145736 | tf_op jit(solution)/shard_map/ppermute | solution.py:333
  12.5 26.7 %collective-permute-start.2 = (bf16[1024,128]{1,0:T(8,128)(2,1)}, bf16[1024,128]{1,0:T(8,128)(2,1)}, u32[]{:S(2)}, u32[]{:S(2)}) collective-permute-start(bf16[1024,128]{1,0:T(8,128)(2,1)} %wk_ref.1), channel_id=1, source_target_pairs={{0,2},{1,3},{2,0},{3,1},{4,6},{5,7},{6,4},{7,5},{8,10},{9,11},{10,... | collective-permute-start | bytes 786440 | tf_op jit(solution)/shard_map/ppermute | solution.py:328
  15.1 24.1 %collective-permute-start.3 = (bf16[1024,128]{1,0:T(8,128)(2,1)}, bf16[1024,128]{1,0:T(8,128)(2,1)}, u32[]{:S(2)}, u32[]{:S(2)}) collective-permute-start(bf16[1024,128]{1,0:T(8,128)(2,1)} %wv_ref.1), channel_id=1, source_target_pairs={{0,2},{1,3},{2,0},{3,1},{4,6},{5,7},{6,4},{7,5},{8,10},{9,11},{10,... | collective-permute-start | bytes 786440 | tf_op jit(solution)/shard_map/ppermute | solution.py:328
  16.3 23.2 %collective-permute-start.1 = (bf16[1024,256]{1,0:T(8,128)(2,1)S(1)}, bf16[1024,256]{1,0:T(8,128)(2,1)}, u32[]{:S(2)}, u32[]{:S(2)}) collective-permute-start(bf16[1024,256]{1,0:T(8,128)(2,1)S(1)} %copy-done.2), channel_id=1, source_target_pairs={{0,2},{1,3},{2,0},{3,1},{4,6},{5,7},{6,4},{7,5},{8,10},{9,11},{10,... | collective-permute-start | bytes 1572872 | tf_op jit(solution)/shard_map/ppermute | solution.py:328
  17.1 33.5 %collective-permute-start.4 = (bf16[256,1024]{1,0:T(8,128)(2,1)}, bf16[256,1024]{1,0:T(8,128)(2,1)}, u32[]{:S(2)}, u32[]{:S(2)}) collective-permute-start(bf16[256,1024]{1,0:T(8,128)(2,1)} %wo_ref.1), channel_id=1, source_target_pairs={{0,2},{1,3},{2,0},{3,1},{4,6},{5,7},{6,4},{7,5},{8,10},{9,11},{10,... | collective-permute-start | bytes 1572872 | tf_op jit(solution)/shard_map/ppermute | solution.py:328
  21.9 51.0 %collective-permute-start.14 = (bf16[512,1024]{1,0:T(8,128)(2,1)}, bf16[512,1024]{1,0:T(8,128)(2,1)}, u32[]{:S(2)}, u32[]{:S(2)}) collective-permute-start(bf16[512,1024]{1,0:T(8,128)(2,1)} %param.27), channel_id=1, source_target_pairs={{0,2},{1,3},{2,0},{3,1},{4,6},{5,7},{6,4},{7,5},{8,10},{9,11},{10,... | collective-permute-start | bytes 3145736 | tf_op jit(solution)/shard_map/ppermute | solution.py:328
  54.5 18.4 %collective-permute-start.5 = (bf16[512,1024]{1,0:T(8,128)(2,1)S(1)}, bf16[512,1024]{1,0:T(8,128)(2,1)S(1)}, u32[]{:S(2)}, u32[]{:S(2)}) collective-permute-start(bf16[512,1024]{1,0:T(8,128)(2,1)S(1)} %dynamic-slice_convert_fusion.5), channel_id=1, source_target_pairs={{0,1},{1,0},{2,3},{3,2},{4,5},{5,4},{6,7},{7,6},{8,9},{9,8},{10,11... | collective-permute-start | bytes 3145736 | tf_op jit(solution)/shard_map/ppermute | solution.py:333
  54.6 23.2 %collective-permute-start.12 = (bf16[512,1024]{1,0:T(8,128)(2,1)}, bf16[512,1024]{1,0:T(8,128)(2,1)S(1)}, u32[]{:S(2)}, u32[]{:S(2)}) collective-permute-start(bf16[512,1024]{1,0:T(8,128)(2,1)} %param.27), channel_id=1, source_target_pairs={{0,1},{1,0},{2,3},{3,2},{4,5},{5,4},{6,7},{7,6},{8,9},{9,8},{10,11... | collective-permute-start | bytes 3145736 | tf_op jit(solution)/shard_map/ppermute | solution.py:333
  72.9 6.9 %collective-permute-start.15 = (bf16[512,1024]{1,0:T(8,128)(2,1)}, bf16[512,1024]{1,0:T(8,128)(2,1)S(1)}, u32[]{:S(2)}, u32[]{:S(2)}) collective-permute-start(bf16[512,1024]{1,0:T(8,128)(2,1)} %collective-permute-done.14), channel_id=1, source_target_pairs={{0,1},{1,0},{2,3},{3,2},{4,5},{5,4},{6,7},{7,6},{8,9},{9,8},{10,11... | collective-permute-start | bytes 3145736 | tf_op jit(solution)/shard_map/ppermute | solution.py:333
  77.9 25.9 %collective-permute-start.8 = (bf16[512,1024]{1,0:T(8,128)(2,1)S(1)}, bf16[512,1024]{1,0:T(8,128)(2,1)S(1)}, u32[]{:S(2)}, u32[]{:S(2)}) collective-permute-start(bf16[512,1024]{1,0:T(8,128)(2,1)S(1)} %get-tuple-element.95), channel_id=1, source_target_pairs={{0,2},{1,3},{2,0},{3,1},{4,6},{5,7},{6,4},{7,5},{8,10},{9,11},{10,... | collective-permute-start | bytes 3145736 | tf_op jit(solution)/shard_map/ppermute | solution.py:328
  105.1 59.7 %collective-permute-start.13 = (bf16[512,1024]{1,0:T(8,128)(2,1)}, bf16[512,1024]{1,0:T(8,128)(2,1)}, u32[]{:S(2)}, u32[]{:S(2)}) collective-permute-start(bf16[512,1024]{1,0:T(8,128)(2,1)} %dynamic-slice_convert_fusion.2), channel_id=1, source_target_pairs={{0,1},{1,0},{2,3},{3,2},{4,5},{5,4},{6,7},{7,6},{8,9},{9,8},{10,11... | collective-permute-start | bytes 3145736 | tf_op jit(solution)/shard_map/ppermute | solution.py:333
  109.7 55.1 %collective-permute-start.7 = (bf16[512,1024]{1,0:T(8,128)(2,1)}, bf16[512,1024]{1,0:T(8,128)(2,1)}, u32[]{:S(2)}, u32[]{:S(2)}) collective-permute-start(bf16[512,1024]{1,0:T(8,128)(2,1)} %dynamic-slice_convert_fusion.4), channel_id=1, source_target_pairs={{0,1},{1,0},{2,3},{3,2},{4,5},{5,4},{6,7},{7,6},{8,9},{9,8},{10,11... | collective-permute-start | bytes 3145736 | tf_op jit(solution)/shard_map/ppermute | solution.py:333
  135.3 17.1 %collective-permute-start.10 = (bf16[512,1024]{1,0:T(8,128)(2,1)}, bf16[512,1024]{1,0:T(8,128)(2,1)S(1)}, u32[]{:S(2)}, u32[]{:S(2)}) collective-permute-start(bf16[512,1024]{1,0:T(8,128)(2,1)} %dynamic-slice_convert_fusion.3), channel_id=1, source_target_pairs={{0,1},{1,0},{2,3},{3,2},{4,5},{5,4},{6,7},{7,6},{8,9},{9,8},{10,11... | collective-permute-start | bytes 3145736 | tf_op jit(solution)/shard_map/ppermute | solution.py:333
  142.8 12.5 %collective-permute-start.16 = (bf16[512,1024]{1,0:T(8,128)(2,1)}, bf16[512,1024]{1,0:T(8,128)(2,1)S(1)}, u32[]{:S(2)}, u32[]{:S(2)}) collective-permute-start(bf16[512,1024]{1,0:T(8,128)(2,1)} %dynamic-slice_convert_fusion.1), channel_id=1, source_target_pairs={{0,1},{1,0},{2,3},{3,2},{4,5},{5,4},{6,7},{7,6},{8,9},{9,8},{10,11... | collective-permute-start | bytes 3145736 | tf_op jit(solution)/shard_map/ppermute | solution.py:333
  152.7 26.6 %collective-permute-start.11 = (bf16[512,1024]{1,0:T(8,128)(2,1)S(1)}, bf16[512,1024]{1,0:T(8,128)(2,1)S(1)}, u32[]{:S(2)}, u32[]{:S(2)}) collective-permute-start(bf16[512,1024]{1,0:T(8,128)(2,1)S(1)} %add_convert_fusion.2), channel_id=1, source_target_pairs={{0,2},{1,3},{2,0},{3,1},{4,6},{5,7},{6,4},{7,5},{8,10},{9,11},{10,... | collective-permute-start | bytes 3145736 | tf_op jit(solution)/shard_map/ppermute | solution.py:328
  155.7 45.9 %collective-permute-start.17 = (bf16[512,1024]{1,0:T(8,128)(2,1)S(1)}, bf16[512,1024]{1,0:T(8,128)(2,1)S(1)}, u32[]{:S(2)}, u32[]{:S(2)}) collective-permute-start(bf16[512,1024]{1,0:T(8,128)(2,1)S(1)} %add_convert_fusion), channel_id=1, source_target_pairs={{0,2},{1,3},{2,0},{3,1},{4,6},{5,7},{6,4},{7,5},{8,10},{9,11},{10,... | collective-permute-start | bytes 3145736 | tf_op jit(solution)/shard_map/ppermute | solution.py:328
  211.0 7.5 %collective-permute-start.18 = (bf16[512,1024]{1,0:T(8,128)(2,1)}, bf16[512,1024]{1,0:T(8,128)(2,1)}, u32[]{:S(2)}, u32[]{:S(2)}) collective-permute-start(bf16[512,1024]{1,0:T(8,128)(2,1)} %get-tuple-element.91), channel_id=1, source_target_pairs={{0,1},{1,0},{2,3},{3,2},{4,5},{5,4},{6,7},{7,6},{8,9},{9,8},{10,11... | collective-permute-start | bytes 3145736 | tf_op jit(solution)/shard_map/ppermute | solution.py:333
  218.1 331.9 %all-reduce.6.cloned.1.call-start = ((), (), s32[]{:S(2)}) async-start(), calls=%async_computation | async-start | bytes 3145728 | tf_op jit(solution)/shard_map/psum | solution.py:459
  240.7 42.5 %collective-permute-start.22 = (bf16[1024,128]{1,0:T(8,128)(2,1)S(1)}, bf16[1024,128]{1,0:T(8,128)(2,1)S(1)}, u32[]{:S(2)}, u32[]{:S(2)}) collective-permute-start(bf16[1024,128]{1,0:T(8,128)(2,1)S(1)} %convolution_convert_fusion.2), channel_id=1, source_target_pairs={{0,2},{1,3},{2,0},{3,1},{4,6},{5,7},{6,4},{7,5},{8,10},{9,11},{10,... | collective-permute-start | bytes 786440 | tf_op jit(solution)/shard_map/ppermute | solution.py:328
  243.5 41.1 %collective-permute-start.21 = (bf16[1024,128]{1,0:T(8,128)(2,1)S(1)}, bf16[1024,128]{1,0:T(8,128)(2,1)S(1)}, u32[]{:S(2)}, u32[]{:S(2)}) collective-permute-start(bf16[1024,128]{1,0:T(8,128)(2,1)S(1)} %convolution_convert_fusion.3), channel_id=1, source_target_pairs={{0,2},{1,3},{2,0},{3,1},{4,6},{5,7},{6,4},{7,5},{8,10},{9,11},{10,... | collective-permute-start | bytes 786440 | tf_op jit(solution)/shard_map/ppermute | solution.py:328
  245.4 43.8 %collective-permute-start.20 = (bf16[1024,256]{1,0:T(8,128)(2,1)}, bf16[1024,256]{1,0:T(8,128)(2,1)S(1)}, u32[]{:S(2)}, u32[]{:S(2)}) collective-permute-start(bf16[1024,256]{1,0:T(8,128)(2,1)} %convolution_convert_fusion.1), channel_id=1, source_target_pairs={{0,2},{1,3},{2,0},{3,1},{4,6},{5,7},{6,4},{7,5},{8,10},{9,11},{10,... | collective-permute-start | bytes 1572872 | tf_op jit(solution)/shard_map/ppermute | solution.py:328
  249.6 36.5 %collective-permute-start.23 = (bf16[256,1024]{1,0:T(8,128)(2,1)S(1)}, bf16[256,1024]{1,0:T(8,128)(2,1)S(1)}, u32[]{:S(2)}, u32[]{:S(2)}) collective-permute-start(bf16[256,1024]{1,0:T(8,128)(2,1)S(1)} %convolution_convert_fusion), channel_id=1, source_target_pairs={{0,2},{1,3},{2,0},{3,1},{4,6},{5,7},{6,4},{7,5},{8,10},{9,11},{10,... | collective-permute-start | bytes 1572872 | tf_op jit(solution)/shard_map/ppermute | solution.py:328
  283.2 172.1 %collective-permute-start.19 = (bf16[512,1024]{1,0:T(8,128)(2,1)}, bf16[512,1024]{1,0:T(8,128)(2,1)}, u32[]{:S(2)}, u32[]{:S(2)}) collective-permute-start(bf16[512,1024]{1,0:T(8,128)(2,1)} %dynamic-slice_convert_fusion), channel_id=1, source_target_pairs={{0,1},{1,0},{2,3},{3,2},{4,5},{5,4},{6,7},{7,6},{8,9},{9,8},{10,11... | collective-permute-start | bytes 3145736 | tf_op jit(solution)/shard_map/ppermute | solution.py:333
  (70 other events, 1016.5 us)
Sparse Core Ops, SparseCore 0:
  218.2 236.8 all-reduce.7
  459.9 89.9 all-reduce.5

commit v2 on v1

--- a/solution.py
+++ b/solution.py
@@ -18,6 +18,7 @@
 F32 = jnp.float32
 BF16 = jnp.bfloat16
 VMEM_LIMIT = 48 * 1024 * 1024
+BACK_LIMIT = 60 * 1024 * 1024
 
 
 def rope_tables(length, width):
@@ -140,42 +141,195 @@
             rinv_ref[rows, low + HD : low + TILE] = jnp.broadcast_to(inv[BLK:], (BLK, HD))
 
 
-def attention_backward(
-    len_ref, g_ref, wo_ref, q_ref, k_ref, v_ref, att_ref, qraw_ref, kraw_ref, rinv_ref,
-    qs_ref, ks_ref, cos_ref, sin_ref,
-    gq_ref, gk_ref, gv_ref, qsg_ref, ksg_ref,
-    vaug_ref, aug_ref, dk_ref, dv_ref,
-):
+class Ring:
+    def __init__(self, count, place, target, turn, chunk, first, rows, own, source, out, land, sends, recvs):
+        self.count, self.place, self.target, self.turn = count, place, target, turn
+        self.chunk, self.first, self.rows = chunk, first, rows
+        self.own, self.source, self.out, self.land = own, source, out, land
+        self.sends, self.recvs = sends, recvs
+        self.done = 0
+
+    def index(self, steps):
+        return lax.rem(self.place + self.turn * steps + 2 * self.count, self.count)
+
+    def part(self, ref, steps):
+        start = pl.multiple_of(self.index(steps) * self.chunk + self.first, 16)
+        return ref.at[pl.ds(start, self.rows), :]
+
+    def copy(self, step, source, target):
+        return pltpu.make_async_remote_copy(
+            src_ref=source,
+            dst_ref=target,
+            send_sem=self.sends.at[step],
+            recv_sem=self.recvs.at[step],
+            device_id={"wide": self.target},
+            device_id_type=pl.DeviceIdType.MESH,
+        )
+
+    def copy_of(self, step):
+        last = self.count - 1
+        if step == 0:
+            return self.copy(0, self.part(self.source, 0), self.land.at[0])
+        if step < last:
+            return self.copy(step, self.land.at[step - 1], self.land.at[step])
+        steps = last - step + 1
+        where = self.part(self.out, steps)
+        return self.copy(step, self.land.at[last - 1] if step == last else where, where)
+
+    def begin(self):
+        self.copy_of(0).start()
+
+    @property
+    def left(self):
+        return 2 * (self.count - 1) - self.done
+
+    def tick(self, keep):
+        step, last = self.done, self.count - 1
+        self.done += 1
+        if step < last:
+            slot = self.land.at[step]
+            self.copy(step, slot, slot).wait_recv()
+            start = pl.multiple_of(self.index(-step - 1) * self.chunk + self.first, 16)
+
+            @pl.loop(0, self.rows // 16)
+            def _(r):
+                at = pl.multiple_of(r * 16, 16)
+                mine = self.own[pl.ds(pl.multiple_of(start + at, 16), 16), :].astype(F32)
+                slot[pl.ds(at, 16), :] = (slot[pl.ds(at, 16), :].astype(F32) + mine).astype(BF16)
+
+            if step == last - 1:
+                kept = pltpu.make_async_copy(slot, self.part(self.out, 1), keep)
+                kept.start()
+                self.copy_of(last).start()
+                kept.wait()
+            else:
+                self.copy_of(step + 1).start()
+        else:
+            where = self.part(self.out, last - step)
+            self.copy(step, where, where).wait_recv()
+            if self.left:
+                self.copy_of(step + 1).start()
+
+    def finish(self):
+        for step in range(2 * (self.count - 1)):
+            self.copy_of(step).wait_send()
+
+
+def ring_rows(rows, count):
+    chunk = -(-rows // (count * 16)) * 16
+    forward = -(-chunk // 32) * 16
+    return chunk, forward, chunk - forward
+
+
+def backward_kernel(plan, *refs):
+    count, narrow, side = plan["wide"], plan["narrow"], plan["side"]
+    groups, own_rows = plan["groups"], plan["own"]
+    taken = 0
+
+    def take(number):
+        nonlocal taken
+        taken += number
+        return refs[taken - number : taken]
+
+    len_ref, qs_ref, ks_ref, ng_ref, g2_ref = take(5)
+    loads_from = take(plan["loads"])
+    outs = take(4)
+    gt_ref, gains_ref = take(2)
+    loaded = take(plan["loads"])
+    lands = take(plan["lands"])
+    all_ref, vaug_ref, aug_ref, dk_ref, dv_ref = take(5)
+    px1, px2, rx1, rx2, own1, own2 = take(6)
+    gn_send, gn_recv, gn_own = take(3)
+    gain_mine, gain_in = take(2)
+    load_sems, ring_sends, ring_recvs, keep_sem, y_sends, y_recvs, gn_sends, gn_recvs, gain_sends, gain_recvs = take(10)
+
+    branch, rows_turned, w_all, tok, gmid, cos_ref, sin_ref, gu_own, gd_own = loaded[:9]
+    group_refs = [loaded[9 + 9 * g : 18 + 9 * g] for g in range(groups)]
+    gu_src, gd_src = loads_from[7], loads_from[8]
+
+    w = lax.axis_index("wide")
+    n = lax.axis_index("narrow")
+    half = count // 2
+    place_ring = lax.rem((1 - w % 2) * (count - w // 2) + (w % 2) * (w // 2 + 1), count)
+
+    def at_place(p):
+        far = lax.rem(p + count - 1, count) // half
+        z = (1 - far) * (p - 1) + far * lax.rem(count - p, count)
+        return 2 * z + 1 - far
+
+    onward = at_place(lax.rem(place_ring + 1, count))
+    behind = at_place(lax.rem(place_ring + count - 1, count))
+    across = lax.rem(n + side, narrow)
+    place = lax.rem(n, side)
+
+    def mate(turn):
+        return n - place + lax.rem(place + turn, side)
+
+    def flip(value, bit):
+        return value + bit - 2 * bit * lax.rem(value // bit, 2)
+
+    doubling = [("narrow", 2**e) for e in range(int(math.log2(narrow)))]
+    doubling += [("wide", 2**e) for e in range(int(math.log2(count)))]
+    partners = [{axis: flip(n if axis == "narrow" else w, bit)} for axis, bit in doubling]
+    peers = [{"wide": onward}, {"wide": behind}, {"narrow": across}]
+    peers += [{"narrow": mate(t)} for t in range(1, side)] + partners
+
+    loads = [
+        pltpu.make_async_copy(s, d, load_sems.at[i])
+        for i, (s, d) in enumerate(zip(loads_from, loaded))
+    ]
+    for load in loads:
+        load.start()
+    waited = set()
+
+    def need(*which):
+        for i in which:
+            if i not in waited:
+                waited.add(i)
+                loads[i].wait()
+
+    barrier = pltpu.get_barrier_semaphore()
+    for peer in peers:
+        pl.semaphore_signal(barrier, inc=1, device_id=peer, device_id_type=pl.DeviceIdType.MESH)
+    pl.semaphore_wait(barrier, len(peers))
+
+    rings = []
+    used = 0
+    for a, (own, source, out, rows) in enumerate(
+        [
+            (gu_own, gu_src, outs[0], plan["rows"][0]),
+            (gd_own, gd_src, outs[1], plan["rows"][1]),
+            (own1, own1, outs[2], plan["rows"][2]),
+            (own2, own2, outs[3], plan["rows"][3]),
+        ]
+    ):
+        chunk, forward, backward = ring_rows(rows, count)
+        pair = []
+        for turn, target, first, size in ((1, onward, 0, forward), (-1, behind, forward, backward)):
+            if size:
+                pair.append(
+                    Ring(
+                        count, place_ring, target, turn, chunk, first, size, own, source, out,
+                        lands[used], ring_sends.at[used], ring_recvs.at[used],
+                    )
+                )
+                used += 1
+        rings.append(pair)
+
+    for pair in rings[:2]:
+        for ring in pair:
+            ring.begin()
+
+    def tick(pair):
+        for ring in pair:
+            if ring.left:
+                ring.tick(keep_sem)
+
     length = len_ref[0]
-    heads = k_ref.shape[1] // HD
     ones = group_ones()
     lane = lanes((BLK, TILE))
-
-    for start in range(0, LEN, BLK):
-        rows = slice(start, start + BLK)
-        grad = contract(g_ref[rows, :], wo_ref[...], 1, 1).astype(BF16).astype(F32)
-        for t in range(heads):
-            cols = slice(t * TILE, (t + 1) * TILE)
-            part = (grad[:, cols] * rinv_ref[rows, cols]).astype(BF16).astype(F32)
-            inner = group_sum(part * att_ref[rows, cols].astype(F32), ones)
-            for which in range(2):
-                mine = part if which == 0 else pltpu.roll(part, HD, 1)
-                sums = pltpu.roll(inner, HD, 1) if which == 0 else inner
-                high = sums.astype(BF16).astype(F32)
-                tail = jnp.where(
-                    lane == HD, -high, jnp.where(lane == HD + 1, high - sums, 0.0)
-                )
-                aug_ref[2 * t + which, rows, :] = jnp.where(lane < HD, mine, tail).astype(BF16)
-        for t in range(heads // 2):
-            v_pair = v_ref[rows, t * TILE : (t + 1) * TILE].astype(F32)
-            mark = jnp.where(lane < HD + 2, 1.0, 0.0)
-            vaug_ref[2 * t, rows, :] = jnp.where(lane < HD, v_pair, mark).astype(BF16)
-            vaug_ref[2 * t + 1, rows, :] = jnp.where(
-                lane < HD, pltpu.roll(v_pair, HD, 1), mark
-            ).astype(BF16)
-
-    dk_ref[...] = jnp.zeros_like(dk_ref)
-    dv_ref[...] = jnp.zeros_like(dv_ref)
+    width = w_all.shape[1] // groups
+    gains = {"q": jnp.zeros((1, TILE), F32), "k": jnp.zeros((1, TILE), F32)}
     col_ids = lax.rem(lax.broadcasted_iota(jnp.int32, (BLK, 2 * BLK), 1), BLK)
     causal = lax.broadcasted_iota(jnp.int32, (BLK, 2 * BLK), 0) <= col_ids
 
@@ -190,57 +344,243 @@
         gain = jnp.sum(turned * unit, axis=0, keepdims=True)
         return inv * (scaled - unit * inner), gain
 
-    q_gain = jnp.zeros((1, TILE), F32)
-    for h in range(heads):
-        keys_turned = jnp.transpose(
-            k_ref[:, (h // 2) * TILE : (h // 2 + 1) * TILE].astype(F32)
-        )[(h % 2) * HD : (h % 2 + 1) * HD].astype(BF16)
-        for i in range(LEN // BLK):
-            rows = slice(i * BLK, (i + 1) * BLK)
-            low = h * TILE
-            q_two = jnp.concatenate(
-                [q_ref[rows, low : low + HD], q_ref[rows, low + HD : low + TILE]], axis=0
-            )
-            aug = jnp.concatenate([aug_ref[2 * h, rows, :], aug_ref[2 * h + 1, rows, :]], axis=0)
-            dq = jnp.zeros((HD, 2 * BLK), F32)
-            for j in range(i + 1):
-                keys = slice(j * BLK, (j + 1) * BLK)
-                weight = jnp.exp(contract(k_ref[keys, h * HD : (h + 1) * HD], q_two, 1, 1))
-                if i == j:
-                    weight = jnp.where(causal, weight, 0.0)
-                slope = (weight * contract(vaug_ref[h, keys, :], aug, 1, 1)).astype(BF16)
-                dv_ref[h, keys, :] += contract(weight.astype(BF16), aug, 1, 0)
-                dk_ref[h, keys, :] += contract(slope, q_two, 1, 0)
-                dq += contract(keys_turned[:, keys], slope, 1, 0)
-            both = jnp.concatenate([dq[:, :BLK], dq[:, BLK:]], axis=0)
-            grad = jnp.transpose(both) * (1.0 / math.sqrt(HD))
-            cols = slice(low, low + TILE)
-            turned = turn_back(grad, cos_ref[rows, :], sin_ref[rows, :])
-            out, gain = norm_back(qraw_ref[rows, cols], turned, qs_ref[...])
-            gq_ref[rows, cols] = out.astype(BF16)
-            q_gain += gain
-    qsg_ref[...] = q_gain
-
-    k_gain = jnp.zeros((1, TILE), F32)
-    for start in range(0, LEN, BLK):
-        rows = slice(start, start + BLK)
-        real = (lax.broadcasted_iota(jnp.int32, (BLK, TILE), 0) + start) < length
-        for t in range(heads // 2):
-            cols = slice(t * TILE, (t + 1) * TILE)
-            grad = jnp.concatenate([dk_ref[2 * t, rows, :], dk_ref[2 * t + 1, rows, :]], axis=1)
-            grad = jnp.where(real, grad, 0.0)
-            turned = turn_back(grad, cos_ref[rows, :], sin_ref[rows, :])
-            out, gain = norm_back(kraw_ref[rows, cols], turned, ks_ref[...])
-            gk_ref[rows, cols] = out.astype(BF16)
-            k_gain += gain
-            values = jnp.where(
-                lane < HD, dv_ref[2 * t, rows, :], pltpu.roll(dv_ref[2 * t + 1, rows, :], HD, 1)
-            )
-            gv_ref[rows, cols] = jnp.where(real, values, 0.0).astype(BF16)
-    ksg_ref[...] = k_gain
+    def attention_pieces(g):
+        q_ref, k_ref, v_ref, att_ref, qraw_ref, kraw_ref, rinv_ref, wo_ref, _ = group_refs[g]
+        heads = k_ref.shape[1] // HD
+        base, nq, nk = g * width, q_ref.shape[1], k_ref.shape[1]
+        for start in range(0, LEN, BLK):
+            rows = slice(start, start + BLK)
+            grad = contract(branch[rows, :], wo_ref[...], 1, 1).astype(BF16).astype(F32)
+            for t in range(heads):
+                cols = slice(t * TILE, (t + 1) * TILE)
+                part = (grad[:, cols] * rinv_ref[rows, cols]).astype(BF16).astype(F32)
+                inner = group_sum(part * att_ref[rows, cols].astype(F32), ones)
+                for which in range(2):
+                    mine = part if which == 0 else pltpu.roll(part, HD, 1)
+                    sums = pltpu.roll(inner, HD, 1) if which == 0 else inner
+                    high = sums.astype(BF16).astype(F32)
+                    tail = jnp.where(
+                        lane == HD, -high, jnp.where(lane == HD + 1, high - sums, 0.0)
+                    )
+                    aug_ref[2 * t + which, rows, :] = jnp.where(lane < HD, mine, tail).astype(BF16)
+            for t in range(heads // 2):
+                v_pair = v_ref[rows, t * TILE : (t + 1) * TILE].astype(F32)
+                mark = jnp.where(lane < HD + 2, 1.0, 0.0)
+                vaug_ref[2 * t, rows, :] = jnp.where(lane < HD, v_pair, mark).astype(BF16)
+                vaug_ref[2 * t + 1, rows, :] = jnp.where(
+                    lane < HD, pltpu.roll(v_pair, HD, 1), mark
+                ).astype(BF16)
+            dk_ref[:, rows, :] = jnp.zeros((heads, BLK, HD), F32)
+            dv_ref[:, rows, :] = jnp.zeros((heads, BLK, TILE), F32)
+            yield
+
+        for h in range(heads):
+            keys_turned = jnp.transpose(
+                k_ref[:, (h // 2) * TILE : (h // 2 + 1) * TILE].astype(F32)
+            )[(h % 2) * HD : (h % 2 + 1) * HD].astype(BF16)
+            for i in range(LEN // BLK):
+                rows = slice(i * BLK, (i + 1) * BLK)
+                low = h * TILE
+                q_two = jnp.concatenate(
+                    [q_ref[rows, low : low + HD], q_ref[rows, low + HD : low + TILE]], axis=0
+                )
+                aug = jnp.concatenate(
+                    [aug_ref[2 * h, rows, :], aug_ref[2 * h + 1, rows, :]], axis=0
+                )
+                dq = jnp.zeros((HD, 2 * BLK), F32)
+                for j in range(i + 1):
+                    keys = slice(j * BLK, (j + 1) * BLK)
+                    weight = jnp.exp(contract(k_ref[keys, h * HD : (h + 1) * HD], q_two, 1, 1))
+                    if i == j:
+                        weight = jnp.where(causal, weight, 0.0)
+                    slope = (weight * contract(vaug_ref[h, keys, :], aug, 1, 1)).astype(BF16)
+                    dv_ref[h, keys, :] += contract(weight.astype(BF16), aug, 1, 0)
+                    dk_ref[h, keys, :] += contract(slope, q_two, 1, 0)
+                    dq += contract(keys_turned[:, keys], slope, 1, 0)
+                both = jnp.concatenate([dq[:, :BLK], dq[:, BLK:]], axis=0)
+                grad = jnp.transpose(both) * (1.0 / math.sqrt(HD))
+                turned = turn_back(grad, cos_ref[rows, :], sin_ref[rows, :])
+                out, gain = norm_back(qraw_ref[rows, low : low + TILE], turned, qs_ref[...])
+                all_ref[rows, base + low : base + low + TILE] = out.astype(BF16)
+                gains["q"] += gain
+                yield
+
+        for start in range(0, LEN, BLK):
+            rows = slice(start, start + BLK)
+            real = (lax.broadcasted_iota(jnp.int32, (BLK, TILE), 0) + start) < length
+            for t in range(heads // 2):
+                low = base + nq + t * TILE
+                grad = jnp.concatenate(
+                    [dk_ref[2 * t, rows, :], dk_ref[2 * t + 1, rows, :]], axis=1
+                )
+                grad = jnp.where(real, grad, 0.0)
+                turned = turn_back(grad, cos_ref[rows, :], sin_ref[rows, :])
+                out, gain = norm_back(
+                    kraw_ref[rows, t * TILE : (t + 1) * TILE], turned, ks_ref[...]
+                )
+                all_ref[rows, low : low + TILE] = out.astype(BF16)
+                gains["k"] += gain
+                values = jnp.where(
+                    lane < HD,
+                    dv_ref[2 * t, rows, :],
+                    pltpu.roll(dv_ref[2 * t + 1, rows, :], HD, 1),
+                )
+                all_ref[rows, low + nk : low + nk + TILE] = jnp.where(real, values, 0.0).astype(
+                    BF16
+                )
+            yield
+
+    def wide_copy(source, target, which):
+        return pltpu.make_async_remote_copy(
+            src_ref=source,
+            dst_ref=target,
+            send_sem=y_sends.at[which],
+            recv_sem=y_recvs.at[which],
+            device_id={"narrow": across},
+            device_id_type=pl.DeviceIdType.MESH,
+        )
+
+    y_out = wide_copy(px2, rx2, 0)
+    y_qkv = wide_copy(px1, rx1, 1)
+
+    def out_grads(which, target):
+        g, first, size = plan["out_parts"][which]
+        target[:size, :] = contract(
+            group_refs[g][8][first : first + size, :], branch[...], 1, 0
+        ).astype(BF16)
+
+    def qkv_grads(which, target):
+        for start in range(0, rows_turned.shape[0], BLK):
+            rows = slice(start, start + BLK)
+            for source, size, to in plan["qkv_parts"][which]:
+                target[rows, to : to + size] = contract(
+                    rows_turned[rows, :], all_ref[:, source : source + size], 1, 0
+                ).astype(BF16)
+            yield
+
+    def gn_copy(turn):
+        return pltpu.make_async_remote_copy(
+            src_ref=gn_send.at[turn - 1],
+            dst_ref=gn_recv.at[turn - 1],
+            send_sem=gn_sends.at[turn - 1],
+            recv_sem=gn_recvs.at[turn - 1],
+            device_id={"narrow": mate(turn)},
+            device_id_type=pl.DeviceIdType.MESH,
+        )
+
+    def gain_copy(step):
+        return pltpu.make_async_remote_copy(
+            src_ref=gain_mine.at[step],
+            dst_ref=gain_in.at[step],
+            send_sem=gain_sends.at[step],
+            recv_sem=gain_recvs.at[step],
+            device_id=partners[step],
+            device_id_type=pl.DeviceIdType.MESH,
+        )
+
+    def compute():
+        first_group = list(range(9, 18))
+        need(0, 5, 6, *first_group)
+        out_grads("partner", px2)
+        if groups > 1:
+            y_out.start()
+            yield
+        yield from attention_pieces(0)
+        need(1)
+        if groups == 1:
+            y_out.start()
+        yield from qkv_grads("partner", px1)
+        y_qkv.start()
+        if groups > 1:
+            need(*range(18, 27))
+            yield from attention_pieces(1)
+        yield from qkv_grads("own", own1)
+        out_grads("own", own2)
+        yield
+        need(2)
+        for turn in [*range(1, side), 0]:
+            for start in range(0, own_rows, BLK):
+                at = pl.multiple_of(lax.rem(place + turn, side) * own_rows + start, BLK)
+                grad = contract(all_ref[pl.ds(at, BLK), :], w_all[...], 1, 1)
+                if turn:
+                    gn_send[turn - 1, start : start + BLK, :] = grad.astype(BF16)
+                else:
+                    gn_own[start : start + BLK, :] = grad
+                yield
+            if turn:
+                gn_copy(turn).start()
+        need(3, 4)
+        for turn in range(1, side):
+            gn_copy(turn).wait_recv()
+        gain_one = jnp.zeros((1, ng_ref.shape[1]), F32)
+        for start in range(0, own_rows, 64):
+            rows = slice(start, start + 64)
+            grad = gn_own[rows, :]
+            for turn in range(1, side):
+                grad += gn_recv[turn - 1, rows, :].astype(F32)
+            values = tok[rows, :].astype(F32)
+            inv = lax.rsqrt(jnp.mean(values * values, axis=1, keepdims=True) + EPSILON)
+            unit = values * inv
+            scaled = grad * ng_ref[...]
+            inner = jnp.mean(unit * scaled, axis=1, keepdims=True)
+            gt_ref[rows, :] = gmid[rows, :] + inv * (scaled - unit * inner)
+            gain_one += jnp.sum(grad * unit, axis=0, keepdims=True)
+        gain_mine[0, 0:1, :] = gain_one
+        gain_mine[0, 1:2, :] = g2_ref[...]
+        spare = jnp.zeros((1, gain_one.shape[1] - TILE), F32)
+        gain_mine[0, 2:3, :] = jnp.concatenate([gains["q"], spare], axis=1)
+        gain_mine[0, 3:4, :] = jnp.concatenate([gains["k"], spare], axis=1)
+        gain_mine[0, 4:8, :] = jnp.zeros((4, gain_one.shape[1]), F32)
+        gain_copy(0).start()
+        yield
+        y_out.wait_recv()
+        y_qkv.wait_recv()
+        for mine, theirs in ((own1, rx1), (own2, rx2)):
+            tall = mine.shape[0] // 16
+
+            @pl.loop(0, tall)
+            def _(r):
+                at = pl.ds(pl.multiple_of(r * 16, 16), 16)
+                mine[at, :] = (mine[at, :].astype(F32) + theirs[at, :].astype(F32)).astype(BF16)
+
+    need(7, 8)
+    turn = 0
+    order = [0, 1]
+    for number, _ in enumerate(compute()):
+        if number % 4 == 3:
+            tick(rings[order[turn % 2]])
+            turn += 1
+    for pair in rings[2:]:
+        for ring in pair:
+            ring.begin()
+    step = 0
+    while any(ring.left for pair in rings for ring in pair):
+        tick(rings[order[turn % 2]])
+        turn += 1
+        tick(rings[2])
+        tick(rings[3])
+        if step < len(doubling):
+            gain_copy(step).wait_recv()
+            total = gain_mine[step] + gain_in[step]
+            if step + 1 < len(doubling):
+                gain_mine[step + 1] = total
+                gain_copy(step + 1).start()
+            else:
+                gains_ref[...] = total
+        step += 1
+    for pair in rings:
+        for ring in pair:
+            ring.finish()
+    y_out.wait_send()
+    y_qkv.wait_send()
+    for turn in range(1, side):
+        gn_copy(turn).wait_send()
+    for step in range(len(doubling)):
+        gain_copy(step).wait_send()
 
 
 VM = pl.BlockSpec(memory_space=pltpu.VMEM)
+ANY = pl.BlockSpec(memory_space=pl.ANY)
 SM = pl.BlockSpec(memory_space=pltpu.SMEM)
 
 
@@ -271,46 +611,79 @@
     )(length, rows, wq, wk, wv, qs, ks, cosine, sine)
 
 
-def run_backward(length, grads, wo, q, k, v, att, q_raw, k_raw, rinv, qs, ks, cosine, sine):
-    nq, nk = q.shape[1], k.shape[1]
-    heads = nk // HD
+def padded(array, count):
+    chunk = ring_rows(array.shape[0], count)[0]
+    extra = chunk * count - array.shape[0]
+    return jnp.pad(array, ((0, extra), (0, 0))) if extra else array
+
+
+def run_backward(plan, small, big, group_arrays, grads_gu, grads_d):
+    count, narrow, side = plan["wide"], plan["narrow"], plan["side"]
     shape = jax.ShapeDtypeStruct
-    return pl.pallas_call(
-        attention_backward,
-        out_shape=(
-            shape((LEN, nq), BF16),
-            shape((LEN, nk), BF16),
-            shape((LEN, nk), BF16),
-            shape((1, TILE), F32),
-            shape((1, TILE), F32),
-        ),
-        in_specs=[SM] + [VM] * 13,
-        out_specs=[VM] * 5,
-        scratch_shapes=[
+    depth = big[0].shape[1]
+    loads = list(big) + [padded(grads_gu, count), padded(grads_d, count)]
+    for arrays in group_arrays:
+        loads += list(arrays)
+    q, k = group_arrays[0][0], group_arrays[0][1]
+    heads = k.shape[1] // HD
+    qkv, outs = plan["qkv_width"], plan["out_rows"]
+    sizes = [grads_gu.shape, grads_d.shape, (depth, qkv), (outs, depth)]
+    plan = dict(plan, loads=len(loads), rows=[s[0] for s in sizes], groups=len(group_arrays))
+    full, lands = [], []
+    for rows, cols in sizes:
+        chunk, forward, backward = ring_rows(rows, count)
+        full.append((chunk * count, cols))
+        lands += [pltpu.VMEM((count - 1, r, cols), BF16) for r in (forward, backward) if r]
+    plan["lands"] = len(lands)
+    steps = 2 * (count - 1)
+    doubling = int(math.log2(narrow)) + int(math.log2(count))
+    own = plan["own"]
+    dma = pltpu.SemaphoreType.DMA
+    results = pl.pallas_call(
+        functools.partial(backward_kernel, plan),
+        out_shape=tuple(shape(s, BF16) for s in full)
+        + (shape((own, depth), F32), shape((8, depth), F32)),
+        in_specs=[SM] + [VM] * 4 + [ANY] * len(loads),
+        out_specs=[ANY] * 4 + [VM] * 2,
+        scratch_shapes=[pltpu.VMEM(a.shape, a.dtype) for a in loads]
+        + lands
+        + [
+            pltpu.VMEM((LEN, big[2].shape[1]), BF16),
             pltpu.VMEM((heads, LEN, TILE), BF16),
             pltpu.VMEM((2 * heads, LEN, TILE), BF16),
             pltpu.VMEM((heads, LEN, HD), F32),
             pltpu.VMEM((heads, LEN, TILE), F32),
+            pltpu.VMEM(full[2], BF16),
+            pltpu.VMEM(full[3], BF16),
+            pltpu.VMEM(full[2], BF16),
+            pltpu.VMEM(full[3], BF16),
+            pltpu.VMEM(full[2], BF16),
+            pltpu.VMEM(full[3], BF16),
+            pltpu.VMEM((side - 1, own, depth), BF16),
+            pltpu.VMEM((side - 1, own, depth), BF16),
+            pltpu.VMEM((own, depth), F32),
+            pltpu.VMEM((doubling, 8, depth), F32),
+            pltpu.VMEM((doubling, 8, depth), F32),
+            dma((len(loads),)),
+            dma((len(lands), steps)),
+            dma((len(lands), steps)),
+            dma,
+            dma((2,)),
+            dma((2,)),
+            dma((side - 1,)),
+            dma((side - 1,)),
+            dma((doubling,)),
+            dma((doubling,)),
         ],
-        compiler_params=pltpu.CompilerParams(vmem_limit_bytes=VMEM_LIMIT),
+        compiler_params=pltpu.CompilerParams(
+            vmem_limit_bytes=BACK_LIMIT, collective_id=1, has_side_effects=True
+        ),
         cost_estimate=pl.CostEstimate(
-            flops=2 * LEN * grads.shape[1] * nq + 24 * LEN * LEN * nq,
-            bytes_accessed=8 * 1024 * 1024,
-            transcendentals=0,
+            flops=20 * 10**9, bytes_accessed=64 * 1024 * 1024, transcendentals=0
         ),
-        name="attention_backward",
-    )(length, grads, wo, q, k, v, att, q_raw, k_raw, rinv, qs, ks, cosine, sine)
-
-
-def ring_order(count):
-    side = 2 ** (int(math.log2(count)) // 2) if count > 1 else 1
-    tall = count // side
-    order = [0]
-    for col in range(tall):
-        steps = range(1, side) if col % 2 == 0 else range(side - 1, 0, -1)
-        order += [col * side + s for s in steps]
-    order += [col * side for col in range(tall - 1, 0, -1)]
-    return order
+        name="backward_and_sums",
+    )(*small, *loads)
+    return [r[: s[0]] for r, s in zip(results[:4], sizes)] + list(results[4:])
 
 
 def on_device(
@@ -410,68 +783,64 @@
     )
     output = middle + to_owners([contract(b[2], w_down, 1, 0) for b in blocks])
     grad_down = contract(hidden, grad_rows, 0, 0).astype(BF16)
-    grad_w_gate = contract(rows_two, grad_gate, 0, 0).astype(BF16)
-    grad_w_up = contract(rows_two, grad_up, 0, 0).astype(BF16)
+    grad_gate_up = contract(
+        rows_two, jnp.concatenate([grad_gate, grad_up], axis=1), 0, 0
+    ).astype(BF16)
 
     back_two, gain_two = row_norm_back(middle, inv_two, ffn_gain, grad_normed_two)
     grad_middle = cotangent.astype(F32) + back_two
     branch = gather(grad_middle.astype(BF16))
 
-    q_gain, k_gain = 0.0, 0.0
-    back_one = 0.0
-    weight_grads = []
-    for s, (wq, wk, wv, wo) in zip(saved, weights):
-        att, q, k, v, q_raw, k_raw, rinv = s
-        gq, gk, gv, qg, kg = run_backward(
-            length, branch, wo, q, k, v, att, q_raw, k_raw, rinv, qs, ks, cosine, sine
-        )
-        q_gain += qg[0, :HD] + qg[0, HD:]
-        k_gain += kg[0, :HD] + kg[0, HD:]
-        back_one += contract(gq, wq, 1, 1) + contract(gk, wk, 1, 1) + contract(gv, wv, 1, 1)
-        weight_grads.append(
-            (
-                contract(rows_one, gq, 0, 0),
-                contract(rows_one, gk, 0, 0),
-                contract(rows_one, gv, 0, 0),
-                contract(att, branch, 0, 0),
-            )
-        )
+    nq, nk = w_query.shape[1], w_key.shape[1]
     if joined:
-        weight_grads = [
-            tuple(
-                jnp.split(w, sequences, axis=1 if n < 3 else 0)[p]
-                for n, w in enumerate(weight_grads[0])
-            )
-            for p in range(sequences)
-        ]
-    own_grads = list(weight_grads[0])
-    for turn in range(1, sequences):
-        for n in range(4):
-            own_grads[n] += across(weight_grads[turn][n].astype(BF16), sequences - turn).astype(F32)
-    grad_normed_one = scatter(back_one)
-    back_one, gain_one = row_norm_back(residual, inv_one, norm_gain, grad_normed_one)
-    grad_tokens = grad_middle + back_one
-
-    grad_down, grad_w_gate, grad_w_up = lax.psum((grad_down, grad_w_gate, grad_w_up), "wide")
-    grad_down, grad_w_gate, grad_w_up, *own_grads = lax.optimization_barrier(
-        (grad_down, grad_w_gate, grad_w_up, *own_grads)
+        order = [0]
+        qkv_parts = {
+            "own": [(0, nq, 0), (2 * nq, nk, nq), (2 * nq + 2 * nk, nk, nq + nk)],
+            "partner": [
+                (nq, nq, 0), (2 * nq + nk, nk, nq), (2 * nq + 3 * nk, nk, nq + nk)
+            ],
+        }
+        out_parts = {"own": (0, 0, nq), "partner": (0, nq, nq)}
+    else:
+        order = [1, 0]
+        qkv_parts = {
+            "partner": [(0, nq + 2 * nk, 0)],
+            "own": [(nq + 2 * nk, nq + 2 * nk, 0)],
+        }
+        out_parts = {"partner": (0, 0, nq), "own": (1, 0, nq)}
+    plan = {
+        "wide": wide, "narrow": narrow, "side": side, "own": own,
+        "qkv_parts": qkv_parts, "out_parts": out_parts,
+        "qkv_width": nq + 2 * nk, "out_rows": nq,
+    }
+    group_arrays = []
+    for g in order:
+        att, q, k, v, q_raw, k_raw, rinv = saved[g]
+        group_arrays.append((q, k, v, att, q_raw, k_raw, rinv, weights[g][3], att.T))
+    w_all = jnp.concatenate([w for g in order for w in weights[g][:3]], axis=1)
+    sum_gu, sum_down, sum_qkv, sum_out, grad_tokens, gains = run_backward(
+        plan,
+        (length, qs, ks, norm_gain[None, :], gain_two[None, :]),
+        (branch, rows_one.T, w_all, tokens, grad_middle, cosine, sine),
+        group_arrays,
+        grad_gate_up,
+        grad_down,
     )
-    summed = lax.psum(tuple(g.astype(BF16) for g in own_grads), "wide")
-    gain_summed = lax.psum((gain_one, gain_two, q_gain, k_gain), ("wide", "narrow"))
+    hidden_units = w_gate.shape[1]
     return (
         output.astype(BF16),
         grad_tokens,
-        gain_summed[0],
-        summed[0].astype(F32),
-        summed[1].astype(F32),
-        summed[2].astype(F32),
-        gain_summed[2],
-        gain_summed[3],
-        summed[3].astype(F32),
-        gain_summed[1],
-        grad_w_gate.astype(F32),
-        grad_w_up.astype(F32),
-        grad_down.astype(F32),
+        gains[0],
+        sum_qkv[:, :nq].astype(F32),
+        sum_qkv[:, nq : nq + nk].astype(F32),
+        sum_qkv[:, nq + nk :].astype(F32),
+        gains[2, :HD] + gains[2, HD:TILE],
+        gains[3, :HD] + gains[3, HD:TILE],
+        sum_out.astype(F32),
+        gains[1],
+        sum_gu[:, :hidden_units].astype(F32),
+        sum_gu[:, hidden_units:].astype(F32),
+        sum_down.astype(F32),
     )
 
 

time: 573 us -> 433 us (0.76)
  waiting for transfers between devices: 259 us -> 27 us
  Pallas kernels: 49.6 us -> 199 us
  local copies, waits for them, and re-layouts: 29 us -> 70.7 us
  blocking collectives: 40.8 us -> 0 us
  matrix products: 114 us -> 78.4 us
  between operations: 15.2 us -> 1.69 us
  starting transfers between devices: 18.9 us -> 12.6 us
    psum x2 -> x0, waiting for transfers between devices: 203 us -> none  [the longest x1 164 us: on_device(): lax.psum((grad_down, grad_w_gate, grad_w_up), 'wide')]
    pallas_call x2 -> x1, Pallas kernels: 29.9 us -> 179 us  [run_backward(): pl.pallas_call(functools.partial(backward_kernel, plan), out_shape=tuple(...]
    psum x1 -> x0, blocking collectives: 40.8 us -> none  [on_device(): lax.psum((gain_one, gain_two, q_gain, k_gain), ('wide', 'narrow'))]
    dot_general x31 -> x16, matrix products: 114 us -> 78.4 us  [contract(): lax.dot_general(left_side, right_side, (((left_dim,), (right_dim,)), ((),...]
    ppermute x12 -> x8, waiting for transfers between devices: 56.1 us -> 27 us  [across(): lax.ppermute(array, 'narrow', [(i, (i + turn * side) % narrow) for i in r...]
    unnamed x136 -> x127, local copies, waits for them, and re-layouts: 12.6 us -> 25.7 us
    dynamic_update_slice x6 -> x8, local copies, waits for them, and re-layouts: 4.16 us -> 15.8 us  [gather(): lax.dynamic_update_slice(whole, within(array, turn), (source * size, 0))]
    convert_element_type x7 -> x8, other arithmetic: 13.6 us -> 23.2 us  [the longest x1 6.87 us: on_device(): sum_gu[:, hidden_units:].astype(F32)]
  transfers between devices with their start and end apart: 26 -> 19, of which waited for: 7 -> 1; matrix products, arithmetic and copies ran while one was open for 26% -> 33% of each run, Pallas kernels for 9% -> 5%
where the time goes in v2:
time: 433 us; the launch traced here: 427 us
  Pallas kernels  199 us (46%)
  matrix products  78.4 us (18%)
  local copies, waits for them, and re-layouts  70.7 us (16%)
  other arithmetic  36.8 us (8%)
  waiting for transfers between devices  27 us (6%)
  starting transfers between devices  12.6 us (3%)
    pallas_call x1, Pallas kernels, run_backward(): pl.pallas_call(functools.partial(backward_kernel, plan), out_shape=tuple(...  179 us
    dot_general x16, matrix products, contract(): lax.dot_general(left_side, right_side, (((left_dim,), (right_dim,)), ((),...  78.4 us
    ppermute x8, waiting for transfers between devices, across(): lax.ppermute(array, 'narrow', [(i, (i + turn * side) % narrow) for i in r...  27 us
    unnamed x127, local copies, waits for them, and re-layouts  25.7 us
    pallas_call x2, Pallas kernels, run_forward(): pl.pallas_call(attention_forward, out_shape=(shape((LEN, nq), BF16), shap...  19.9 us
    dynamic_update_slice x8, local copies, waits for them, and re-layouts, gather(): lax.dynamic_update_slice(whole, within(array, turn), (source * size, 0))  15.8 us
    ppermute x8, starting transfers between devices, across(): lax.ppermute(array, 'narrow', [(i, (i + turn * side) % narrow) for i in r...  9.92 us
  transfers between devices with their start and end apart: 19, of which 1 were waited for; matrix products, arithmetic and copies ran while one was open for 33% of the time, Pallas kernels for 5%

profile of v2, /device:TPU:0, one launch (start us, length us, event | category | flops | bytes accessed | tf_op | source)
XLA Modules:
  0.0 426.8 jit_solution(8821710461765023641)
XLA Ops:
  25.3 4.1 copy.29.x_ref
  30.5 9.8 %attention_forward.2 = (bf16[1024,256]{1,0:T(8,128)(2,1)S(1)}, bf16[1024,256]{1,0:T(8,128)(2,1)S(1)}, bf16[1024,128]{1,0:T(8,128)(2,1)S(1)}, bf16[1024,128]{1,0:...) custom-call(s32[1]{0:T(128)} %dynamic_slice.33.len_ref.refs_0_, ...), custom_call_target="tpu_custom_call" | custom-call | flops 3221225472 | bytes 8388608 | tf_op jit(solution)/shard_map/attention_forward/pallas_call | solution.py:590
  45.6 10.2 %attention_forward.3 = (bf16[1024,256]{1,0:T(8,128)(2,1)S(1)}, bf16[1024,256]{1,0:T(8,128)(2,1)S(1)}, bf16[1024,128]{1,0:T(8,128)(2,1)S(1)}, bf16[1024,128]{1,0:...) custom-call(s32[1]{0:T(128)} %dynamic_slice.33.len_ref.refs_0_, ...), custom_call_target="tpu_custom_call" | custom-call | flops 3221225472 | bytes 8388608 | tf_op jit(solution)/shard_map/attention_forward/pallas_call | solution.py:590
  94.1 5.4 %fusion.37 = f32[1024,1152]{1,0:T(8,128)S(1)} fusion(bf16[1024,1024]{0,1:T(8,128)(2,1)} %constant_dynamic-update-slice_fusion.14, bf16[1024,1152]{1,0:T(8,128)(2,1)} %param.24), kind=kOutput, calls=%fused_computation.94 | convolution fusion | flops 2415919104 | bytes 9175040 | tf_op jit(solution)/shard_map/dot_general | solution.py:46
  99.5 3.0 fusion.38
  102.5 8.5 %multiply_convert_fusion.2 = (bf16[1024,1152]{1,0:T(8,128)(2,1)S(1)}, bf16[1024,1152]{1,0:T(8,128)(2,1)S(1)}, bf16[1024,1152]{1,0:T(8,128)(2,1)}) fusion(f32[1024,1152]{1,0:T(8,128)S(1)} %fusion.37, f32[1024,1152]{1,0:T(8,128)S(1)} %fusion.38, bf16[1024,1024]{0,1:T(8,128)(2,1)} %constant_dynamic-update-slice_fusion.10, bf16[1152,1024]{1,0:T(8,128)(2,1)S(1)} %copy-done), kind=kOutput, calls=%fused_computation.15 | convolution fusion | flops 2434793472 | bytes 20971520 | tf_op jit(solution)/shard_map/dot_general | solution.py:46
  111.1 2.9 fusion.43
  114.1 2.9 convolution_add_fusion.2
  125.7 5.4 %fusion.40 = f32[1024,1152]{1,0:T(8,128)S(1)} fusion(bf16[1024,1024]{0,1:T(8,128)(2,1)} %constant_dynamic-update-slice_fusion.12, bf16[1024,1152]{1,0:T(8,128)(2,1)} %param.24), kind=kOutput, calls=%fused_computation.97 | convolution fusion | flops 2415919104 | bytes 9175040 | tf_op jit(solution)/shard_map/dot_general | solution.py:46
  131.1 3.0 fusion.41
  134.1 6.1 %multiply_convert_fusion = (bf16[1024,1152]{1,0:T(8,128)(2,1)S(1)}, bf16[1024,1152]{1,0:T(8,128)(2,1)S(1)}, bf16[1024,1152]{1,0:T(8,128)(2,1)S(1)}) fusion(f32[1024,1152]{1,0:T(8,128)S(1)} %fusion.40, f32[1024,1152]{1,0:T(8,128)S(1)} %fusion.41, bf16[1024,1024]{0,1:T(8,128)(2,1)S(1)} %copy-done.39, bf16[1152,1024]{1,0:T(8,128)(2,1)S(1)} %copy-done), kind=kOutput, calls=%fused_computation.13 | convolution fusion | flops 2434793472 | bytes 20971520 | tf_op jit(solution)/shard_map/dot_general | solution.py:46
  140.3 2.9 fusion.42
  143.7 2.9 fusion.44
  146.6 2.9 convolution_add_fusion.1
  150.0 2.9 fusion.39
  159.2 17.6 %fusion.8.refs_12_ = bf16[1024,2304]{1,0:T(8,128)(2,1)} fusion(bf16[1024,1152]{1,0:T(8,128)(2,1)} %copy-done.53, bf16[1024,1152]{1,0:T(8,128)(2,1)} %copy-done.52, bf16[1024,1152]{1,0:T(8,128)(2,1)} %copy-done.55, bf16[1024,1152]{1,0:T(8,128)(2,1)} %copy-done.54, bf16[1024,1024]{0,1:T(8,128)(2,1)} %constant_dynamic-update-slice_fusion.12, ...), kind=kOutput, calls=%fused_computation.8 | convolution fusion | flops 9712173056 | bytes 18350080 | tf_op jit(solution)/shard_map/dot_general | solution.py:46
  176.9 27.0 %collective-permute-done.17 = bf16[512,1024]{1,0:T(8,128)(2,1)} collective-permute-done((bf16[512,1024]{1,0:T(8,128)(2,1)}, bf16[512,1024]{1,0:T(8,128)(2,1)}, u32[]{:S(2)}, u32[]{:S(2)}) %collective-permute-start.17) | collective-permute-done | bytes 1048608 | tf_op jit(solution)/shard_map/ppermute | solution.py:701
  203.9 3.7 multiply_reduce_fusion
  208.5 4.3 %fusion.34 = (bf16[512,1024]{1,0:T(8,128)(2,1)S(1)}, f32[512,1024]{1,0:T(8,128)}, bf16[512,1024]{1,0:T(8,128)(2,1)}) fusion(f32[512]{0:T(512)S(1)} %broadcast_multiply_fusion, f32[512,1024]{1,0:T(8,128)S(1)} %copy-done.21, f32[512]{0:T(512)S(1)} %get-tuple-element.75, f32[512,1024]{1,0:T(8,128)S(1)} %get-tuple-element.57, f32[1024]{0:T(1024)S(1)} %copy-done.44, ...), kind=kLoop, calls=%fused_computation.91 | loop fusion | flops 7340032 | bytes 13641732 | tf_op jit(solution)/shard_map/convert_element_type | solution.py:792
  212.9 8.2 %fusion.21.refs_13_ = bf16[1152,1024]{1,0:T(8,128)(2,1)} fusion(bf16[1024,1024]{0,1:T(8,128)(2,1)S(1)} %copy-done.40, bf16[1024,1024]{0,1:T(8,128)(2,1)} %constant_dynamic-update-slice_fusion.10, bf16[1024,1152]{1,0:T(8,128)(2,1)S(1)} %copy-done.59, bf16[1024,1152]{1,0:T(8,128)(2,1)S(1)} %copy-done.57), kind=kOutput, calls=%fused_computation.27 | convolution fusion | flops 4850843648 | bytes 11272192 | tf_op jit(solution)/shard_map/dot_general | solution.py:46
  225.4 2.6 copy.42.refs_5_
  228.0 179.5 %backward_and_sums.1 = (bf16[1024,2304]{1,0:T(8,128)(2,1)}, bf16[1152,1024]{1,0:T(8,128)(2,1)}, bf16[1024,512]{1,0:T(8,128)(2,1)}, bf16[256,1024]{1,0:T(8,128)(2...) custom-call(s32[1]{0:T(128)} %dynamic_slice.33.len_ref.refs_0_, f32[1,128]{1,0:T(1,128)} %copy-done.8, f32[1,128]{1,0:T(1,128)} %copy-done.9, ...), custom_call_target="tpu_custom_call" | custom-call | flops 20000000000 | bytes 67108864 | tf_op jit(solution)/shard_map/backward_and_sums/pallas_call | solution.py:642
  414.6 6.9 %slice_convert_fusion = (f32[1024,1152]{1,0:T(8,128)}, f32[1024,1152]{1,0:T(8,128)}) fusion(bf16[1024,2304]{1,0:T(8,128)(2,1)} %get-tuple-element.51), kind=kLoop, calls=%fused_computation.31 | loop fusion | flops 2359296 | bytes 14155776 | tf_op jit(solution)/shard_map/convert_element_type | solution.py:842
  421.4 2.7 convert_element_type.139
  (219 shorter events, 99.9 us)
Async XLA Ops:
  0.6 101.9 %copy-start = (bf16[1152,1024]{1,0:T(8,128)(2,1)S(1)}, bf16[1152,1024]{1,0:T(8,128)(2,1)}, u32[]{:S(2)}) copy-start(bf16[1152,1024]{1,0:T(8,128)(2,1)} %param.26) | copy-start | bytes 7077892
  4.9 13.8 %collective-permute-start = (bf16[512,1024]{1,0:T(8,128)(2,1)}, bf16[512,1024]{1,0:T(8,128)(2,1)}, u32[]{:S(2)}, u32[]{:S(2)}) collective-permute-start(bf16[512,1024]{1,0:T(8,128)(2,1)} %fusion.28), channel_id=1, source_target_pairs={{0,1},{1,0},{2,3},{3,2},{4,5},{5,4},{6,7},{7,6},{8,9},{9,8},{10,11... | collective-permute-start | bytes 3145736 | tf_op jit(solution)/shard_map/ppermute | solution.py:706
  5.4 39.0 %collective-permute-start.1 = (bf16[1024,256]{1,0:T(8,128)(2,1)}, bf16[1024,256]{1,0:T(8,128)(2,1)}, u32[]{:S(2)}, u32[]{:S(2)}) collective-permute-start(bf16[1024,256]{1,0:T(8,128)(2,1)} %wq_ref.1), channel_id=1, source_target_pairs={{0,2},{1,3},{2,0},{3,1},{4,6},{5,7},{6,4},{7,5},{8,10},{9,11},{10,... | collective-permute-start | bytes 1572872 | tf_op jit(solution)/shard_map/ppermute | solution.py:701
  7.9 36.4 %collective-permute-start.2 = (bf16[1024,128]{1,0:T(8,128)(2,1)}, bf16[1024,128]{1,0:T(8,128)(2,1)}, u32[]{:S(2)}, u32[]{:S(2)}) collective-permute-start(bf16[1024,128]{1,0:T(8,128)(2,1)} %wk_ref.1), channel_id=1, source_target_pairs={{0,2},{1,3},{2,0},{3,1},{4,6},{5,7},{6,4},{7,5},{8,10},{9,11},{10,... | collective-permute-start | bytes 786440 | tf_op jit(solution)/shard_map/ppermute | solution.py:701
  8.0 36.4 %collective-permute-start.3 = (bf16[1024,128]{1,0:T(8,128)(2,1)}, bf16[1024,128]{1,0:T(8,128)(2,1)}, u32[]{:S(2)}, u32[]{:S(2)}) collective-permute-start(bf16[1024,128]{1,0:T(8,128)(2,1)} %wv_ref.1), channel_id=1, source_target_pairs={{0,2},{1,3},{2,0},{3,1},{4,6},{5,7},{6,4},{7,5},{8,10},{9,11},{10,... | collective-permute-start | bytes 786440 | tf_op jit(solution)/shard_map/ppermute | solution.py:701
  9.9 48.0 %collective-permute-start.4 = (bf16[256,1024]{1,0:T(8,128)(2,1)}, bf16[256,1024]{1,0:T(8,128)(2,1)}, u32[]{:S(2)}, u32[]{:S(2)}) collective-permute-start(bf16[256,1024]{1,0:T(8,128)(2,1)} %refs_30_.1), channel_id=1, source_target_pairs={{0,2},{1,3},{2,0},{3,1},{4,6},{5,7},{6,4},{7,5},{8,10},{9,11},{10,... | collective-permute-start | bytes 1572872 | tf_op jit(solution)/shard_map/ppermute | solution.py:701
  18.7 47.6 %collective-permute-start.14 = (bf16[512,1024]{0,1:T(8,128)(2,1)}, bf16[512,1024]{0,1:T(8,128)(2,1)}, u32[]{:S(2)}, u32[]{:S(2)}) collective-permute-start(bf16[512,1024]{0,1:T(8,128)(2,1)} %copy.35), channel_id=1, source_target_pairs={{0,2},{1,3},{2,0},{3,1},{4,6},{5,7},{6,4},{7,5},{8,10},{9,11},{10,... | collective-permute-start | bytes 3145736 | tf_op jit(solution)/shard_map/ppermute | solution.py:701
  44.3 34.2 %copy-start.2 = (bf16[1024,256]{1,0:T(8,128)(2,1)}, bf16[1024,256]{1,0:T(8,128)(2,1)S(1)}, u32[]{:S(2)}) copy-start(bf16[1024,256]{1,0:T(8,128)(2,1)S(1)} %get-tuple-element.33.refs_26_) | copy-start | bytes 1572868
  59.9 6.5 %collective-permute-start.5 = (bf16[512,1024]{1,0:T(8,128)(2,1)S(1)}, bf16[512,1024]{1,0:T(8,128)(2,1)S(1)}, u32[]{:S(2)}, u32[]{:S(2)}) collective-permute-start(bf16[512,1024]{1,0:T(8,128)(2,1)S(1)} %dynamic-slice_convert_fusion.4), channel_id=1, source_target_pairs={{0,1},{1,0},{2,3},{3,2},{4,5},{5,4},{6,7},{7,6},{8,9},{9,8},{10,11... | collective-permute-start | bytes 3145736 | tf_op jit(solution)/shard_map/ppermute | solution.py:706
  60.0 21.1 %collective-permute-start.12 = (bf16[512,1024]{0,1:T(8,128)(2,1)}, bf16[512,1024]{0,1:T(8,128)(2,1)}, u32[]{:S(2)}, u32[]{:S(2)}) collective-permute-start(bf16[512,1024]{0,1:T(8,128)(2,1)} %copy.35), channel_id=1, source_target_pairs={{0,1},{1,0},{2,3},{3,2},{4,5},{5,4},{6,7},{7,6},{8,9},{9,8},{10,11... | collective-permute-start | bytes 3145736 | tf_op jit(solution)/shard_map/ppermute | solution.py:706
  66.3 21.7 %collective-permute-start.15 = (bf16[512,1024]{0,1:T(8,128)(2,1)}, bf16[512,1024]{0,1:T(8,128)(2,1)}, u32[]{:S(2)}, u32[]{:S(2)}) collective-permute-start(bf16[512,1024]{0,1:T(8,128)(2,1)} %collective-permute-done.14), channel_id=1, source_target_pairs={{0,1},{1,0},{2,3},{3,2},{4,5},{5,4},{6,7},{7,6},{8,9},{9,8},{10,11... | collective-permute-start | bytes 3145736 | tf_op jit(solution)/shard_map/ppermute | solution.py:706
  68.4 23.0 %collective-permute-start.6 = (bf16[512,1024]{1,0:T(8,128)(2,1)}, bf16[512,1024]{1,0:T(8,128)(2,1)}, u32[]{:S(2)}, u32[]{:S(2)}) collective-permute-start(bf16[512,1024]{1,0:T(8,128)(2,1)} %multiply_convert_fusion.6), channel_id=1, source_target_pairs={{0,1},{1,0},{2,3},{3,2},{4,5},{5,4},{6,7},{7,6},{8,9},{9,8},{10,11... | collective-permute-start | bytes 3145736 | tf_op jit(solution)/shard_map/ppermute | solution.py:706
  86.3 27.7 %collective-permute-start.8 = (bf16[512,1024]{1,0:T(8,128)(2,1)}, bf16[512,1024]{1,0:T(8,128)(2,1)}, u32[]{:S(2)}, u32[]{:S(2)}) collective-permute-start(bf16[512,1024]{1,0:T(8,128)(2,1)} %multiply_convert_fusion.6), channel_id=1, source_target_pairs={{0,2},{1,3},{2,0},{3,1},{4,6},{5,7},{6,4},{7,5},{8,10},{9,11},{10,... | collective-permute-start | bytes 3145736 | tf_op jit(solution)/shard_map/ppermute | solution.py:701
  114.0 9.1 %collective-permute-start.9 = (bf16[512,1024]{1,0:T(8,128)(2,1)}, bf16[512,1024]{1,0:T(8,128)(2,1)}, u32[]{:S(2)}, u32[]{:S(2)}) collective-permute-start(bf16[512,1024]{1,0:T(8,128)(2,1)} %collective-permute-done.8), channel_id=1, source_target_pairs={{0,1},{1,0},{2,3},{3,2},{4,5},{5,4},{6,7},{7,6},{8,9},{9,8},{10,11... | collective-permute-start | bytes 3145736 | tf_op jit(solution)/shard_map/ppermute | solution.py:706
  119.3 57.6 %collective-permute-start.13 = (bf16[512,1024]{1,0:T(8,128)(2,1)}, bf16[512,1024]{1,0:T(8,128)(2,1)}, u32[]{:S(2)}, u32[]{:S(2)}) collective-permute-start(bf16[512,1024]{1,0:T(8,128)(2,1)} %dynamic-slice_convert_fusion.1), channel_id=1, source_target_pairs={{0,1},{1,0},{2,3},{3,2},{4,5},{5,4},{6,7},{7,6},{8,9},{9,8},{10,11... | collective-permute-start | bytes 3145736 | tf_op jit(solution)/shard_map/ppermute | solution.py:706
  143.4 11.1 %collective-permute-start.10 = (bf16[512,1024]{1,0:T(8,128)(2,1)S(1)}, bf16[512,1024]{1,0:T(8,128)(2,1)S(1)}, u32[]{:S(2)}, u32[]{:S(2)}) collective-permute-start(bf16[512,1024]{1,0:T(8,128)(2,1)S(1)} %dynamic-slice_convert_fusion.2), channel_id=1, source_target_pairs={{0,1},{1,0},{2,3},{3,2},{4,5},{5,4},{6,7},{7,6},{8,9},{9,8},{10,11... | collective-permute-start | bytes 3145736 | tf_op jit(solution)/shard_map/ppermute | solution.py:706
  149.7 6.9 %collective-permute-start.16 = (bf16[512,1024]{1,0:T(8,128)(2,1)S(1)}, bf16[512,1024]{1,0:T(8,128)(2,1)S(1)}, u32[]{:S(2)}, u32[]{:S(2)}) collective-permute-start(bf16[512,1024]{1,0:T(8,128)(2,1)S(1)} %dynamic-slice_convert_fusion), channel_id=1, source_target_pairs={{0,1},{1,0},{2,3},{3,2},{4,5},{5,4},{6,7},{7,6},{8,9},{9,8},{10,11... | collective-permute-start | bytes 3145736 | tf_op jit(solution)/shard_map/ppermute | solution.py:706
  154.2 53.4 %collective-permute-start.7 = (bf16[512,1024]{1,0:T(8,128)(2,1)}, bf16[512,1024]{1,0:T(8,128)(2,1)S(1)}, u32[]{:S(2)}, u32[]{:S(2)}) collective-permute-start(bf16[512,1024]{1,0:T(8,128)(2,1)} %dynamic-slice_convert_fusion.3), channel_id=1, source_target_pairs={{0,1},{1,0},{2,3},{3,2},{4,5},{5,4},{6,7},{7,6},{8,9},{9,8},{10,11... | collective-permute-start | bytes 3145736 | tf_op jit(solution)/shard_map/ppermute | solution.py:706
  155.8 51.7 %collective-permute-start.11 = (bf16[512,1024]{1,0:T(8,128)(2,1)}, bf16[512,1024]{1,0:T(8,128)(2,1)}, u32[]{:S(2)}, u32[]{:S(2)}) collective-permute-start(bf16[512,1024]{1,0:T(8,128)(2,1)} %add_convert_fusion.2), channel_id=1, source_target_pairs={{0,2},{1,3},{2,0},{3,1},{4,6},{5,7},{6,4},{7,5},{8,10},{9,11},{10,... | collective-permute-start | bytes 3145736 | tf_op jit(solution)/shard_map/ppermute | solution.py:701
  158.0 45.9 %copy-start.21 = (f32[512,1024]{1,0:T(8,128)S(1)}, f32[512,1024]{1,0:T(8,128)}, u32[]{:S(2)}) copy-start(f32[512,1024]{1,0:T(8,128)} %copy-done.20) | copy-start | bytes 6291460
  158.0 45.9 %collective-permute-start.17 = (bf16[512,1024]{1,0:T(8,128)(2,1)}, bf16[512,1024]{1,0:T(8,128)(2,1)}, u32[]{:S(2)}, u32[]{:S(2)}) collective-permute-start(bf16[512,1024]{1,0:T(8,128)(2,1)} %add_convert_fusion), channel_id=1, source_target_pairs={{0,2},{1,3},{2,0},{3,1},{4,6},{5,7},{6,4},{7,5},{8,10},{9,11},{10,... | collective-permute-start | bytes 3145736 | tf_op jit(solution)/shard_map/ppermute | solution.py:701
  176.9 31.7 %copy-start.25 = (bf16[512,1024]{1,0:T(8,128)(2,1)S(1)}, bf16[512,1024]{1,0:T(8,128)(2,1)}, u32[]{:S(2)}) copy-start(bf16[512,1024]{1,0:T(8,128)(2,1)} %param.27) | copy-start | bytes 3145732
  176.9 31.7 %copy-start.30 = (f32[1024,1024]{1,0:T(8,128)S(1)}, f32[1024,1024]{1,0:T(8,128)}, u32[]{:S(2)}) copy-start(f32[1024,1024]{1,0:T(8,128)} %copy-done.29) | copy-start | bytes 12582916
  212.9 10.9 %collective-permute-start.18 = (bf16[512,1024]{1,0:T(8,128)(2,1)S(1)}, bf16[512,1024]{1,0:T(8,128)(2,1)}, u32[]{:S(2)}, u32[]{:S(2)}) collective-permute-start(bf16[512,1024]{1,0:T(8,128)(2,1)S(1)} %get-tuple-element.55), channel_id=1, source_target_pairs={{0,1},{1,0},{2,3},{3,2},{4,5},{5,4},{6,7},{7,6},{8,9},{9,8},{10,11... | collective-permute-start | bytes 3145736 | tf_op jit(solution)/shard_map/ppermute | solution.py:706
  (55 other events, 261.0 us)

commit v3 on v2

v3 whole, which is shorter than its diff:
```python
import functools
import math

import jax
import jax.numpy as jnp
from jax import lax
from jax.experimental import pallas as pl
from jax.experimental.pallas import tpu as pltpu
from jax.sharding import PartitionSpec as P

HD = 64
LEN = 1024
BLK = 256
TILE = 2 * HD

EPSILON = 1e-05
ROPE_BASE = 1000000.0
F32 = jnp.float32
BF16 = jnp.bfloat16
VMEM_LIMIT = 48 * 1024 * 1024
BACK_LIMIT = 60 * 1024 * 1024


def rope_tables(length, width):
    half_width = width // 2
    frequency = ROPE_BASE ** (-(2.0 * jnp.arange(half_width, dtype=jnp.float32)) / width)
    angles = jnp.arange(length, dtype=jnp.float32)[:, None] * frequency[None, :]
    return (jnp.cos(angles), jnp.sin(angles))


def row_norm(values_in, gain_vec):
    inv_rms = lax.rsqrt(jnp.mean(values_in * values_in, axis=-1, keepdims=True) + EPSILON)
    return (values_in * inv_rms * gain_vec, inv_rms)


def contract(left_side, right_side, left_dim, right_dim):
    return lax.dot_general(
        left_side,
        right_side,
        (((left_dim,), (right_dim,)), ((), ())),
        preferred_element_type=F32,
    )


def lanes(shape):
    return lax.broadcasted_iota(jnp.int32, shape, 1)


def group_ones():
    rows = lax.broadcasted_iota(jnp.int32, (TILE, TILE), 0) // HD
    cols = lax.broadcasted_iota(jnp.int32, (TILE, TILE), 1) // HD
    return jnp.where(rows == cols, 1.0, 0.0).astype(BF16)


def group_sum(values_in, ones):
    high = values_in.astype(BF16)
    rest = (values_in - high.astype(F32)).astype(BF16)
    return contract(high, ones, 1, 0) + contract(rest, ones, 1, 0)


def swap_halves(values_in):
    half = HD // 2
    front = lax.rem(lanes(values_in.shape), HD) < half
    return jnp.where(
        front, pltpu.roll(values_in, TILE - half, 1), pltpu.roll(values_in, half, 1)
    )


def attention_forward(
    len_ref, x_ref, wq_ref, wk_ref, wv_ref, qs_ref, ks_ref, cos_ref, sin_ref,
    att_ref, q_ref, k_ref, v_ref, qraw_ref, kraw_ref, rinv_ref,
    vaug_ref,
):
    length = len_ref[0]
    heads = wk_ref.shape[1] // HD
    ones = group_ones()

    def norm_rope(raw, scale, cosine, sine):
        inv = lax.rsqrt(group_sum(raw * raw, ones) * (1.0 / HD) + EPSILON)
        scaled = raw * inv * scale
        return scaled * cosine + swap_halves(scaled) * sine

    for start in range(0, LEN, BLK):
        rows = slice(start, start + BLK)
        x = x_ref[rows, :]
        cosine, sine = cos_ref[rows, :], sin_ref[rows, :]
        real = (lax.broadcasted_iota(jnp.int32, (BLK, TILE), 0) + start) < length
        q_raw = contract(x, wq_ref[...], 1, 0)
        qraw_ref[rows, :] = q_raw
        for t in range(heads):
            cols = slice(t * TILE, (t + 1) * TILE)
            turned = norm_rope(q_raw[:, cols], qs_ref[...], cosine, sine)
            q_ref[rows, cols] = (turned * (1.0 / math.sqrt(HD))).astype(BF16)
        k_raw = contract(x, wk_ref[...], 1, 0)
        kraw_ref[rows, :] = k_raw
        v_raw = contract(x, wv_ref[...], 1, 0)
        for t in range(heads // 2):
            cols = slice(t * TILE, (t + 1) * TILE)
            turned = norm_rope(k_raw[:, cols], ks_ref[...], cosine, sine)
            k_ref[rows, cols] = jnp.where(real, turned, 0.0).astype(BF16)
            v_pair = jnp.where(real, v_raw[:, cols], 0.0)
            v_ref[rows, cols] = v_pair.astype(BF16)
            lane = lanes((BLK, TILE))
            mark = jnp.where(real & (lane == HD), 1.0, 0.0)
            vaug_ref[2 * t, rows, :] = jnp.where(lane < HD, v_pair, mark).astype(BF16)
            vaug_ref[2 * t + 1, rows, :] = jnp.where(
                lane < HD, pltpu.roll(v_pair, HD, 1), mark
            ).astype(BF16)

    row_ids = lax.rem(lax.broadcasted_iota(jnp.int32, (2 * BLK, BLK), 0), BLK)
    causal = lax.broadcasted_iota(jnp.int32, (2 * BLK, BLK), 1) <= row_ids
    for h in range(heads):
        for i in range(LEN // BLK):
            rows = slice(i * BLK, (i + 1) * BLK)
            low = h * TILE
            q_two = jnp.concatenate(
                [q_ref[rows, low : low + HD], q_ref[rows, low + HD : low + TILE]], axis=0
            )
            total = jnp.zeros((2 * BLK, TILE), F32)
            for j in range(i + 1):
                keys = slice(j * BLK, (j + 1) * BLK)
                scores = contract(q_two, k_ref[keys, h * HD : (h + 1) * HD], 1, 1)
                weight = jnp.exp(scores)
                if i == j:
                    weight = jnp.where(causal, weight, 0.0)
                total += contract(weight.astype(BF16), vaug_ref[h, keys, :], 1, 0)
            inv = 1.0 / total[:, HD : HD + 1]
            mixed = total[:, :HD] * inv
            att_ref[rows, low : low + HD] = mixed[:BLK].astype(BF16)
            att_ref[rows, low + HD : low + TILE] = mixed[BLK:].astype(BF16)
            rinv_ref[rows, low : low + HD] = jnp.broadcast_to(inv[:BLK], (BLK, HD))
            rinv_ref[rows, low + HD : low + TILE] = jnp.broadcast_to(inv[BLK:], (BLK, HD))


class Ring:
    def __init__(self, count, place, target, turn, chunk, first, rows, own, source, out, land, sends, recvs):
        self.count, self.place, self.target, self.turn = count, place, target, turn
        self.chunk, self.first, self.rows = chunk, first, rows
        self.own, self.source, self.out, self.land = own, source, out, land
        self.sends, self.recvs = sends, recvs
        self.done = 0

    def index(self, steps):
        return lax.rem(self.place + self.turn * steps + 2 * self.count, self.count)

    def part(self, ref, steps):
        start = pl.multiple_of(self.index(steps) * self.chunk + self.first, 16)
        return ref.at[pl.ds(start, self.rows), :]

    def copy(self, step, source, target):
        return pltpu.make_async_remote_copy(
            src_ref=source,
            dst_ref=target,
            send_sem=self.sends.at[step],
            recv_sem=self.recvs.at[step],
            device_id={"wide": self.target},
            device_id_type=pl.DeviceIdType.MESH,
        )

    def copy_of(self, step):
        last = self.count - 1
        if step == 0:
            return self.copy(0, self.part(self.source, 0), self.land.at[0])
        if step < last:
            return self.copy(step, self.land.at[step - 1], self.land.at[step])
        steps = last - step + 1
        where = self.part(self.out, steps)
        return self.copy(step, self.land.at[last - 1] if step == last else where, where)

    def begin(self):
        self.copy_of(0).start()

    @property
    def left(self):
        return 2 * (self.count - 1) - self.done

    def tick(self, keep):
        step, last = self.done, self.count - 1
        self.done += 1
        if step < last:
            slot = self.land.at[step]
            self.copy(step, slot, slot).wait_recv()
            start = pl.multiple_of(self.index(-step - 1) * self.chunk + self.first, 16)

            @pl.loop(0, self.rows // 16)
            def _(r):
                at = pl.multiple_of(r * 16, 16)
                mine = self.own[pl.ds(pl.multiple_of(start + at, 16), 16), :].astype(F32)
                slot[pl.ds(at, 16), :] = (slot[pl.ds(at, 16), :].astype(F32) + mine).astype(BF16)

            if step == last - 1:
                kept = pltpu.make_async_copy(slot, self.part(self.out, 1), keep)
                kept.start()
                self.copy_of(last).start()
                kept.wait()
            else:
                self.copy_of(step + 1).start()
        else:
            where = self.part(self.out, last - step)
            self.copy(step, where, where).wait_recv()
            if self.left:
                self.copy_of(step + 1).start()

    def finish(self):
        for step in range(2 * (self.count - 1)):
            self.copy_of(step).wait_send()


def ring_rows(rows, count):
    chunk = -(-rows // (count * 16)) * 16
    forward = -(-chunk // 32) * 16
    return chunk, forward, chunk - forward


def main_kernel(plan, *refs):
    count, narrow, side = plan["wide"], plan["narrow"], plan["side"]
    groups, own_rows = plan["groups"], plan["own"]
    taken = 0

    def take(number):
        nonlocal taken
        taken += number
        return refs[taken - number : taken]

    len_ref, qs_ref, ks_ref, ng_ref, fg_ref = take(5)
    xin, cin, wg_in, wu_in, wd_in, mid_in, tok_in, cos_in, sin_in, turned_in, w_all_in = take(11)
    groups_in = [take(9) for _ in range(groups)]
    gu_out, gd_out, a1_out, a2_out, out_out, gt_out = take(6)
    (gains_ref,) = take(1)
    x_l, x_r, c_l, c_r = take(4)
    gu_own, gd_own, px1, px2, rx1, rx2, own1, own2 = take(8)
    lands = take(plan["lands"])
    send_b, send_o, got_bl, got_ol, got_br, got_or = take(6)
    got_gn = got_br
    far_b, far_o, own_b, own_o, ownr_b, ownr_o = take(6)
    branch = x_r
    gain_mine, gain_in = take(2)
    load_sems, ring_sends, ring_recvs, keep_sem, sends, recvs, free_sem = take(7)

    w = lax.axis_index("wide")
    n = lax.axis_index("narrow")
    half = count // 2
    place_ring = lax.rem((1 - w % 2) * (count - w // 2) + (w % 2) * (w // 2 + 1), count)

    def at_place(p):
        far = lax.rem(p + count - 1, count) // half
        z = (1 - far) * (p - 1) + far * lax.rem(count - p, count)
        return 2 * z + 1 - far

    onward = at_place(lax.rem(place_ring + 1, count))
    behind = at_place(lax.rem(place_ring + count - 1, count))
    across = lax.rem(n + side, narrow)
    place = lax.rem(n, side)
    turns = range(1, side)

    def mate(turn):
        return n - place + lax.rem(place + turn, side)

    def flip(value, bit):
        return value + bit - 2 * bit * lax.rem(value // bit, 2)

    doubling = [("narrow", 2**e) for e in range(int(math.log2(narrow)))]
    doubling += [("wide", 2**e) for e in range(int(math.log2(count)))]
    partners = [{axis: flip(n if axis == "narrow" else w, bit)} for axis, bit in doubling]
    peers = [{"wide": onward}, {"wide": behind}, {"narrow": across}]
    peers += [{"narrow": mate(t)} for t in turns] + partners

    barrier = pltpu.get_barrier_semaphore()
    for peer in peers:
        pl.semaphore_signal(barrier, inc=1, device_id=peer, device_id_type=pl.DeviceIdType.MESH)
    pl.semaphore_wait(barrier, len(peers))

    numbers = {}
    unsent = []

    def remote(name, source, target, device):
        number = numbers.setdefault(name, len(numbers))
        return pltpu.make_async_remote_copy(
            src_ref=source,
            dst_ref=target,
            send_sem=sends.at[number],
            recv_sem=recvs.at[number],
            device_id=device,
            device_id_type=pl.DeviceIdType.MESH,
        )

    def send(name, source, target, device):
        copy = remote(name, source, target, device)
        copy.start()
        unsent.append((name, source, target, device))

    def sent(name):
        for entry in [e for e in unsent if e[0][: len(name)] == name]:
            remote(*entry).wait_send()
            unsent.remove(entry)

    def received(name, target, device):
        remote(name, target, target, device).wait_recv()

    def block(ref, turn):
        start = pl.multiple_of(lax.rem(place + turn, side) * own_rows, BLK)
        return ref.at[pl.ds(start, own_rows), :]

    to_across = {"narrow": across}

    def to_mates(name, source, target):
        for t in turns:
            send(f"{name}{t}", source, target, {"narrow": mate(t)})

    def from_mates(name, ref):
        for t in turns:
            received(f"{name}{t}", block(ref, side - t), {"narrow": mate(t)})

    loading = {}

    def load(name, source, target):
        copy = pltpu.make_async_copy(source, target, load_sems.at[len(loading)])
        loading[name] = [copy]
        copy.start()

    def need(*names):
        for name in names:
            if loading[name]:
                loading[name].pop().wait()

    rings = []
    used = 0
    for own, out, rows in (
        (gu_own, gu_out, plan["rows"][0]),
        (gd_own, gd_out, plan["rows"][1]),
        (own1, a1_out, plan["rows"][2]),
        (own2, a2_out, plan["rows"][3]),
    ):
        chunk, forward, backward = ring_rows(rows, count)
        pair = []
        for turn, target, first, size in ((1, onward, 0, forward), (-1, behind, forward, backward)):
            if size:
                pair.append(
                    Ring(
                        count, place_ring, target, turn, chunk, first, size, own, own, out,
                        lands[used], ring_sends.at[used], ring_recvs.at[used],
                    )
                )
                used += 1
        rings.append(pair)

    def begin(pair):
        for ring in pair:
            ring.begin()

    def tick(pair):
        for ring in pair:
            if ring.left:
                ring.tick(keep_sem)

    units = wg_in.shape[1]

    def feed_forward(wg, wu, wd, hid, gg, gu):
        load("x", xin, block(x_l, 0))
        load("wg", wg_in, wg)
        load("wu", wu_in, wu)
        load("c", cin, block(c_l, 0))
        load("wd", wd_in, wd)
        send("xy", xin, block(x_r, 0), to_across)
        to_mates("xl", xin, block(x_l, 0))
        to_mates("cl", cin, block(c_l, 0))
        send("cy", cin, block(c_r, 0), to_across)

        def rows_pass(x, c, turn, back_to, out_to):
            @pl.loop(0, own_rows // BLK)
            def _(r):
                to = pl.ds(pl.multiple_of(r * BLK, BLK), BLK)
                at = lax.rem(place + turn, side) * own_rows + r * BLK
                rows = pl.ds(pl.multiple_of(at, BLK), BLK)
                gate = contract(x[rows, :], wg[...], 1, 0)
                up = contract(x[rows, :], wu[...], 1, 0)
                grad = contract(c[rows, :], wd[...], 1, 1)
                share = 1.0 / (1.0 + jnp.exp(-gate))
                silu = gate * share
                hid[rows, :] = (silu * up).astype(BF16)
                gg[rows, :] = (grad * up * (share + silu * (1.0 - share))).astype(BF16)
                gu[rows, :] = (grad * silu).astype(BF16)
                back = contract(gg[rows, :], wg[...], 1, 1)
                back += contract(gu[rows, :], wu[...], 1, 1)
                back_to[to, :] = back.astype(BF16)
                out_to[to, :] = contract(hid[rows, :], wd[...], 1, 0).astype(BF16)

        depth = x_l.shape[1]

        def weight_pass(x, c, more):
            step = 384 if units % 384 == 0 else units
            for start in range(0, units, step):
                rows = slice(start, start + step)
                part = contract(hid[:, rows], c[...], 0, 0)
                if more:
                    part += gd_own[rows, :].astype(F32)
                gd_own[rows, :] = part.astype(BF16)
            if more:
                begin(rings[1])
            for start in range(0, depth, BLK):
                rows = slice(start, start + BLK)
                for first, grad in ((0, gg), (units, gu)):
                    part = contract(x[:, rows], grad[...], 0, 0)
                    cols = slice(first, first + units)
                    if more:
                        part += gu_own[rows, cols].astype(F32)
                    gu_own[rows, cols] = part.astype(BF16)

        extra = gd_own.shape[0] - units
        if extra:
            gd_own[units:, :] = jnp.zeros((extra, depth), BF16)
        need("x", "wg", "wu", "c", "wd")
        rows_pass(x_l, c_l, 0, own_b, own_o)
        from_mates("xl", x_l)
        from_mates("cl", c_l)
        for t in turns:
            rows_pass(x_l, c_l, t, send_b.at[t - 1], send_o.at[t - 1])
            send(f"bl{t}", send_b.at[t - 1], got_bl.at[t - 1], {"narrow": mate(t)})
            send(f"ol{t}", send_o.at[t - 1], got_ol.at[t - 1], {"narrow": mate(t)})
        weight_pass(x_l, c_l, False)

        received("xy", block(x_r, 0), to_across)
        to_mates("xr", block(x_r, 0), block(x_r, 0))
        received("cy", block(c_r, 0), to_across)
        to_mates("cr", block(c_r, 0), block(c_r, 0))
        sent("bl")
        sent("ol")
        from_mates("xr", x_r)
        from_mates("cr", c_r)
        for t in turns:
            rows_pass(x_r, c_r, t, send_b.at[t - 1], send_o.at[t - 1])
            send(f"br{t}", send_b.at[t - 1], got_br.at[t - 1], {"narrow": mate(t)})
            send(f"or{t}", send_o.at[t - 1], got_or.at[t - 1], {"narrow": mate(t)})
        rows_pass(x_r, c_r, 0, ownr_b, ownr_o)
        for name, mine, got, far in (("b", ownr_b, got_br, far_b), ("o", ownr_o, got_or, far_o)):
            for t in turns:
                received(f"{name}r{t}", got.at[t - 1], {"narrow": mate(t)})

            @pl.loop(0, own_rows // 32)
            def _(r):
                rows = pl.ds(pl.multiple_of(r * 32, 32), 32)
                total = mine[rows, :].astype(F32)
                for t in turns:
                    total += got[t - 1, rows, :].astype(F32)
                mine[rows, :] = total.astype(BF16)

            send(name + "y", mine, far, to_across)
        weight_pass(x_r, c_r, True)
        begin(rings[0])
        for name in ("xy", "xl", "cl", "cy", "xr", "cr", "br", "or"):
            sent(name)

    weights = [pltpu.VMEM(ref.shape, BF16) for ref in (wg_in, wu_in, wd_in)]
    pl.run_scoped(feed_forward, *weights, *[pltpu.VMEM((LEN, units), BF16) for _ in range(3)])

    for t in turns:
        pl.semaphore_signal(
            free_sem, inc=1, device_id={"narrow": mate(t)}, device_id_type=pl.DeviceIdType.MESH
        )

    def attention(mid, gmid, tok, cos_ref, sin_ref, vaug_ref, aug_ref, dk_ref, dv_ref, *rest):
        group = rest[:9]
        spare = list(rest[9:])
        w_all = c_l if w_all_in.shape == x_r.shape else spare.pop(0)
        all_ref = x_l if w_all_in.shape == x_r.shape else spare.pop(0)
        rows_turned = c_r
        q_ref, k_ref, v_ref, att_ref, qraw_ref, kraw_ref, rinv_ref, wo_ref, attt_ref = group

        load("mid", mid_in, mid)

        def load_group(g):
            for i, (source, target) in enumerate(zip(groups_in[g], group)):
                load(f"group{g}_{i}", source, target)

        def need_group(g):
            need(*[f"group{g}_{i}" for i in range(9)])

        load_group(0)
        load("cos", cos_in, cos_ref)
        load("sin", sin_in, sin_ref)
        load("turned", turned_in, rows_turned)
        load("tok", tok_in, tok)

        length = len_ref[0]
        ones = group_ones()
        lane = lanes((BLK, TILE))
        width = w_all.shape[1] // groups
        heads = k_ref.shape[1] // HD
        nq, nk = q_ref.shape[1], k_ref.shape[1]
        gains = {"q": jnp.zeros((1, TILE), F32), "k": jnp.zeros((1, TILE), F32)}
        col_ids = lax.rem(lax.broadcasted_iota(jnp.int32, (BLK, 2 * BLK), 1), BLK)
        causal = lax.broadcasted_iota(jnp.int32, (BLK, 2 * BLK), 0) <= col_ids

        def turn_back(grad, cosine, sine):
            return grad * cosine - swap_halves(grad) * sine

        def norm_back(raw, turned, scale):
            inv = lax.rsqrt(group_sum(raw * raw, ones) * (1.0 / HD) + EPSILON)
            scaled = turned * scale
            unit = raw * inv
            inner = group_sum(unit * scaled, ones) * (1.0 / HD)
            gain = jnp.sum(turned * unit, axis=0, keepdims=True)
            return inv * (scaled - unit * inner), gain

        def attention_pieces(g):
            base = g * width
            for start in range(0, LEN, BLK):
                rows = slice(start, start + BLK)
                grad = contract(branch[rows, :], wo_ref[...], 1, 1).astype(BF16).astype(F32)
                for t in range(heads):
                    cols = slice(t * TILE, (t + 1) * TILE)
                    part = (grad[:, cols] * rinv_ref[rows, cols]).astype(BF16).astype(F32)
                    inner = group_sum(part * att_ref[rows, cols].astype(F32), ones)
                    for which in range(2):
                        mine = part if which == 0 else pltpu.roll(part, HD, 1)
                        sums = pltpu.roll(inner, HD, 1) if which == 0 else inner
                        high = sums.astype(BF16).astype(F32)
                        tail = jnp.where(
                            lane == HD, -high, jnp.where(lane == HD + 1, high - sums, 0.0)
                        )
                        aug_ref[2 * t + which, rows, :] = jnp.where(lane < HD, mine, tail).astype(
                            BF16
                        )
                for t in range(heads // 2):
                    v_pair = v_ref[rows, t * TILE : (t + 1) * TILE].astype(F32)
                    mark = jnp.where(lane < HD + 2, 1.0, 0.0)
                    vaug_ref[2 * t, rows, :] = jnp.where(lane < HD, v_pair, mark).astype(BF16)
                    vaug_ref[2 * t + 1, rows, :] = jnp.where(
                        lane < HD, pltpu.roll(v_pair, HD, 1), mark
                    ).astype(BF16)
                dk_ref[:, rows, :] = jnp.zeros((heads, BLK, HD), F32)
                dv_ref[:, rows, :] = jnp.zeros((heads, BLK, TILE), F32)
                yield

            for h in range(heads):
                keys_turned = jnp.transpose(
                    k_ref[:, (h // 2) * TILE : (h // 2 + 1) * TILE].astype(F32)
                )[(h % 2) * HD : (h % 2 + 1) * HD].astype(BF16)
                for i in range(LEN // BLK):
                    rows = slice(i * BLK, (i + 1) * BLK)
                    low = h * TILE
                    q_two = jnp.concatenate(
                        [q_ref[rows, low : low + HD], q_ref[rows, low + HD : low + TILE]], axis=0
                    )
                    aug = jnp.concatenate(
                        [aug_ref[2 * h, rows, :], aug_ref[2 * h + 1, rows, :]], axis=0
                    )
                    dq = jnp.zeros((HD, 2 * BLK), F32)
                    for j in range(i + 1):
                        keys = slice(j * BLK, (j + 1) * BLK)
                        weight = jnp.exp(
                            contract(k_ref[keys, h * HD : (h + 1) * HD], q_two, 1, 1)
                        )
                        if i == j:
                            weight = jnp.where(causal, weight, 0.0)
                        slope = (weight * contract(vaug_ref[h, keys, :], aug, 1, 1)).astype(BF16)
                        dv_ref[h, keys, :] += contract(weight.astype(BF16), aug, 1, 0)
                        dk_ref[h, keys, :] += contract(slope, q_two, 1, 0)
                        dq += contract(keys_turned[:, keys], slope, 1, 0)
                    both = jnp.concatenate([dq[:, :BLK], dq[:, BLK:]], axis=0)
                    grad = jnp.transpose(both) * (1.0 / math.sqrt(HD))
                    turned = turn_back(grad, cos_ref[rows, :], sin_ref[rows, :])
                    out, gain = norm_back(qraw_ref[rows, low : low + TILE], turned, qs_ref[...])
                    all_ref[rows, base + low : base + low + TILE] = out.astype(BF16)
                    gains["q"] += gain
                    yield

            for start in range(0, LEN, BLK):
                rows = slice(start, start + BLK)
                real = (lax.broadcasted_iota(jnp.int32, (BLK, TILE), 0) + start) < length
                for t in range(heads // 2):
                    low = base + nq + t * TILE
                    grad = jnp.concatenate(
                        [dk_ref[2 * t, rows, :], dk_ref[2 * t + 1, rows, :]], axis=1
                    )
                    grad = jnp.where(real, grad, 0.0)
                    turned = turn_back(grad, cos_ref[rows, :], sin_ref[rows, :])
                    out, gain = norm_back(
                        kraw_ref[rows, t * TILE : (t + 1) * TILE], turned, ks_ref[...]
                    )
                    all_ref[rows, low : low + TILE] = out.astype(BF16)
                    gains["k"] += gain
                    values = jnp.where(
                        lane < HD,
                        dv_ref[2 * t, rows, :],
                        pltpu.roll(dv_ref[2 * t + 1, rows, :], HD, 1),
                    )
                    all_ref[rows, low + nk : low + nk + TILE] = jnp.where(
                        real, values, 0.0
                    ).astype(BF16)
                yield

        def out_grads(which, target):
            first, size = plan["out_parts"][which]
            target[:size, :] = contract(
                attt_ref[first : first + size, :], branch[...], 1, 0
            ).astype(BF16)
            if target.shape[0] > size:
                target[size:, :] = jnp.zeros((target.shape[0] - size, target.shape[1]), BF16)

        def qkv_grads(which, target):
            for start in range(0, rows_turned.shape[0], BLK):
                rows = slice(start, start + BLK)
                for source, size, to in plan["qkv_parts"][which]:
                    target[rows, to : to + size] = contract(
                        rows_turned[rows, :], all_ref[:, source : source + size], 1, 0
                    ).astype(BF16)
                yield

        def gain_copy(step):
            return (f"gain{step}", gain_mine.at[step], gain_in.at[step], partners[step])

        def compute():
            need("mid")
            for t in turns:
                received(f"bl{t}", got_bl.at[t - 1], {"narrow": mate(t)})
            received("by", far_b, to_across)
            gain_two = jnp.zeros((1, fg_ref.shape[1]), F32)
            own_branch, own_cot = block(branch, 0), block(c_l, 0)
            for start in range(0, own_rows, 64):
                rows = slice(start, start + 64)
                grad = own_b[rows, :].astype(F32) + far_b[rows, :].astype(F32)
                for t in turns:
                    grad += got_bl[t - 1, rows, :].astype(F32)
                values = mid[rows, :]
                inv = lax.rsqrt(jnp.mean(values * values, axis=1, keepdims=True) + EPSILON)
                unit = values * inv
                scaled = grad * fg_ref[...]
                inner = jnp.mean(unit * scaled, axis=1, keepdims=True)
                total = own_cot[rows, :].astype(F32) + inv * (scaled - unit * inner)
                gmid[rows, :] = total
                own_branch[rows, :] = total.astype(BF16)
                gain_two += jnp.sum(grad * unit, axis=0, keepdims=True)
            load("w_all", w_all_in, w_all)
            gain_mine[0, 1:2, :] = gain_two
            pl.semaphore_wait(free_sem, side - 1)
            to_mates("br_", own_branch, own_branch)
            need_group(0)
            need("cos", "sin")
            from_mates("br_", branch)
            yield
            out_grads("partner", px2)
            send("o2", px2, rx2, to_across)
            if groups == 1:
                out_grads("own", own2)
            yield
            yield from attention_pieces(0)
            need("turned")
            yield from qkv_grads("partner", px1)
            send("o1", px1, rx1, to_across)
            if groups > 1:
                load_group(1)
            for t in turns:
                received(f"ol{t}", got_ol.at[t - 1], {"narrow": mate(t)})
            received("oy", far_o, to_across)
            for start in range(0, own_rows, 64):
                rows = slice(start, start + 64)
                total = mid[rows, :] + own_o[rows, :].astype(F32) + far_o[rows, :].astype(F32)
                for t in turns:
                    total += got_ol[t - 1, rows, :].astype(F32)
                own_o[rows, :] = total.astype(BF16)
            load("output", own_o, out_out)
            yield
            if groups > 1:
                need_group(1)
                out_grads("own", own2)
                yield
                yield from attention_pieces(1)
            yield from qkv_grads("own", own1)
            need("w_all", "tok")
            sent("by")
            for turn in [*turns, 0]:
                for start in range(0, own_rows, BLK):
                    at = pl.multiple_of(lax.rem(place + turn, side) * own_rows + start, BLK)
                    grad = contract(all_ref[pl.ds(at, BLK), :], w_all[...], 1, 1).astype(BF16)
                    if turn:
                        send_b[turn - 1, start : start + BLK, :] = grad
                    else:
                        own_b[start : start + BLK, :] = grad
                    yield
                if turn:
                    send(
                        f"gn{turn}", send_b.at[turn - 1], got_gn.at[turn - 1], {"narrow": mate(turn)}
                    )
            for t in turns:
                received(f"gn{t}", got_gn.at[t - 1], {"narrow": mate(t)})
            gain_one = jnp.zeros((1, ng_ref.shape[1]), F32)
            for start in range(0, own_rows, 64):
                rows = slice(start, start + 64)
                grad = own_b[rows, :].astype(F32)
                for t in turns:
                    grad += got_gn[t - 1, rows, :].astype(F32)
                values = tok[rows, :].astype(F32)
                inv = lax.rsqrt(jnp.mean(values * values, axis=1, keepdims=True) + EPSILON)
                unit = values * inv
                scaled = grad * ng_ref[...]
                inner = jnp.mean(unit * scaled, axis=1, keepdims=True)
                gmid[rows, :] += inv * (scaled - unit * inner)
                gain_one += jnp.sum(grad * unit, axis=0, keepdims=True)
            load("grad_tokens", gmid, gt_out)
            gain_mine[0, 0:1, :] = gain_one
            spare = jnp.zeros((1, gain_one.shape[1] - TILE), F32)
            gain_mine[0, 2:3, :] = jnp.concatenate([gains["q"], spare], axis=1)
            gain_mine[0, 3:4, :] = jnp.concatenate([gains["k"], spare], axis=1)
            gain_mine[0, 4:8, :] = jnp.zeros((4, gain_one.shape[1]), F32)
            send(*gain_copy(0))
            yield
            received("o2", rx2, to_across)
            received("o1", rx1, to_across)
            for mine, theirs in ((own1, rx1), (own2, rx2)):
                tall = mine.shape[0] // 16

                @pl.loop(0, tall)
                def _(r):
                    at = pl.ds(pl.multiple_of(r * 16, 16), 16)
                    mine[at, :] = (mine[at, :].astype(F32) + theirs[at, :].astype(F32)).astype(
                        BF16
                    )

        turn = 0
        order = [1, 0]
        for number, _ in enumerate(compute()):
            if number % 4 == 3:
                tick(rings[order[turn % 2]])
                turn += 1
        for pair in rings[2:]:
            begin(pair)
        step = 0
        while any(ring.left for pair in rings for ring in pair):
            tick(rings[order[turn % 2]])
            turn += 1
            tick(rings[2])
            tick(rings[3])
            if step < len(doubling):
                name, mine, other, device = gain_copy(step)
                received(name, other, device)
                total = gain_mine[step] + gain_in[step]
                if step + 1 < len(doubling):
                    gain_mine[step + 1] = total
                    send(*gain_copy(step + 1))
                else:
                    gains_ref[...] = total
            step += 1
        for pair in rings:
            for ring in pair:
                ring.finish()
        sent("")
        need("output", "grad_tokens")

    depth = x_l.shape[1]
    k_shape = groups_in[0][1].shape
    heads = k_shape[1] // HD
    scratch = [
        pltpu.VMEM((own_rows, depth), F32),
        pltpu.VMEM((own_rows, depth), F32),
        pltpu.VMEM((own_rows, depth), BF16),
        pltpu.VMEM((LEN, TILE), F32),
        pltpu.VMEM((LEN, TILE), F32),
        pltpu.VMEM((heads, LEN, TILE), BF16),
        pltpu.VMEM((2 * heads, LEN, TILE), BF16),
        pltpu.VMEM((heads, LEN, HD), F32),
        pltpu.VMEM((heads, LEN, TILE), F32),
    ]
    scratch += [pltpu.VMEM(ref.shape, ref.dtype) for ref in groups_in[0]]
    if w_all_in.shape != x_r.shape:
        scratch += [pltpu.VMEM(w_all_in.shape, BF16), pltpu.VMEM((LEN, w_all_in.shape[1]), BF16)]
    pl.run_scoped(attention, *scratch)


VM = pl.BlockSpec(memory_space=pltpu.VMEM)
ANY = pl.BlockSpec(memory_space=pl.ANY)
SM = pl.BlockSpec(memory_space=pltpu.SMEM)


def run_forward(length, rows, wq, wk, wv, qs, ks, cosine, sine):
    nq, nk = wq.shape[1], wk.shape[1]
    shape = jax.ShapeDtypeStruct
    return pl.pallas_call(
        attention_forward,
        out_shape=(
            shape((LEN, nq), BF16),
            shape((LEN, nq), BF16),
            shape((LEN, nk), BF16),
            shape((LEN, nk), BF16),
            shape((LEN, nq), F32),
            shape((LEN, nk), F32),
            shape((LEN, nq), F32),
        ),
        in_specs=[SM] + [VM] * 8,
        out_specs=[VM] * 7,
        scratch_shapes=[pltpu.VMEM((nk // HD, LEN, TILE), BF16)],
        compiler_params=pltpu.CompilerParams(vmem_limit_bytes=VMEM_LIMIT),
        cost_estimate=pl.CostEstimate(
            flops=2 * LEN * rows.shape[1] * 2 * nq + 8 * LEN * LEN * nq,
            bytes_accessed=8 * 1024 * 1024,
            transcendentals=0,
        ),
        name="attention_forward",
    )(length, rows, wq, wk, wv, qs, ks, cosine, sine)


def run_main(plan, small, big, group_arrays):
    count, narrow, side = plan["wide"], plan["narrow"], plan["side"]
    shape = jax.ShapeDtypeStruct
    own, depth = big[0].shape
    units = big[2].shape[1]
    sizes = [(depth, 2 * units), (units, depth), (depth, plan["qkv_width"]), (plan["out_rows"], depth)]
    plan = dict(plan, rows=[s[0] for s in sizes], groups=len(group_arrays), own=own)
    full, lands = [], []
    for rows, cols in sizes:
        chunk, forward, backward = ring_rows(rows, count)
        full.append((chunk * count, cols))
        lands += [pltpu.VMEM((count - 1, r, cols), BF16) for r in (forward, backward) if r]
    plan["lands"] = len(lands)
    steps = 2 * (count - 1)
    doubling = int(math.log2(narrow)) + int(math.log2(count))
    dma = pltpu.SemaphoreType.DMA
    inputs = [*small, *big, *[a for arrays in group_arrays for a in arrays]]
    rest = (own, depth)
    mates = (side - 1, own, depth)
    scratch = [pltpu.VMEM((LEN, depth), BF16) for _ in range(4)]
    scratch += [pltpu.VMEM(full[i], BF16) for i in (0, 1, 2, 3, 2, 3, 2, 3)]
    scratch += lands
    scratch += [pltpu.VMEM(mates, BF16) for _ in range(6)]
    scratch += [pltpu.VMEM(rest, BF16) for _ in range(6)]
    scratch += [pltpu.VMEM((doubling, 8, depth), F32) for _ in range(2)]
    moves = 6 + 10 * (side - 1) + doubling
    scratch += [
        dma((len(big) + 9 * len(group_arrays) + 2,)),
        dma((len(lands), steps)),
        dma((len(lands), steps)),
        dma,
        dma((moves,)),
        dma((moves,)),
        pltpu.SemaphoreType.REGULAR,
    ]
    results = pl.pallas_call(
        functools.partial(main_kernel, plan),
        out_shape=tuple(shape(s, BF16) for s in full)
        + (shape(rest, BF16), shape(rest, F32), shape((8, depth), F32)),
        in_specs=[SM] + [VM] * 4 + [ANY] * (len(inputs) - 5),
        out_specs=[ANY] * 6 + [VM],
        scratch_shapes=scratch,
        compiler_params=pltpu.CompilerParams(
            vmem_limit_bytes=BACK_LIMIT, collective_id=1, has_side_effects=True
        ),
        cost_estimate=pl.CostEstimate(
            flops=60 * 10**9, bytes_accessed=64 * 1024 * 1024, transcendentals=0
        ),
        name="main",
    )(*inputs)
    return [r[: s[0]] for r, s in zip(results[:4], sizes)] + list(results[4:])


def on_device(
    wide, narrow,
    tokens, lengths, norm_gain, w_query, w_key, w_value, query_scale, key_scale, w_out,
    ffn_gain, w_gate, w_up, w_down, cotangent,
):
    sequences = lengths.shape[0]
    side = narrow // sequences
    own = tokens.shape[0]
    me = lax.axis_index("narrow")
    place, mine = lax.rem(me, side), me // side

    def across(array, turn=1):
        return lax.ppermute(
            array, "narrow", [(i, (i + turn * side) % narrow) for i in range(narrow)]
        )

    def within(array, turn):
        return lax.ppermute(
            array,
            "narrow",
            [(i, (i // side) * side + (i % side + turn) % side) for i in range(narrow)],
        )

    def gather(array):
        size = array.shape[0]
        whole = jnp.zeros((side * size,) + array.shape[1:], array.dtype)
        whole = lax.dynamic_update_slice(whole, array, (place * size, 0))
        for turn in range(1, side):
            source = lax.rem(place + side - turn, side)
            whole = lax.dynamic_update_slice(whole, within(array, turn), (source * size, 0))
        return whole

    def scatter(parts):
        size = parts.shape[0] // side
        total = lax.dynamic_slice_in_dim(parts, place * size, size).astype(F32)
        for turn in range(1, side):
            target = lax.rem(place + turn, side)
            total += within(
                lax.dynamic_slice_in_dim(parts, target * size, size).astype(BF16), turn
            ).astype(F32)
        return total

    cosine, sine = rope_tables(LEN, HD)
    cosine = jnp.concatenate([cosine] * 4, axis=1)
    sine = jnp.concatenate([-sine, sine, -sine, sine], axis=1)
    qs = jnp.concatenate([query_scale] * 2)[None, :]
    ks = jnp.concatenate([key_scale] * 2)[None, :]
    length = lax.dynamic_slice_in_dim(lengths, mine, 1)

    weights = [(w_query, w_key, w_value, w_out)]
    weights += [tuple(across(w, t) for w in weights[0]) for t in range(1, sequences)]
    joined = w_key.shape[1] % TILE != 0
    if joined:
        weights = [
            tuple(jnp.concatenate(ws, axis=1 if n < 3 else 0) for n, ws in enumerate(zip(*weights)))
        ]

    residual = tokens.astype(F32)
    normed_one, inv_one = row_norm(residual, norm_gain)
    rows_one = gather(normed_one.astype(BF16))
    saved = [run_forward(length, rows_one, *w[:3], qs, ks, cosine, sine) for w in weights]
    mixed = contract(saved[0][0], weights[0][3], 1, 0)
    for s, w in zip(saved[1:], weights[1:]):
        mixed += contract(s[0], w[3], 1, 0)
    middle = residual + scatter(mixed)

    normed_two, inv_two = row_norm(middle, ffn_gain)
    low_two = normed_two.astype(BF16)

    nq, nk = w_query.shape[1], w_key.shape[1]
    if joined:
        order = [0]
        qkv_parts = {
            "own": [(0, nq, 0), (2 * nq, nk, nq), (2 * nq + 2 * nk, nk, nq + nk)],
            "partner": [
                (nq, nq, 0), (2 * nq + nk, nk, nq), (2 * nq + 3 * nk, nk, nq + nk)
            ],
        }
        out_parts = {"own": (0, nq), "partner": (nq, nq)}
    else:
        order = [1, 0]
        qkv_parts = {
            "partner": [(0, nq + 2 * nk, 0)],
            "own": [(nq + 2 * nk, nq + 2 * nk, 0)],
        }
        out_parts = {"partner": (0, nq), "own": (0, nq)}
    plan = {
        "wide": wide, "narrow": narrow, "side": side,
        "qkv_parts": qkv_parts, "out_parts": out_parts,
        "qkv_width": nq + 2 * nk, "out_rows": nq,
    }
    group_arrays = []
    for g in order:
        att, q, k, v, q_raw, k_raw, rinv = saved[g]
        group_arrays.append((q, k, v, att, q_raw, k_raw, rinv, weights[g][3], att.T))
    w_all = jnp.concatenate([w for g in order for w in weights[g][:3]], axis=1)
    sum_gu, sum_down, sum_qkv, sum_out, output, grad_tokens, gains = run_main(
        plan,
        (length, qs, ks, norm_gain[None, :], ffn_gain[None, :]),
        (
            low_two, cotangent, w_gate, w_up, w_down, middle, tokens, cosine, sine,
            rows_one.T, w_all,
        ),
        group_arrays,
    )
    hidden_units = w_gate.shape[1]
    return (
        output,
        grad_tokens,
        gains[0],
        sum_qkv[:, :nq].astype(F32),
        sum_qkv[:, nq : nq + nk].astype(F32),
        sum_qkv[:, nq + nk :].astype(F32),
        gains[2, :HD] + gains[2, HD:TILE],
        gains[3, :HD] + gains[3, HD:TILE],
        sum_out.astype(F32),
        gains[1],
        sum_gu[:, :hidden_units].astype(F32),
        sum_gu[:, hidden_units:].astype(F32),
        sum_down.astype(F32),
    )


def solution(mesh):
    rows = P(("wide", "narrow"), None)
    columns, depth, copied = P(None, "narrow"), P("narrow", None), P()
    return jax.shard_map(
        functools.partial(on_device, mesh.shape["wide"], mesh.shape["narrow"]),
        mesh=mesh,
        in_specs=(
            rows, P("wide"), copied, columns, columns, columns, copied, copied, depth,
            copied, columns, columns, depth, rows,
        ),
        out_specs=(
            rows, rows, copied, columns, columns, columns, copied, copied, depth,
            copied, columns, columns, depth,
        ),
        check_vma=False,
    )
```

time: 433 us -> 357 us (0.82)
  Pallas kernels: 199 us -> 287 us
  matrix products: 78.4 us -> 4 us
  local copies, waits for them, and re-layouts: 70.7 us -> 33.9 us
  waiting for transfers between devices: 27 us -> 0.02 us
  other arithmetic: 36.8 us -> 21.6 us
  starting transfers between devices: 12.6 us -> 5.15 us
    pallas_call x1, Pallas kernels: 179 us -> 267 us  [run_main(): pl.pallas_call(functools.partial(main_kernel, plan), out_shape=tuple((sha...]
    dot_general x16 -> x2, matrix products: 78.4 us -> 4 us  [contract(): lax.dot_general(left_side, right_side, (((left_dim,), (right_dim,)), ((),...]
    ppermute x8 -> x4, waiting for transfers between devices: 27 us -> 0.01 us  [across(): lax.ppermute(array, 'narrow', [(i, (i + turn * side) % narrow) for i in r...]
    convert_element_type x4 -> x0, other arithmetic: 9.63 us -> none  [the longest x1 4.34 us: on_device(): branch = gather(grad_middle.astype(BF16))]
    unnamed x127 -> x78, local copies, waits for them, and re-layouts: 25.7 us -> 16.4 us
    dynamic_update_slice x8 -> x2, local copies, waits for them, and re-layouts: 15.8 us -> 6.63 us  [gather(): lax.dynamic_update_slice(whole, within(array, turn), (source * size, 0))]
    ppermute x5 -> x0, local copies, waits for them, and re-layouts: 8.25 us -> none  [the longest x4 6.76 us: within(): lax.ppermute(array, 'narrow', [(i, i // side * side + (i % side + turn) %...]
    ppermute x8 -> x4, starting transfers between devices: 9.92 us -> 4.7 us  [across(): lax.ppermute(array, 'narrow', [(i, (i + turn * side) % narrow) for i in r...]
  transfers between devices with their start and end apart: 19 -> 6, of which waited for: 1 -> 0; matrix products, arithmetic and copies ran while one was open for 33% -> 5% of each run, Pallas kernels for 5% -> 6%
where the time goes in v3:
time: 357 us; the launch traced here: 352 us
  Pallas kernels  287 us (80%)
  local copies, waits for them, and re-layouts  33.9 us (9%)
  other arithmetic  21.6 us (6%)
  starting transfers between devices  5.15 us (1%)
  matrix products  4 us (1%)
    pallas_call x1, Pallas kernels, run_main(): pl.pallas_call(functools.partial(main_kernel, plan), out_shape=tuple((sha...  267 us
    pallas_call x2, Pallas kernels, run_forward(): pl.pallas_call(attention_forward, out_shape=(shape((LEN, nq), BF16), shap...  19.4 us
    unnamed x78, local copies, waits for them, and re-layouts  16.4 us
  transfers between devices with their start and end apart: 6, of which 0 were waited for; matrix products, arithmetic and copies ran while one was open for 5% of the time, Pallas kernels for 6%

profile of v3, /device:TPU:0, one launch (start us, length us, event | category | flops | bytes accessed | tf_op | source)
XLA Modules:
  0.0 352.4 jit_solution(11618400681173520153)
XLA Ops:
  0.7 1.5 copy.27
  2.5 1.6 broadcast_in_dim.25
  4.1 1.6 constant_dynamic-update-slice_fusion.7
  6.2 2.6 collective-permute-start.2
  8.8 1.9 collective-permute-start.1
  11.5 2.0 fusion.5
  14.5 2.5 constant_dynamic-update-slice_fusion.6
  17.0 4.1 %copy.28.x_ref = bf16[1024,1024]{1,0:T(8,128)(2,1)} copy(bf16[1024,1024]{0,1:T(8,128)(2,1)} %constant_dynamic-update-slice_fusion.6) | data formatting | bytes 4194304 | tf_op jit(solution)/shard_map/dynamic_update_slice | solution.py:884
  21.1 9.5 %attention_forward.2 = (bf16[1024,256]{1,0:T(8,128)(2,1)S(1)}, bf16[1024,256]{1,0:T(8,128)(2,1)S(1)}, bf16[1024,128]{1,0:T(8,128)(2,1)S(1)}, bf16[1024,128]{1,0:...) custom-call(s32[1]{0:T(128)} %dynamic_slice.9.len_ref.refs_0_, ...), custom_call_target="tpu_custom_call" | custom-call | flops 3221225472 | bytes 8388608 | tf_op jit(solution)/shard_map/attention_forward/pallas_call | solution.py:778
  36.3 9.9 %attention_forward.3 = (bf16[1024,256]{1,0:T(8,128)(2,1)S(1)}, bf16[1024,256]{1,0:T(8,128)(2,1)S(1)}, bf16[1024,128]{1,0:T(8,128)(2,1)S(1)}, bf16[1024,128]{1,0:...) custom-call(s32[1]{0:T(128)} %dynamic_slice.9.len_ref.refs_0_, ...), custom_call_target="tpu_custom_call" | custom-call | flops 3221225472 | bytes 8388608 | tf_op jit(solution)/shard_map/attention_forward/pallas_call | solution.py:778
  46.3 2.2 fusion.8
  48.5 1.8 convolution_add_fusion
  53.2 1.7 constant_dynamic-update-slice_fusion.3
  59.2 2.4 multiply_reduce_fusion
  61.6 1.8 copy.33.refs_10_
  63.7 1.3 copy.32.refs_5_
  65.0 267.2 %main.1 = (bf16[1024,2304]{1,0:T(8,128)(2,1)}, bf16[1152,1024]{1,0:T(8,128)(2,1)}, bf16[1024,512]{1,0:T(8,128)(2,1)}, bf16[256,1024]{1,0:T(8,128)(2,1)}, bf16[51...) custom-call(s32[1]{0:T(128)} %dynamic_slice.9.len_ref.refs_0_, f32[1,128]{1,0:T(1,128)} %copy-done.10, ...), custom_call_target="tpu_custom_call" | custom-call | flops 60000002048 | bytes 67108864 | tf_op jit(solution)/shard_map/main/pallas_call | solution.py:837
  332.2 1.4 add_bitcast_fusion
  333.6 1.4 fusion.7
  335.0 2.2 slice_convert_fusion.2
  337.3 2.1 slice_convert_fusion.3
  340.4 2.9 convert_element_type.47
  344.5 4.3 %slice_convert_fusion = (f32[1024,1152]{1,0:T(8,128)}, f32[1024,1152]{1,0:T(8,128)}) fusion(bf16[1024,2304]{1,0:T(8,128)(2,1)S(1)} %copy-done.25), kind=kLoop, calls=%fused_computation.3 | loop fusion | flops 2359296 | bytes 14155776 | tf_op jit(solution)/shard_map/convert_element_type | solution.py:973
  350.8 1.3 copy.44
  (98 shorter events, 19.8 us)
Async XLA Ops:
  2.2 3.6 %copy-start.22 = (bf16[512,1024]{0,1:T(8,128)(2,1)}, bf16[512,1024]{0,1:T(8,128)(2,1)S(1)}, u32[]{:S(2)}) copy-start(bf16[512,1024]{0,1:T(8,128)(2,1)S(1)} %copy.27) | copy-start | bytes 3145732
  4.1 4.7 %copy-start.6 = (bf16[1024,128]{1,0:T(8,128)(2,1)S(1)}, bf16[1024,128]{1,0:T(8,128)(2,1)}, u32[]{:S(2)}) copy-start(bf16[1024,128]{1,0:T(8,128)(2,1)} %wv_ref.1) | copy-start | bytes 786436
  4.1 4.8 %copy-start.4 = (bf16[1024,256]{1,0:T(8,128)(2,1)S(1)}, bf16[1024,256]{1,0:T(8,128)(2,1)}, u32[]{:S(2)}) copy-start(bf16[1024,256]{1,0:T(8,128)(2,1)} %wq_ref.1) | copy-start | bytes 1572868
  4.1 6.8 %copy-start.34 = (s32[2]{0:T(128)S(1)}, s32[2]{0:T(128)}, u32[]{:S(2)}) copy-start(s32[2]{0:T(128)} %param.15) | copy-start | bytes 28
  5.7 8.7 %collective-permute-start = (bf16[512,1024]{0,1:T(8,128)(2,1)}, bf16[512,1024]{0,1:T(8,128)(2,1)}, u32[]{:S(2)}, u32[]{:S(2)}) collective-permute-start(bf16[512,1024]{0,1:T(8,128)(2,1)} %get-tuple-element.58), channel_id=1, source_target_pairs={{0,1},{1,0},{2,3},{3,2},{4,5},{5,4},{6,7},{7,6},{8,9},{9,8},{10,11... | collective-permute-start | bytes 3145736 | tf_op jit(solution)/shard_map/ppermute | solution.py:872
  6.2 28.4 %collective-permute-start.2 = (bf16[1024,128]{1,0:T(8,128)(2,1)S(1)}, bf16[1024,128]{1,0:T(8,128)(2,1)S(1)}, u32[]{:S(2)}, u32[]{:S(2)}) collective-permute-start(bf16[1024,128]{1,0:T(8,128)(2,1)S(1)} %copy-done.5), channel_id=1, source_target_pairs={{0,2},{1,3},{2,0},{3,1},{4,6},{5,7},{6,4},{7,5},{8,10},{9,11},{10,... | collective-permute-start | bytes 786440 | tf_op jit(solution)/shard_map/ppermute | solution.py:867
  8.8 26.6 %collective-permute-start.3 = (bf16[1024,128]{1,0:T(8,128)(2,1)S(1)}, bf16[1024,128]{1,0:T(8,128)(2,1)}, u32[]{:S(2)}, u32[]{:S(2)}) collective-permute-start(bf16[1024,128]{1,0:T(8,128)(2,1)S(1)} %copy-done.6), channel_id=1, source_target_pairs={{0,2},{1,3},{2,0},{3,1},{4,6},{5,7},{6,4},{7,5},{8,10},{9,11},{10,... | collective-permute-start | bytes 786440 | tf_op jit(solution)/shard_map/ppermute | solution.py:867
  8.8 26.5 %collective-permute-start.1 = (bf16[1024,256]{1,0:T(8,128)(2,1)S(1)}, bf16[1024,256]{1,0:T(8,128)(2,1)S(1)}, u32[]{:S(2)}, u32[]{:S(2)}) collective-permute-start(bf16[1024,256]{1,0:T(8,128)(2,1)S(1)} %copy-done.4), channel_id=1, source_target_pairs={{0,2},{1,3},{2,0},{3,1},{4,6},{5,7},{6,4},{7,5},{8,10},{9,11},{10,... | collective-permute-start | bytes 1572872 | tf_op jit(solution)/shard_map/ppermute | solution.py:867
  10.8 35.5 %collective-permute-start.4 = (bf16[256,1024]{1,0:T(8,128)(2,1)}, bf16[256,1024]{1,0:T(8,128)(2,1)}, u32[]{:S(2)}, u32[]{:S(2)}) collective-permute-start(bf16[256,1024]{1,0:T(8,128)(2,1)} %refs_32_.1), channel_id=1, source_target_pairs={{0,2},{1,3},{2,0},{3,1},{4,6},{5,7},{6,4},{7,5},{8,10},{9,11},{10,... | collective-permute-start | bytes 1572872 | tf_op jit(solution)/shard_map/ppermute | solution.py:867
  11.5 2.9 copy-start.33
  14.4 21.0 %copy-start.2 = (f32[1024,128]{1,0:T(8,128)}, f32[1024,128]{1,0:T(8,128)S(1)}, u32[]{:S(2)}) copy-start(f32[1024,128]{1,0:T(8,128)S(1)} %get-tuple-element.70.cos_ref.refs_12_) | copy-start | bytes 1572868
  14.4 21.0 %copy-start.3 = (f32[1024,128]{1,0:T(8,128)}, f32[1024,128]{1,0:T(8,128)S(1)}, u32[]{:S(2)}) copy-start(f32[1024,128]{1,0:T(8,128)S(1)} %get-tuple-element.71.sin_ref.refs_13_) | copy-start | bytes 1572868
  14.5 20.9 %copy-start.10 = (f32[1,128]{1,0:T(1,128)}, f32[1,128]{1,0:T(1,128)S(1)}, u32[]{:S(2)}) copy-start(f32[1,128]{1,0:T(1,128)S(1)} %get-tuple-element.72.qs_ref.refs_1_) | copy-start | bytes 1540
  14.5 20.9 %copy-start.11 = (f32[1,128]{1,0:T(1,128)}, f32[1,128]{1,0:T(1,128)S(1)}, u32[]{:S(2)}) copy-start(f32[1,128]{1,0:T(1,128)S(1)} %get-tuple-element.73.ks_ref.refs_2_) | copy-start | bytes 1540
  34.6 23.6 %copy-start.1 = (bf16[1024,256]{1,0:T(8,128)(2,1)}, bf16[1024,256]{1,0:T(8,128)(2,1)S(1)}, u32[]{:S(2)}) copy-start(bf16[1024,256]{1,0:T(8,128)(2,1)S(1)} %get-tuple-element.34.refs_28_) | copy-start | bytes 1572868
  46.3 10.9 %copy-start = (bf16[1024,256]{1,0:T(8,128)(2,1)}, bf16[1024,256]{1,0:T(8,128)(2,1)S(1)}, u32[]{:S(2)}) copy-start(bf16[1024,256]{1,0:T(8,128)(2,1)S(1)} %get-tuple-element.35.refs_19_) | copy-start | bytes 1572868
  50.4 4.5 %copy-start.24 = (f32[1024,1024]{0,1:T(8,128)}, f32[1024,1024]{0,1:T(8,128)S(1)}, u32[]{:S(2)}) copy-start(f32[1024,1024]{0,1:T(8,128)S(1)} %convolution_add_fusion) | copy-start | bytes 12582916
  51.6 4.8 %copy-start.7 = (bf16[1024,128]{1,0:T(8,128)(2,1)S(1)}, bf16[1024,128]{1,0:T(8,128)(2,1)}, u32[]{:S(2)}) copy-start(bf16[1024,128]{1,0:T(8,128)(2,1)} %wv_ref.1) | copy-start | bytes 786436
  51.7 7.6 %collective-permute-start.5 = (bf16[512,1024]{0,1:T(8,128)(2,1)}, bf16[512,1024]{0,1:T(8,128)(2,1)}, u32[]{:S(2)}, u32[]{:S(2)}) collective-permute-start(bf16[512,1024]{0,1:T(8,128)(2,1)} %dynamic-slice_convert_fusion), channel_id=1, source_target_pairs={{0,1},{1,0},{2,3},{3,2},{4,5},{5,4},{6,7},{7,6},{8,9},{9,8},{10,11... | collective-permute-start | bytes 3145736 | tf_op jit(solution)/shard_map/ppermute | solution.py:872
  55.7 3.5 copy-start.23
  332.2 7.2 %copy-start.29 = (bf16[256,1024]{1,0:T(8,128)(2,1)S(1)}, bf16[256,1024]{1,0:T(8,128)(2,1)}, u32[]{:S(2)}) copy-start(bf16[256,1024]{1,0:T(8,128)(2,1)} %get-tuple-element.52) | copy-start | bytes 1572868
  335.0 5.4 %copy-start.26 = (bf16[1152,1024]{1,0:T(8,128)(2,1)S(1)}, bf16[1152,1024]{1,0:T(8,128)(2,1)}, u32[]{:S(2)}) copy-start(bf16[1152,1024]{1,0:T(8,128)(2,1)} %get-tuple-element.54) | copy-start | bytes 7077892
  340.4 4.0 %copy-start.25 = (bf16[1024,2304]{1,0:T(8,128)(2,1)S(1)}, bf16[1024,2304]{1,0:T(8,128)(2,1)}, u32[]{:S(2)}) copy-start(bf16[1024,2304]{1,0:T(8,128)(2,1)} %get-tuple-element.53) | copy-start | bytes 14155780
  344.5 4.4 %copy-start.28 = (bf16[512,1024]{1,0:T(8,128)(2,1)S(1)}, bf16[512,1024]{1,0:T(8,128)(2,1)}, u32[]{:S(2)}) copy-start(bf16[512,1024]{1,0:T(8,128)(2,1)} %get-tuple-element.87) | copy-start | bytes 3145732
  (17 other events, 27.6 us)
